TPU v7x, 32 devices: a whole 2x2x4 slice. The times are simulated.
32 devices in a mesh: tracer: 2 (over y), gx: 4 (over x, core), gy: 4 (over z).
Axes of the slice: x: 2, y: 2, z: 4, core: 2. Of those that a mesh axis runs over, the one named last changes fastest.
Arguments:
- tracers: float32 [24, 16, 32, 512], P('tracer', None, 'gx', 'gy'), may hold values from 0.05 to 2
- fluxes: float32 [3, 16, 32, 512], P(None, 'tracer', 'gx', 'gy'), may hold values from -0.15 to 0.15
- diff_east: float32 [32, 512], P('gx', 'gy'), may hold values from 0.01 to 0.1
- diff_north: float32 [32, 512], P('gx', 'gy'), may hold values from 0.01 to 0.1
- column_depth: int32 [32, 512], P('gx', 'gy'), may hold values from 0 to 16
- grazers: float32 [16, 32, 512], P(None, 'gx', 'gy'), may hold values from 0.2 to 0.9
- groups: int32 [24], P('tracer'), may hold values from 0 to 15
- preference: float32 [16], replicated, may hold values from 0.1 to 1
Outputs:
- advanced: float32 [24, 16, 32, 512], P('tracer', None, 'gx', 'gy')
Inputs may be any that keep to these rules, and one draw needn't show every extreme that they name: A cell at level k is sea iff k < column_depth of its column.
All inputs are finite; a program needn't handle non-finite values.
Results may differ from a plain program's by a relative error of at most 0.0003.
Values sent between devices are 32-bit elements; how exact they have to be, the bound alone decides.
No kernel may reach another device: no remote copies, remote signals or barrier semaphores. Data moves between devices by JAX's collectives and lax.ppermute only.
A program may use at most 64 MiB of HBM per device.

v0:
```python
import jax
import jax.numpy as jnp
from jax import lax
from jax.sharding import PartitionSpec as P

STEPS = 2


def with_halo(cells, sides, width):
    for axis, dim in sides:
        count = lax.axis_size(axis)
        ends = count - 1
        head = lax.slice_in_dim(cells, 0, width, axis=dim)
        tail = lax.slice_in_dim(cells, cells.shape[dim] - width, cells.shape[dim], axis=dim)
        cells = jnp.concatenate(
            [
                lax.ppermute(tail, axis, [(i, (i + 1) % count) for i in range(ends)]),
                cells,
                lax.ppermute(head, axis, [((i + 1) % count, i) for i in range(ends)]),
            ],
            axis=dim,
        )
    return cells


def minmod(jump_low, jump_high):
    return jnp.maximum(0.0, jnp.minimum(jump_low, jump_high)) + jnp.minimum(
        0.0, jnp.maximum(jump_low, jump_high)
    )


def window(values, low_end, high_end, direction):
    return lax.slice_in_dim(values, low_end, high_end, axis=direction % values.ndim)


def face_terms(tracer_field, open_faces, face_flux, face_kappa, direction):
    length = tracer_field.shape[direction % tracer_field.ndim] - 4
    jump_face = open_faces * (
        window(tracer_field, 1, length + 4, direction)
        - window(tracer_field, 0, length + 3, direction)
    )
    slopes = minmod(
        window(jump_face, 0, length + 2, direction), window(jump_face, 1, length + 3, direction)
    )
    left_value = window(tracer_field, 1, length + 2, direction) + 0.5 * window(
        slopes, 0, length + 1, direction
    )
    right_value = window(tracer_field, 2, length + 3, direction) - 0.5 * window(
        slopes, 1, length + 2, direction
    )
    carried = face_flux * jnp.where(face_flux > 0.0, left_value, right_value)
    if face_kappa is not None:
        carried = carried - face_kappa * window(jump_face, 1, length + 2, direction)
    return window(carried, 0, length, direction) - window(carried, 1, length + 1, direction)


def on_device(tracers, fluxes, diff_east, diff_north, column_depth, grazers, groups, preference):
    tr_dev, levels, rows_dev, cols_dev = tracers.shape
    total_tracers = tr_dev * lax.axis_size("tracer")
    level_index = lax.broadcasted_iota(jnp.int32, (levels, rows_dev, cols_dev), 0)
    wet_cells = (level_index < column_depth[None]).astype(jnp.float32)
    all_fluxes = lax.all_gather(fluxes, "tracer", axis=1, tiled=True)
    stacked = jnp.concatenate(
        [all_fluxes[0], all_fluxes[1], wet_cells, diff_east[None], diff_north[None]], 0
    )
    rimmed = with_halo(stacked, (("gx", 1), ("gy", 2)), 2)
    east_ext = rimmed[:levels]
    north_ext = rimmed[levels : 2 * levels]
    downward = all_fluxes[2]
    wet_ext = rimmed[-(levels + 2) : -2]
    kx_ext = rimmed[-2]
    ky_ext = rimmed[-1]
    open_x = wet_ext[:, :-1, 2:-2] * wet_ext[:, 1:, 2:-2]
    open_y = wet_ext[:, 2:-2, :-1] * wet_ext[:, 2:-2, 1:]
    flux_x = east_ext[:, 1 : rows_dev + 2, 2:-2] * open_x[:, 1 : rows_dev + 2]
    kappa_x = kx_ext[None, 1 : rows_dev + 2, 2:-2] * open_x[:, 1 : rows_dev + 2]
    flux_y = north_ext[:, 2:-2, 1 : cols_dev + 2] * open_y[:, :, 1 : cols_dev + 2]
    kappa_y = ky_ext[None, 2:-2, 1 : cols_dev + 2] * open_y[:, :, 1 : cols_dev + 2]
    wet_z = jnp.pad(wet_cells, ((2, 2), (0, 0), (0, 0)))
    open_z = wet_z[:-1] * wet_z[1:]
    flux_z = jnp.pad(downward, ((1, 0), (0, 0), (0, 0))) * open_z[1 : levels + 2]
    group_match = (
        groups[:, None] == lax.broadcasted_iota(jnp.int32, (1, preference.shape[0]), 1)
    ).astype(jnp.float32)
    grazing_pref = jnp.sum(group_match * preference[None, :], axis=1)
    tracer_field = tracers
    for step_index in range(STEPS):
        prey_local = jnp.sum(grazing_pref[:, None, None, None] * tracer_field, axis=0)
        prey_total = lax.psum(prey_local, "tracer")
        factor = grazers / (1.0 + 4.0 * prey_total / total_tracers)
        extended = with_halo(tracer_field, (("gx", 2), ("gy", 3)), 2)
        tendency = face_terms(extended[:, :, :, 2:-2], open_x, flux_x, kappa_x, -2)
        tendency = tendency + face_terms(extended[:, :, 2:-2, :], open_y, flux_y, kappa_y, -1)
        padded_z = jnp.pad(tracer_field, ((0, 0), (2, 2), (0, 0), (0, 0)))
        tendency = tendency + face_terms(padded_z, open_z, flux_z, None, -3)
        tracer_field = (
            tracer_field + tendency - grazing_pref[:, None, None, None] * factor * tracer_field
        )
    return tracer_field


def solution(mesh):
    placed = (
        P("tracer", None, "gx", "gy"),
        P(None, "tracer", "gx", "gy"),
        P("gx", "gy"),
        P("gx", "gy"),
        P("gx", "gy"),
        P(None, "gx", "gy"),
        P("tracer"),
        P(),
    )
    return jax.shard_map(
        on_device,
        mesh=mesh,
        in_specs=placed,
        out_specs=P("tracer", None, "gx", "gy"),
        check_vma=False,
    )
```

profile of v0, /device:TPU:0, one launch (start us, length us, event | category | flops | bytes accessed | tf_op | source)
XLA Modules:
  0.0 146.4 jit_solution(9993847357524137815)
XLA Ops:
  6.5 1.0 copy.272
  7.5 6.4 %all_gather.3 = f32[3,16,8,128]{3,1,2,0:T(8,128)S(1)} all-gather(f32[3,8,8,128]{3,1,2,0:T(8,128)S(1)} %copy.272), channel_id=1, replica_groups=mesh['tracer'=2,'gx'=4,'gy'=4] {'tracer'}, dimensions={1}, use_global_device_ids=true | all-gather | bytes 294912 | tf_op jit(solution)/shard_map/all_gather | solution.py:62
  14.7 0.7 concatenate.51
  15.4 1.3 collective-permute-start
  16.7 1.3 collective-permute-start.1
  18.2 0.8 fusion.54
  19.0 5.1 %collective-permute-start.2 = (f32[12,16,2,128]{3,1,2,0:T(8,128)}, f32[12,16,2,128]{3,1,2,0:T(8,128)S(1)}, u32[]{:S(2)}, u32[]{:S(2)}) collective-permute-start(f32[12,16,2,128]{3,1,2,0:T(8,128)} %get-tuple-element.22), channel_id=1, source_target_pairs={{0,4},{4,8},{8,12},{1,5},{5,9},{9,13},{2,6},{6,10},{10,14},{3,7},{... | collective-permute-start | bytes 589832 | tf_op jit(solution)/shard_map/ppermute | solution.py:17
  24.1 1.3 collective-permute-start.3
  27.4 1.5 %fusion.14 = f32[12,17,8,128]{3,1,2,0:T(8,128)} fusion(f32[12,16,8,128]{3,1,2,0:T(8,128)S(1)} %copy.285, f32[12,18,8,128]{3,1,2,0:T(8,128)S(1)} %minimum_add_fusion.3, f32[17,8,128]{2,0,1:T(8,128)S(1)} %get-tuple-element.12, pred[17,8,128]{2,0,1:T(8,128)(4,1)S(1)} %get-tuple-element.11), kind=kLoop, calls=%fused_computation.42 | loop fusion | flops 1253376 | bytes 3380224 | tf_op jit(solution)/shard_map/mul | solution.py:51
  29.1 3.5 %collective-permute-start.4 = (f32[50,12,2]{2,0,1:T(8,128)S(1)}, f32[50,12,2]{2,0,1:T(8,128)S(1)}, u32[]{:S(2)}, u32[]{:S(2)}) collective-permute-start(f32[50,12,2]{2,0,1:T(8,128)S(1)} %get-tuple-element.23), channel_id=1, source_target_pairs={{0,1},{1,2},{2,3},{4,5},{5,6},{6,7},{8,9},{9,10},{10,11},{12,13},{... | collective-permute-start | bytes 14408 | tf_op jit(solution)/shard_map/ppermute | solution.py:17
  32.6 1.3 collective-permute-start.5
  34.6 5.0 %collective-permute-done.4 = f32[50,12,2]{2,0,1:T(8,128)S(1)} collective-permute-done((f32[50,12,2]{2,0,1:T(8,128)S(1)}, f32[50,12,2]{2,0,1:T(8,128)S(1)}, u32[]{:S(2)}, u32[]{:S(2)}) %collective-permute-start.4) | collective-permute-done | bytes 4832 | tf_op jit(solution)/shard_map/ppermute | solution.py:17
  39.6 4.7 %collective-permute-done.5 = f32[50,12,2]{2,0,1:T(8,128)S(1)} collective-permute-done((f32[50,12,2]{2,0,1:T(8,128)S(1)}, f32[50,12,2]{2,0,1:T(8,128)S(1)}, u32[]{:S(2)}, u32[]{:S(2)}) %collective-permute-start.5) | collective-permute-done | bytes 4832 | tf_op jit(solution)/shard_map/ppermute | solution.py:19
  44.9 0.8 slice_multiply_fusion.16
  45.6 0.8 broadcast_compare_fusion
  47.1 3.9 %all-reduce.7.cloned.1.call-done = f32[16,8,128]{2,0,1:T(8,128)} async-done(((f32[16,8,128]{2,0,1:T(8,128)}), f32[16,8,128]{2,0,1:T(8,128)}) %all-reduce.7.cloned.1.call-update) | async-done | bytes 65552 | tf_op jit(solution)/shard_map/psum | solution.py:89
  51.0 1.5 %add_divide_fusion.1 = f32[16,8,128]{2,0,1:T(8,128)} fusion(f32[16,8,128]{2,0,1:T(8,128)} %all-reduce.7.cloned.1.call-done, f32[16,8,128]{2,1,0:T(8,128)S(1)} %copy-done.26), kind=kLoop, calls=%fused_computation.120 | loop fusion | flops 49152 | bytes 196608 | tf_op jit(solution)/shard_map/div | solution.py:90
  52.8 1.8 %fusion.52 = (f32[12,16,12,2]{3,1,2,0:T(8,128)}, f32[12,16,12,2]{3,1,2,0:T(8,128)}) fusion(f32[12,16,12,128]{3,1,2,0:T(8,128)S(1)} %constant_dynamic-update-slice_fusion), kind=kLoop, calls=%fused_computation.139 | loop fusion | bytes 73728 | tf_op jit(solution)/shard_map/slice | solution.py:14
  54.6 1.1 minimum_add_fusion.5
  55.8 3.2 %copy.278 = f32[12,16,12,2]{2,1,3,0:T(8,128)} copy(f32[12,16,12,2]{3,1,2,0:T(8,128)} %get-tuple-element.15) | data formatting | bytes 36864 | tf_op jit(solution)/shard_map/slice | solution.py:14
  59.0 4.1 %collective-permute-start.6 = (f32[12,16,12,2]{2,1,3,0:T(8,128)}, f32[12,16,12,2]{2,1,3,0:T(8,128)}, u32[]{:S(2)}, u32[]{:S(2)}) collective-permute-start(f32[12,16,12,2]{2,1,3,0:T(8,128)} %copy.278), channel_id=1, source_target_pairs={{0,1},{1,2},{2,3},{4,5},{5,6},{6,7},{8,9},{9,10},{10,11},{12,13},{... | collective-permute-start | bytes 55304 | tf_op jit(solution)/shard_map/ppermute | solution.py:17
  63.0 3.2 %copy.280 = f32[12,16,12,2]{2,1,3,0:T(8,128)} copy(f32[12,16,12,2]{3,1,2,0:T(8,128)} %get-tuple-element.16) | data formatting | bytes 36864 | tf_op jit(solution)/shard_map/slice | solution.py:13
  66.2 1.5 collective-permute-start.7
  67.7 2.7 %fusion.31 = f32[12,16,9,128]{3,1,2,0:T(8,128)} fusion(f32[12,16,11,128]{3,1,2,0:T(8,128)S(1)} %fusion.25, f32[12,16,10,128]{3,1,2,0:T(8,128)} %minimum_add_fusion.5, f32[12,16,2,128]{3,1,2,0:T(8,128)S(1)} %collective-permute-done.3, f32[12,16,8,128]{3,1,2,0:T(8,128)S(1)} %copy.285, f32[12,16,2,128]{3,1,2,0:T(8,128)S(1)} %collective-permute-done.2, ...), kind=kLoop, calls=%fused_computation.76 | loop fusion | flops 2211840 | bytes 4884480 | tf_op jit(solution)/shard_map/sub | solution.py:53
  70.4 2.3 %copy.279 = f32[12,16,12,2]{3,1,2,0:T(8,128)S(1)} copy(f32[12,16,12,2]{2,1,3,0:T(8,128)} %collective-permute-done.6) | data formatting | bytes 36864 | tf_op jit(solution)/shard_map/ppermute | solution.py:17
  72.6 1.7 %collective-permute-done.7 = f32[12,16,12,2]{2,1,3,0:T(8,128)} collective-permute-done((f32[12,16,12,2]{2,1,3,0:T(8,128)}, f32[12,16,12,2]{2,1,3,0:T(8,128)}, u32[]{:S(2)}, u32[]{:S(2)}) %collective-permute-start.7) | collective-permute-done | bytes 18464 | tf_op jit(solution)/shard_map/ppermute | solution.py:19
  74.3 2.3 %copy.282 = f32[12,16,12,2]{3,1,2,0:T(8,128)S(1)} copy(f32[12,16,12,2]{2,1,3,0:T(8,128)} %collective-permute-done.7) | data formatting | bytes 36864 | tf_op jit(solution)/shard_map/ppermute | solution.py:19
  76.6 1.0 pad_maximum_fusion
  79.1 1.5 %fusion.6 = f32[12,16,8,129]{3,1,2,0:T(8,128)S(1)} fusion(f32[12,16,8,131]{3,1,2,0:T(8,128)S(1)} %fusion.11, f32[12,16,8,130]{3,1,2,0:T(8,128)S(1)} %minimum_add_fusion.1, f32[12,16,12,2]{3,1,2,0:T(8,128)S(1)} %copy.282, f32[12,16,12,128]{3,1,2,0:T(8,128)S(1)} %constant_dynamic-update-slice_fusion, f32[12,16,12,2]{3,1,2,0:T(8,128)S(1)} %copy.279, ...), kind=kLoop, calls=%fused_computation.19 | loop fusion | flops 1981440 | bytes 4535424 | tf_op jit(solution)/shard_map/sub | solution.py:53
  80.8 1.2 multiply_reduce_fusion
  82.3 1.3 collective-permute-start.8
  83.7 1.4 collective-permute-start.9
  85.4 1.5 %fusion.20 = f32[12,17,8,128]{3,1,2,0:T(8,128)} fusion(f32[12,16,8,128]{3,1,2,0:T(8,128)S(1)} %get-tuple-element.6, f32[12,18,8,128]{3,1,2,0:T(8,128)S(1)} %minimum_add_fusion.2, f32[17,8,128]{2,0,1:T(8,128)S(1)} %copy-done.18, pred[17,8,128]{2,0,1:T(8,128)(4,1)S(1)} %copy-done.29), kind=kLoop, calls=%fused_computation.48 | loop fusion | flops 1253376 | bytes 3380224 | tf_op jit(solution)/shard_map/mul | solution.py:51
  86.9 21.7 %all-reduce.9.cloned.1.call-done = f32[16,8,128]{2,0,1:T(8,128)} async-done(((f32[16,8,128]{2,0,1:T(8,128)}), f32[16,8,128]{2,0,1:T(8,128)}) %all-reduce.9.cloned.1.call-update) | async-done | bytes 65552 | tf_op jit(solution)/shard_map/psum | solution.py:89
  108.6 1.5 %add_divide_fusion = f32[16,8,128]{2,0,1:T(8,128)} fusion(f32[16,8,128]{2,0,1:T(8,128)} %all-reduce.9.cloned.1.call-done, f32[16,8,128]{2,1,0:T(8,128)S(1)} %copy-done.27), kind=kLoop, calls=%fused_computation.119 | loop fusion | flops 49152 | bytes 196608 | tf_op jit(solution)/shard_map/div | solution.py:90
  110.1 0.8 copy-done.10
  111.0 1.8 %fusion.51 = (f32[12,16,12,2]{3,1,2,0:T(8,128)}, f32[12,16,12,2]{3,1,2,0:T(8,128)}) fusion(f32[12,16,12,128]{3,1,2,0:T(8,128)S(1)} %pad_maximum_fusion.10), kind=kLoop, calls=%fused_computation.138 | loop fusion | bytes 73728 | tf_op jit(solution)/shard_map/slice | solution.py:14
  113.0 3.2 %copy.290 = f32[12,16,12,2]{2,1,3,0:T(8,128)} copy(f32[12,16,12,2]{3,1,2,0:T(8,128)} %get-tuple-element.13) | data formatting | bytes 36864 | tf_op jit(solution)/shard_map/slice | solution.py:14
  116.2 4.1 %collective-permute-start.10 = (f32[12,16,12,2]{2,1,3,0:T(8,128)}, f32[12,16,12,2]{2,1,3,0:T(8,128)}, u32[]{:S(2)}, u32[]{:S(2)}) collective-permute-start(f32[12,16,12,2]{2,1,3,0:T(8,128)} %copy.290), channel_id=1, source_target_pairs={{0,1},{1,2},{2,3},{4,5},{5,6},{6,7},{8,9},{9,10},{10,11},{12,13},{... | collective-permute-start | bytes 55304 | tf_op jit(solution)/shard_map/ppermute | solution.py:17
  120.3 3.2 %copy.292 = f32[12,16,12,2]{2,1,3,0:T(8,128)} copy(f32[12,16,12,2]{3,1,2,0:T(8,128)} %get-tuple-element.14) | data formatting | bytes 36864 | tf_op jit(solution)/shard_map/slice | solution.py:13
  123.5 1.5 %collective-permute-start.11 = (f32[12,16,12,2]{2,1,3,0:T(8,128)}, f32[12,16,12,2]{2,1,3,0:T(8,128)}, u32[]{:S(2)}, u32[]{:S(2)}) collective-permute-start(f32[12,16,12,2]{2,1,3,0:T(8,128)} %copy.292), channel_id=1, source_target_pairs={{1,0},{2,1},{3,2},{5,4},{6,5},{7,6},{9,8},{10,9},{11,10},{13,12},{... | collective-permute-start | bytes 55304 | tf_op jit(solution)/shard_map/ppermute | solution.py:19
  125.0 1.2 fusion.26
  126.2 2.3 %copy.291 = f32[12,16,12,2]{3,1,2,0:T(8,128)S(1)} copy(f32[12,16,12,2]{2,1,3,0:T(8,128)} %collective-permute-done.10) | data formatting | bytes 36864 | tf_op jit(solution)/shard_map/ppermute | solution.py:17
  128.5 3.2 %collective-permute-done.11 = f32[12,16,12,2]{2,1,3,0:T(8,128)} collective-permute-done((f32[12,16,12,2]{2,1,3,0:T(8,128)}, f32[12,16,12,2]{2,1,3,0:T(8,128)}, u32[]{:S(2)}, u32[]{:S(2)}) %collective-permute-start.11) | collective-permute-done | bytes 18464 | tf_op jit(solution)/shard_map/ppermute | solution.py:19
  131.6 2.3 %copy.294 = f32[12,16,12,2]{3,1,2,0:T(8,128)S(1)} copy(f32[12,16,12,2]{2,1,3,0:T(8,128)} %collective-permute-done.11) | data formatting | bytes 36864 | tf_op jit(solution)/shard_map/ppermute | solution.py:19
  133.9 1.0 pad_maximum_fusion.1
  136.3 1.5 %fusion = f32[12,16,8,129]{3,1,2,0:T(8,128)S(1)} fusion(f32[12,16,8,131]{3,1,2,0:T(8,128)S(1)} %fusion.5, f32[12,16,8,130]{3,1,2,0:T(8,128)S(1)} %minimum_add_fusion, f32[12,16,12,2]{3,1,2,0:T(8,128)S(1)} %copy.294, f32[12,16,2,128]{3,1,2,0:T(8,128)S(1)} %collective-permute-done.9, f32[12,16,8,128]{3,1,2,0:T(8,128)S(1)} %get-tuple-element.6, ...), kind=kLoop, calls=%fused_computation.3 | loop fusion | flops 2774016 | bytes 4535424 | tf_op jit(solution)/shard_map/sub | solution.py:53
  138.4 1.1 copy.301
  (115 shorter events, 9.5 us)
Async XLA Ops:
  6.5 11.5 %copy-start = (f32[12,16,8,128]{3,2,1,0:T(8,128)S(1)}, f32[12,16,8,128]{3,2,1,0:T(8,128)}, u32[]{:S(2)}) copy-start(f32[12,16,8,128]{3,2,1,0:T(8,128)} %param.8) | copy-start | bytes 2359300
  6.5 44.5 %all-reduce.7.cloned.1.call-start = ((), (), s32[]{:S(2)}) async-start(), calls=%async_computation | async-start | bytes 131072 | tf_op jit(solution)/shard_map/psum | solution.py:89
  15.4 13.5 %collective-permute-start = (f32[50,2,128]{2,0,1:T(8,128)S(1)}, f32[50,2,128]{2,0,1:T(8,128)S(1)}, u32[]{:S(2)}, u32[]{:S(2)}) collective-permute-start(f32[50,2,128]{2,0,1:T(8,128)S(1)} %get-tuple-element.25), channel_id=1, source_target_pairs={{0,4},{4,8},{8,12},{1,5},{5,9},{9,13},{2,6},{6,10},{10,14},{3,7},{... | collective-permute-start | bytes 153608 | tf_op jit(solution)/shard_map/ppermute | solution.py:17
  16.7 8.6 %copy-start.32 = (f32[16]{0:T(128)S(1)}, f32[16]{0:T(128)}, u32[]{:S(2)}) copy-start(f32[16]{0:T(128)} %param.15) | copy-start | bytes 196
  16.7 8.6 %copy-start.33 = (s32[12]{0:T(128)S(1)}, s32[12]{0:T(128)}, u32[]{:S(2)}) copy-start(s32[12]{0:T(128)} %param.14) | copy-start | bytes 148
  16.7 12.2 %collective-permute-start.1 = (f32[50,2,128]{2,0,1:T(8,128)S(1)}, f32[50,2,128]{2,0,1:T(8,128)S(1)}, u32[]{:S(2)}, u32[]{:S(2)}) collective-permute-start(f32[50,2,128]{2,0,1:T(8,128)S(1)} %get-tuple-element.26), channel_id=1, source_target_pairs={{4,0},{8,4},{12,8},{5,1},{9,5},{13,9},{6,2},{10,6},{14,10},{7,3},{... | collective-permute-start | bytes 153608 | tf_op jit(solution)/shard_map/ppermute | solution.py:19
  19.0 33.5 %collective-permute-start.2 = (f32[12,16,2,128]{3,1,2,0:T(8,128)}, f32[12,16,2,128]{3,1,2,0:T(8,128)S(1)}, u32[]{:S(2)}, u32[]{:S(2)}) collective-permute-start(f32[12,16,2,128]{3,1,2,0:T(8,128)} %get-tuple-element.22), channel_id=1, source_target_pairs={{0,4},{4,8},{8,12},{1,5},{5,9},{9,13},{2,6},{6,10},{10,14},{3,7},{... | collective-permute-start | bytes 589832 | tf_op jit(solution)/shard_map/ppermute | solution.py:17
  24.1 28.6 %collective-permute-start.3 = (f32[12,16,2,128]{3,1,2,0:T(8,128)}, f32[12,16,2,128]{3,1,2,0:T(8,128)S(1)}, u32[]{:S(2)}, u32[]{:S(2)}) collective-permute-start(f32[12,16,2,128]{3,1,2,0:T(8,128)} %get-tuple-element.21), channel_id=1, source_target_pairs={{4,0},{8,4},{12,8},{5,1},{9,5},{13,9},{6,2},{10,6},{14,10},{7,3},{... | collective-permute-start | bytes 589832 | tf_op jit(solution)/shard_map/ppermute | solution.py:19
  26.4 82.2 %all-reduce.9.cloned.1.call-start = ((), (), s32[]{:S(2)}) async-start(), calls=%async_computation.1 | async-start | bytes 131072 | tf_op jit(solution)/shard_map/psum | solution.py:89
  26.4 0.7 copy-start.11
  26.7 0.7 copy-start.17
  26.7 0.7 copy-start.28
  29.1 23.6 %copy-start.9 = (f32[16,11,128]{2,0,1:T(8,128)}, f32[16,11,128]{2,0,1:T(8,128)S(1)}, u32[]{:S(2)}) copy-start(f32[16,11,128]{2,0,1:T(8,128)S(1)} %slice_multiply_fusion.18) | copy-start | bytes 270340
  29.1 10.5 %collective-permute-start.4 = (f32[50,12,2]{2,0,1:T(8,128)S(1)}, f32[50,12,2]{2,0,1:T(8,128)S(1)}, u32[]{:S(2)}, u32[]{:S(2)}) collective-permute-start(f32[50,12,2]{2,0,1:T(8,128)S(1)} %get-tuple-element.23), channel_id=1, source_target_pairs={{0,1},{1,2},{2,3},{4,5},{5,6},{6,7},{8,9},{9,10},{10,11},{12,13},{... | collective-permute-start | bytes 14408 | tf_op jit(solution)/shard_map/ppermute | solution.py:17
  32.6 11.7 %collective-permute-start.5 = (f32[50,12,2]{2,0,1:T(8,128)S(1)}, f32[50,12,2]{2,0,1:T(8,128)S(1)}, u32[]{:S(2)}, u32[]{:S(2)}) collective-permute-start(f32[50,12,2]{2,0,1:T(8,128)S(1)} %get-tuple-element.24), channel_id=1, source_target_pairs={{1,0},{2,1},{3,2},{5,4},{6,5},{7,6},{9,8},{10,9},{11,10},{13,12},{... | collective-permute-start | bytes 14408 | tf_op jit(solution)/shard_map/ppermute | solution.py:19
  34.6 33.1 %copy-start.30 = (pred[16,9,128]{2,0,1:T(8,128)(4,1)}, pred[16,9,128]{2,0,1:T(8,128)(4,1)S(1)}, u32[]{:S(2)}) copy-start(pred[16,9,128]{2,0,1:T(8,128)(4,1)S(1)} %get-tuple-element.7) | copy-start | bytes 55300
  44.7 6.4 %copy-start.26 = (f32[16,8,128]{2,1,0:T(8,128)S(1)}, f32[16,8,128]{2,1,0:T(8,128)}, u32[]{:S(2)}) copy-start(f32[16,8,128]{2,1,0:T(8,128)} %param.13) | copy-start | bytes 196612
  44.8 7.7 %copy-start.6 = (f32[16,8,131]{2,0,1:T(8,128)}, f32[16,8,131]{2,0,1:T(8,128)S(1)}, u32[]{:S(2)}) copy-start(f32[16,8,131]{2,0,1:T(8,128)S(1)} %maximum_multiply_fusion) | copy-start | bytes 201220
  55.8 11.9 %copy-start.19 = (f32[16,9,128]{2,0,1:T(8,128)S(1)}, f32[16,9,128]{2,0,1:T(8,128)}, u32[]{:S(2)}) copy-start(f32[16,9,128]{2,0,1:T(8,128)} %get-tuple-element.8) | copy-start | bytes 221188
  59.0 11.4 %collective-permute-start.6 = (f32[12,16,12,2]{2,1,3,0:T(8,128)}, f32[12,16,12,2]{2,1,3,0:T(8,128)}, u32[]{:S(2)}, u32[]{:S(2)}) collective-permute-start(f32[12,16,12,2]{2,1,3,0:T(8,128)} %copy.278), channel_id=1, source_target_pairs={{0,1},{1,2},{2,3},{4,5},{5,6},{6,7},{8,9},{9,10},{10,11},{12,13},{... | collective-permute-start | bytes 55304 | tf_op jit(solution)/shard_map/ppermute | solution.py:17
  66.2 8.1 %collective-permute-start.7 = (f32[12,16,12,2]{2,1,3,0:T(8,128)}, f32[12,16,12,2]{2,1,3,0:T(8,128)}, u32[]{:S(2)}, u32[]{:S(2)}) collective-permute-start(f32[12,16,12,2]{2,1,3,0:T(8,128)} %copy.280), channel_id=1, source_target_pairs={{1,0},{2,1},{3,2},{5,4},{6,5},{7,6},{9,8},{10,9},{11,10},{13,12},{... | collective-permute-start | bytes 55304 | tf_op jit(solution)/shard_map/ppermute | solution.py:19
  76.6 1.0 copy-start.7
  78.1 0.9 copy-start.13
  78.1 1.0 copy-start.15
  78.1 1.0 copy-start.22
  79.1 1.6 %copy-start.1 = (f32[12,16,8,128]{3,2,1,0:T(8,128)S(1)}, f32[12,16,8,128]{3,2,1,0:T(8,128)}, u32[]{:S(2)}) copy-start(f32[12,16,8,128]{3,2,1,0:T(8,128)} %param.8) | copy-start | bytes 2359300
  79.1 1.6 %copy-start.3 = (f32[12,16,9,128]{3,1,2,0:T(8,128)S(1)}, f32[12,16,9,128]{3,1,2,0:T(8,128)}, u32[]{:S(2)}) copy-start(f32[12,16,9,128]{3,1,2,0:T(8,128)} %fusion.31) | copy-start | bytes 2654212
  79.1 1.8 %copy-start.4 = (f32[12,17,8,128]{3,1,2,0:T(8,128)S(1)}, f32[12,17,8,128]{3,1,2,0:T(8,128)}, u32[]{:S(2)}) copy-start(f32[12,17,8,128]{3,1,2,0:T(8,128)} %fusion.14) | copy-start | bytes 2506756
  79.1 1.8 %copy-start.25 = (f32[16,8,128]{2,0,1:T(8,128)S(1)}, f32[16,8,128]{2,0,1:T(8,128)}, u32[]{:S(2)}) copy-start(f32[16,8,128]{2,0,1:T(8,128)} %add_divide_fusion.1) | copy-start | bytes 196612
  80.8 1.2 copy-start.12
  82.3 27.7 %collective-permute-start.8 = (f32[12,16,2,128]{3,1,2,0:T(8,128)S(1)}, f32[12,16,2,128]{3,1,2,0:T(8,128)S(1)}, u32[]{:S(2)}, u32[]{:S(2)}) collective-permute-start(f32[12,16,2,128]{3,1,2,0:T(8,128)S(1)} %get-tuple-element.19), channel_id=1, source_target_pairs={{0,4},{4,8},{8,12},{1,5},{5,9},{9,13},{2,6},{6,10},{10,14},{3,7},{... | collective-permute-start | bytes 589832 | tf_op jit(solution)/shard_map/ppermute | solution.py:17
  83.6 1.8 %copy-start.18 = (f32[17,8,128]{2,0,1:T(8,128)S(1)}, f32[17,8,128]{2,0,1:T(8,128)}, u32[]{:S(2)}) copy-start(f32[17,8,128]{2,0,1:T(8,128)} %copy-done.17) | copy-start | bytes 208900
  83.6 1.8 %copy-start.29 = (pred[17,8,128]{2,0,1:T(8,128)(4,1)S(1)}, pred[17,8,128]{2,0,1:T(8,128)(4,1)}, u32[]{:S(2)}) copy-start(pred[17,8,128]{2,0,1:T(8,128)(4,1)} %copy-done.28) | copy-start | bytes 52228
  83.7 26.4 %collective-permute-start.9 = (f32[12,16,2,128]{3,1,2,0:T(8,128)S(1)}, f32[12,16,2,128]{3,1,2,0:T(8,128)S(1)}, u32[]{:S(2)}, u32[]{:S(2)}) collective-permute-start(f32[12,16,2,128]{3,1,2,0:T(8,128)S(1)} %get-tuple-element.20), channel_id=1, source_target_pairs={{4,0},{8,4},{12,8},{5,1},{9,5},{13,9},{6,2},{10,6},{14,10},{7,3},{... | collective-permute-start | bytes 589832 | tf_op jit(solution)/shard_map/ppermute | solution.py:19
  85.4 23.1 %copy-start.27 = (f32[16,8,128]{2,1,0:T(8,128)S(1)}, f32[16,8,128]{2,1,0:T(8,128)}, u32[]{:S(2)}) copy-start(f32[16,8,128]{2,1,0:T(8,128)} %param.13) | copy-start | bytes 196612
  110.0 0.9 copy-start.10
  113.0 12.0 %copy-start.20 = (f32[16,9,128]{2,0,1:T(8,128)S(1)}, f32[16,9,128]{2,0,1:T(8,128)}, u32[]{:S(2)}) copy-start(f32[16,9,128]{2,0,1:T(8,128)} %get-tuple-element.8) | copy-start | bytes 221188
  113.0 12.0 %copy-start.21 = (f32[16,9,128]{2,0,1:T(8,128)S(1)}, f32[16,9,128]{2,0,1:T(8,128)}, u32[]{:S(2)}) copy-start(f32[16,9,128]{2,0,1:T(8,128)} %slice_multiply_fusion.19) | copy-start | bytes 221188
  113.0 12.0 %copy-start.31 = (pred[16,9,128]{2,0,1:T(8,128)(4,1)S(1)}, pred[16,9,128]{2,0,1:T(8,128)(4,1)}, u32[]{:S(2)}) copy-start(pred[16,9,128]{2,0,1:T(8,128)(4,1)} %copy-done.30) | copy-start | bytes 55300
  116.2 10.0 %collective-permute-start.10 = (f32[12,16,12,2]{2,1,3,0:T(8,128)}, f32[12,16,12,2]{2,1,3,0:T(8,128)}, u32[]{:S(2)}, u32[]{:S(2)}) collective-permute-start(f32[12,16,12,2]{2,1,3,0:T(8,128)} %copy.290), channel_id=1, source_target_pairs={{0,1},{1,2},{2,3},{4,5},{5,6},{6,7},{8,9},{9,10},{10,11},{12,13},{... | collective-permute-start | bytes 55304 | tf_op jit(solution)/shard_map/ppermute | solution.py:17
  123.5 8.1 %collective-permute-start.11 = (f32[12,16,12,2]{2,1,3,0:T(8,128)}, f32[12,16,12,2]{2,1,3,0:T(8,128)}, u32[]{:S(2)}, u32[]{:S(2)}) collective-permute-start(f32[12,16,12,2]{2,1,3,0:T(8,128)} %copy.292), channel_id=1, source_target_pairs={{1,0},{2,1},{3,2},{5,4},{6,5},{7,6},{9,8},{10,9},{11,10},{13,12},{... | collective-permute-start | bytes 55304 | tf_op jit(solution)/shard_map/ppermute | solution.py:19
  133.9 1.0 copy-start.8
  135.4 0.9 copy-start.14
  135.4 1.0 copy-start.16
  135.4 1.0 copy-start.23
  136.3 1.6 %copy-start.2 = (f32[12,16,9,128]{3,1,2,0:T(8,128)S(1)}, f32[12,16,9,128]{3,1,2,0:T(8,128)}, u32[]{:S(2)}) copy-start(f32[12,16,9,128]{3,1,2,0:T(8,128)} %fusion.26) | copy-start | bytes 2654212
  136.3 1.6 %copy-start.5 = (f32[12,17,8,128]{3,1,2,0:T(8,128)S(1)}, f32[12,17,8,128]{3,1,2,0:T(8,128)}, u32[]{:S(2)}) copy-start(f32[12,17,8,128]{3,1,2,0:T(8,128)} %fusion.20) | copy-start | bytes 2506756
  136.3 1.6 %copy-start.24 = (f32[16,8,128]{2,0,1:T(8,128)S(1)}, f32[16,8,128]{2,0,1:T(8,128)}, u32[]{:S(2)}) copy-start(f32[16,8,128]{2,0,1:T(8,128)} %add_divide_fusion) | copy-start | bytes 196612
Sparse Core Ops, SparseCore 0:
  26.5 24.4 all-reduce.6
  85.5 22.9 all-reduce.8
where the time goes:
time: 147 us; the launch traced here: 146 us
  waiting for transfers between devices  40.2 us (27%)
  local copies, waits for them, and re-layouts  32.7 us (22%)
  starting transfers between devices  27.6 us (19%)
  other arithmetic  25.3 us (17%)
  between operations  14.1 us (10%)
  blocking collectives  6.42 us (4%)
    psum x2, waiting for transfers between devices, on_device(): prey_total = lax.psum(prey_local, 'tracer')  25.6 us
    ppermute x6, starting transfers between devices, with_halo(): lax.ppermute(tail, axis, [(i, (i + 1) % count) for i in range(ends)])  19.3 us
    slice x7, local copies, waits for them, and re-layouts, with_halo(): lax.slice_in_dim(cells, cells.shape[dim] - width, cells.shape[dim], axis=...  10.2 us
    ppermute x6, waiting for transfers between devices, with_halo(): lax.ppermute(head, axis, [((i + 1) % count, i) for i in range(ends)])  9.6 us
    ppermute x6, starting transfers between devices, with_halo(): lax.ppermute(head, axis, [((i + 1) % count, i) for i in range(ends)])  8.26 us
    slice x3, local copies, waits for them, and re-layouts, with_halo(): head = lax.slice_in_dim(cells, 0, width, axis=dim)  7.12 us
    sub x4, other arithmetic, face_terms(): carried = carried - face_kappa * window(jump_face, 1, length + 2, direction)  6.93 us
    all_gather x1, blocking collectives, on_device(): all_fluxes = lax.all_gather(fluxes, 'tracer', axis=1, tiled=True)  6.42 us
  transfers between devices with their start and end apart: 14, of which 6 were waited for; matrix products, arithmetic and copies ran while one was open for 19% of the time, Pallas kernels for 0%

commit v1 on v0

--- a/solution.py
+++ b/solution.py
@@ -1,9 +1,15 @@
+import functools
+
 import jax
 import jax.numpy as jnp
 from jax import lax
+from jax.experimental import pallas as pl
+from jax.experimental.pallas import tpu as pltpu
 from jax.sharding import PartitionSpec as P
 
 STEPS = 2
+SUB = 8
+LIM = 48 * 1024 * 1024
 
 
 def with_halo(cells, sides, width):
@@ -54,7 +60,7 @@
     return window(carried, 0, length, direction) - window(carried, 1, length + 1, direction)
 
 
-def on_device(tracers, fluxes, diff_east, diff_north, column_depth, grazers, groups, preference):
+def plain(tracers, fluxes, diff_east, diff_north, column_depth, grazers, groups, preference):
     tr_dev, levels, rows_dev, cols_dev = tracers.shape
     total_tracers = tr_dev * lax.axis_size("tracer")
     level_index = lax.broadcasted_iota(jnp.int32, (levels, rows_dev, cols_dev), 0)
@@ -99,6 +105,583 @@
     return tracer_field
 
 
+class Geo:
+    def __init__(self, tr_dev, levels, rows, cols):
+        self.T, self.L, self.R, self.C = tr_dev, levels, rows, cols
+        self.LH = levels // SUB
+        self.tile = rows * levels
+        self.slots = -(-(tr_dev + 3) // 4) * 4
+        self.slots2 = -(-tr_dev // 4) * 4
+        at = 0
+        self.off = {}
+        for name, count in (
+            ("hx", (rows + 3) * levels),
+            ("px", (rows + 1) * levels),
+            ("mx", (rows + 1) * levels),
+            ("kx", (rows + 1) * SUB),
+            ("hy", self.tile),
+            ("py", self.tile),
+            ("my", self.tile),
+            ("ky", rows * SUB),
+            ("hz", self.tile),
+            ("pz", self.tile),
+            ("mz", self.tile),
+            ("hs", SUB),
+            ("ps", SUB),
+            ("ms", SUB),
+            ("ks", SUB),
+        ):
+            self.off[name] = at
+            at += count
+        self.coefs = at
+
+
+def lanes(shape=(SUB, 128)):
+    return lax.broadcasted_iota(jnp.int32, shape, 1)
+
+
+def sublanes(shape=(SUB, 128)):
+    return lax.broadcasted_iota(jnp.int32, shape, 0)
+
+
+def roll(v, by, axis):
+    by = by % v.shape[axis]
+    return v if by == 0 else pltpu.roll(v, by, axis)
+
+
+def pack_strips(parts):
+    lane = lanes()
+    packed = jnp.zeros((SUB, 128), jnp.float32)
+    for k, part in enumerate(parts):
+        inside = (lane >= 8 * k + 2) & (lane < 8 * k + 6)
+        packed = jnp.where(inside, roll(part, 8 * k + 4, 1), packed)
+    return packed
+
+
+def message_strips(packed, low):
+    place = lanes() % 8
+    out = jnp.zeros((SUB, 128), jnp.float32)
+    for m, one in enumerate(packed):
+        moved = roll(one, 2 * m - (4 if low else 2), 1)
+        out = jnp.where((place == 2 * m) | (place == 2 * m + 1), moved, out)
+    return out
+
+
+def full_strips(own, from_lower, from_upper, m):
+    place = lanes() % 8
+    out = jnp.where(place < 2, roll(from_lower, -2 * m, 1), roll(from_upper, 6 - 2 * m, 1))
+    out = jnp.where((place >= 2) & (place < 4), roll(own, -2, 1), out)
+    return jnp.where((place >= 4) & (place < 6), roll(own, 2, 1), out)
+
+
+def taste_of(groups_ref, pref_ref, t):
+    return pref_ref[groups_ref[t]]
+
+
+def is_even(axis):
+    return lax.rem(lax.axis_index(axis), 2) == 0
+
+
+def edges_kernel(g, fluxes_ref, out_ref):
+    base = g.R * SUB
+    out_ref[0:SUB, :] = fluxes_ref[pl.ds(g.R - 1, SUB, stride=g.R), :]
+    parts = []
+    for r in range(g.R):
+        row = fluxes_ref[pl.ds(base + r, SUB, stride=g.R), :]
+        parts += [row] * g.LH
+    out_ref[SUB : 2 * SUB, :] = pack_strips(parts)
+
+
+def load_kernel(g, tracers_ref, groups_ref, pref_ref, field_ref, strips_ref, prey_ref):
+    def one(t, carry):
+        taste = taste_of(groups_ref, pref_ref, t)
+        base = pl.multiple_of(t * g.tile, g.tile)
+        parts = []
+        for r in range(g.R):
+            for lh in range(g.LH):
+                at = (r * g.LH + lh) * SUB
+                v = tracers_ref[pl.ds(base + lh * SUB * g.R + r, SUB, stride=g.R), :]
+                field_ref[pl.ds(base + at, SUB), :] = v
+                parts.append(v)
+                prey_ref[at : at + SUB, :] += taste * v
+        strips_ref[pl.ds(pl.multiple_of(t * SUB, SUB), SUB), :] = pack_strips(parts)
+        return carry
+
+    prey_ref[...] = jnp.zeros_like(prey_ref)
+    lax.fori_loop(0, g.T, one, 0)
+
+
+def first_messages_kernel(
+    g, field_ref, strips_ref, mine_ref, other_ref, depth_ref, east_ref, north_ref,
+    xev_ref, xod_ref, yev_ref, yod_ref,
+):
+    x_even, y_even = is_even("gx"), is_even("gy")
+    first = lax.axis_index("tracer") == 0
+    single = lax.axis_size("tracer") != 2
+    zero = jnp.zeros((SUB, 128), jnp.float32)
+
+    def put(ref_ev, ref_od, at, even, low, high):
+        ref_ev[at, :] = jnp.where(even, high, low)
+        ref_od[at, :] = jnp.where(even, low, high)
+
+    def one(t, carry):
+        base = pl.multiple_of(t * g.tile, g.tile)
+        for i in range(2 * g.LH):
+            low = field_ref[pl.ds(base + i * SUB, SUB), :]
+            high = field_ref[pl.ds(base + g.tile - 2 * g.L + i * SUB, SUB), :]
+            at = pl.ds(pl.multiple_of(t * 2 * g.L, SUB) + i * SUB, SUB)
+            put(xev_ref, xod_ref, at, x_even, low, high)
+        return carry
+
+    lax.fori_loop(0, g.T, one, 0)
+    mine, other = mine_ref[...], other_ref[...]
+    lower = mine if single else jnp.where(first, mine, other)
+    upper = other if single else jnp.where(first, other, mine)
+    at = g.T * 2 * g.L
+    for lh, half in enumerate((lower, upper)):
+        put(xev_ref, xod_ref, slice(at, at + SUB), x_even, zero, half[0:SUB])
+        at += SUB
+    depth = depth_ref[...].astype(jnp.float32)
+    put(xev_ref, xod_ref, slice(at, at + SUB), x_even, depth, roll(depth, 2, 0))
+    at += SUB
+    put(xev_ref, xod_ref, slice(at, at + SUB), x_even, zero, roll(east_ref[...], 1, 0))
+
+    half_of = (lanes() // 8) % g.LH
+    packed = [strips_ref[t * SUB : (t + 1) * SUB, :] for t in range(g.T)]
+    packed.append(pack_strips(spread_rows(g, depth)))
+    packed.append(jnp.where(half_of == 0, lower[SUB : 2 * SUB], upper[SUB : 2 * SUB]))
+    packed.append(pack_strips(spread_rows(g, north_ref[...])))
+    for v in range(0, len(packed), 4):
+        low = message_strips(packed[v : v + 4], True)
+        high = message_strips(packed[v : v + 4], False)
+        put(yev_ref, yod_ref, slice(v * 2, v * 2 + SUB), y_even, low, high)
+
+
+def spread_rows(g, rows):
+    parts = []
+    for r in range(g.R):
+        parts += [jnp.broadcast_to(rows[r : r + 1, :], (SUB, 128))] * g.LH
+    return parts
+
+
+def coefficients(
+    g, cf, xl, yl, yu, mine_ref, other_ref, fluxes_mine, fluxes_other, depth_ref, east_ref, north_ref
+):
+    lane, sub = lanes(), sublanes()
+    first = lax.axis_index("tracer") == 0
+    single = lax.axis_size("tracer") != 2
+    depth = depth_ref[...].astype(jnp.float32)
+    depth_low, depth_high = xl(g.LH)
+    east = east_ref[...]
+    east_low, _ = xl(g.LH + 1)
+    north = north_ref[...]
+    level = [(sub + SUB * lh).astype(jnp.float32) for lh in range(g.LH)]
+
+    def spread(rows, r):
+        return jnp.broadcast_to(rows[r : r + 1, :], (SUB, 128))
+
+    depths = [spread(depth_low, 0), spread(depth_low, 1)]
+    depths += [spread(depth, r) for r in range(g.R)]
+    depths += [spread(depth_high, 0), spread(depth_high, 1)]
+    wet = [[level[lh] < d for lh in range(g.LH)] for d in depths]
+
+    def flux(dim, r, lh):
+        at = pl.ds(dim * g.R * SUB + r, SUB, stride=g.R)
+        a, b = fluxes_mine[at, :], fluxes_other[at, :]
+        if single:
+            return (a, b)[lh]
+        return jnp.where(first, (a, b)[lh], (b, a)[lh])
+
+    def store(name, index, value):
+        at = g.off[name] + index * SUB
+        cf[at : at + SUB, :] = value
+
+    def put(name, index, opened, h, f):
+        f = jnp.where(opened, f, 0.0)
+        store("h" + name, h, jnp.where(opened, 0.5, 0.0))
+        store("p" + name, index, jnp.maximum(f, 0.0))
+        store("m" + name, index, jnp.minimum(f, 0.0))
+
+    for f in range(-1, g.R + 2):
+        for lh in range(g.LH):
+            opened = wet[f + 1][lh] & wet[f + 2][lh]
+            h = (f + 1) * g.LH + lh
+            if 0 <= f <= g.R:
+                below = xl(lh)[0] if f == 0 else flux(0, f - 1, lh)
+                put("x", f * g.LH + lh, opened, h, below)
+            else:
+                store("hx", h, jnp.where(opened, 0.5, 0.0))
+        if 0 <= f <= g.R:
+            store("kx", f, 2.0 * (spread(east_low, 0) if f == 0 else spread(east, f - 1)))
+
+    for r in range(g.R):
+        before = roll(depths[r + 2], 1, 1)
+        store("ky", r, 2.0 * roll(spread(north, r), 1, 1))
+        for lh in range(g.LH):
+            k = r * g.LH + lh
+            here = wet[r + 2][lh]
+            opened = here & (level[lh] < before) & (lane > 0)
+            put("y", k, opened, k, roll(flux(1, r, lh), 1, 1))
+        flux_z = [roll(flux(2, r, lh), 1, 0) for lh in range(g.LH)]
+        for lh in range(g.LH):
+            k = r * g.LH + lh
+            here = wet[r + 2][lh]
+            above = flux_z[lh] if lh == 0 else jnp.where(sub == 0, flux_z[lh - 1], flux_z[lh])
+            opened = here if lh else here & (sub > 0)
+            put("z", k, opened, k, above)
+
+    place = lane % 8
+    half_of = (lane // 8) % g.LH
+    mine, other = mine_ref[SUB : 2 * SUB, :], other_ref[SUB : 2 * SUB, :]
+    lower = mine if single else jnp.where(first, mine, other)
+    upper = other if single else jnp.where(first, other, mine)
+    own = (
+        pack_strips(spread_rows(g, depth)),
+        jnp.where(half_of == 0, lower, upper),
+        pack_strips(spread_rows(g, north)),
+    )
+    full = []
+    for i, one in enumerate(own):
+        slot = g.T + i
+        full.append(full_strips(one, yl(slot // 4), yu(slot // 4), slot % 4))
+    wet_s = (sub + SUB * half_of).astype(jnp.float32) < full[0]
+    opened = jnp.where(wet_s, 1.0, 0.0) * roll(jnp.where(wet_s, 1.0, 0.0), 1, 1)
+    opened = (opened > 0.0) & (place != 0) & (place != 4)
+    put("s", 0, opened, 0, roll(full[1], 1, 1))
+    store("ks", 0, 2.0 * roll(full[2], 1, 1))
+
+
+def limited(a, b):
+    least, most = jnp.minimum(a, b), jnp.maximum(a, b)
+    return jnp.maximum(least, jnp.minimum(most, 0.0))
+
+
+def advance(g, cf, strip_fix, at_row, taste, factor, emit):
+    lane, sub = lanes(), sublanes()
+    ends = (lane == 0) | (lane == 127)
+    top, bottom = sub == 0, sub == SUB - 1
+
+    def coef(name, index):
+        at = g.off[name] + index * SUB
+        return cf[at : at + SUB, :]
+
+    slope_fix, carried_fix = strip_fix
+    before = {}
+    cell, jump_next, right, carried = {}, {}, {}, {}
+    for lh in range(g.LH):
+        c2, c1, c0 = at_row(-2, lh), at_row(-1, lh), at_row(0, lh)
+        j1 = coef("hx", lh) * (c1 - c2)
+        j0 = coef("hx", g.LH + lh) * (c0 - c1)
+        s1 = limited(j1, j0)
+        cell[lh], jump_next[lh] = c0, j0
+        before[lh] = c1 + s1
+
+    def x_face(f, lh, left, right, jump):
+        k = f * g.LH + lh
+        return coef("px", k) * left + coef("mx", k) * right - coef("kx", f) * jump
+
+    for r in range(g.R):
+        news = []
+        here = [cell[lh] for lh in range(g.LH)]
+        for lh in range(g.LH):
+            k = r * g.LH + lh
+            c = cell[lh]
+            up = at_row(r + 1, lh)
+            j_low = jump_next[lh]
+            j_up = coef("hx", (r + 2) * g.LH + lh) * (up - c)
+            s = limited(j_low, j_up)
+            if r == 0:
+                carried[lh] = x_face(0, lh, before[lh], c - s, j_low)
+            left = c + s
+            up2 = at_row(r + 2, lh)
+            j_up2 = coef("hx", (r + 3) * g.LH + lh) * (up2 - up)
+            s_up = limited(j_up, j_up2)
+            out = x_face(r + 1, lh, left, up - s_up, j_up)
+            new = c + (carried[lh] - out)
+            carried[lh], cell[lh], jump_next[lh] = out, up, j_up
+            j = coef("hy", k) * (c - roll(c, 1, 1))
+            s = limited(j, roll(j, -1, 1))
+            s = jnp.where(ends, roll(slope_fix, -(8 * k + 2), 1), s)
+            flow = coef("py", k) * roll(c + s, 1, 1) + coef("my", k) * (c - s)
+            flow = flow - coef("ky", r) * j
+            new = new + (flow - roll(flow, -1, 1))
+            new = new + jnp.where(ends, roll(carried_fix, -(8 * k + 2), 1), 0.0)
+            at = k * SUB
+            new = new - (taste * factor[at : at + SUB, :]) * c
+            news.append(new)
+        def shift_down(v):
+            rolled = [roll(x, 1, 0) for x in v]
+            return [rolled[0]] + [
+                jnp.where(top, rolled[i - 1], rolled[i]) for i in range(1, g.LH)
+            ]
+
+        def shift_up(v):
+            rolled = [roll(x, -1, 0) for x in v]
+            return [
+                jnp.where(bottom, rolled[(i + 1) % g.LH], rolled[i]) for i in range(g.LH)
+            ]
+
+        index = [r * g.LH + lh for lh in range(g.LH)]
+        above = shift_down(here)
+        j = [coef("hz", k) * (c - a) for k, c, a in zip(index, here, above)]
+        s = [limited(a, b) for a, b in zip(j, shift_up(j))]
+        left = shift_down([c + v for c, v in zip(here, s)])
+        flow = [
+            coef("pz", k) * a + coef("mz", k) * (c - v)
+            for k, a, c, v in zip(index, left, here, s)
+        ]
+        for lh, (a, b, new) in enumerate(zip(flow, shift_up(flow), news)):
+            emit(r, lh, new + (a - b))
+
+
+def strip_fixes(g, cf, full):
+    def coef(name):
+        return cf[g.off[name] : g.off[name] + SUB, :]
+
+    at_two = lanes() % 8 == 2
+    j = coef("hs") * (full - roll(full, 1, 1))
+    s = limited(j, roll(j, -1, 1))
+    flow = coef("ps") * roll(full + s, 1, 1) + coef("ms") * (full - s) - coef("ks") * j
+    return jnp.where(at_two, s, roll(s, -4, 1)), jnp.where(at_two, flow, -roll(flow, -5, 1))
+
+
+def split_sides(even, ev, od):
+    return jnp.where(even, od, ev), jnp.where(even, ev, od)
+
+
+def set_factor(g, total, factor, grazers_ref, mine_ref, others, scale_rows=0):
+    for r in range(g.R):
+        for lh in range(g.LH):
+            at = (r * g.LH + lh) * SUB
+            prey = mine_ref[at : at + SUB, :]
+            for ref in others:
+                prey = prey + ref[scale_rows + at : scale_rows + at + SUB, :]
+            grazers = grazers_ref[pl.ds(lh * SUB * g.R + r, SUB, stride=g.R), :]
+            factor[at : at + SUB, :] = grazers / (1.0 + 4.0 * prey / total)
+
+
+def rows_of(g, field_ref, xev_ref, xod_ref, x_even, t):
+    base = pl.multiple_of(t * g.tile, g.tile)
+    halo = pl.multiple_of(t * 2 * g.L, 2 * g.L)
+    seen = {}
+
+    def at_row(r, lh):
+        if (r, lh) not in seen:
+            if 0 <= r < g.R:
+                seen[r, lh] = field_ref[pl.ds(base + r * g.L + lh * SUB, SUB), :]
+            else:
+                i = r + 2 if r < 0 else r - g.R
+                at = pl.ds(halo + i * g.L + lh * SUB, SUB)
+                low, high = split_sides(x_even, xev_ref[at, :], xod_ref[at, :])
+                seen[r, lh] = low if r < 0 else high
+        return seen[r, lh]
+
+    return at_row
+
+
+def y_sides(y_even, yev_ref, yod_ref, v):
+    at = pl.ds(v * SUB, SUB)
+    return split_sides(y_even, yev_ref[at, :], yod_ref[at, :])
+
+
+def unpack_strips(g, strips_ref, yev_ref, yod_ref, y_even, full_ref):
+    for t in range(g.T):
+        low, high = y_sides(y_even, yev_ref, yod_ref, t // 4)
+        full_ref[t * SUB : (t + 1) * SUB, :] = full_strips(
+            strips_ref[t * SUB : (t + 1) * SUB, :], low, high, t % 4
+        )
+
+
+def step_one_kernel(
+    g, total, n_other,
+    field_ref, strips_ref, xev_ref, xod_ref, yev_ref, yod_ref, mine_ref, other_ref,
+    bulk_ref, depth_ref, east_ref, north_ref, grazers_ref, groups_ref, pref_ref, *rest,
+):
+    others, rest = rest[:n_other], rest[n_other:]
+    (out_ref, xev2_ref, xod2_ref, yev2_ref, yod2_ref, strips2_ref, prey2_ref, cf,
+     factor, full_ref) = rest
+    x_even, y_even = is_even("gx"), is_even("gy")
+    prey_rows = 3 * g.R * SUB
+
+    def xl(i):
+        at = pl.ds(g.T * 2 * g.L + i * SUB, SUB)
+        return split_sides(x_even, xev_ref[at, :], xod_ref[at, :])
+
+    coefficients(
+        g, cf, xl,
+        lambda v: y_sides(y_even, yev_ref, yod_ref, v)[0],
+        lambda v: y_sides(y_even, yev_ref, yod_ref, v)[1],
+        mine_ref, other_ref, bulk_ref, others[0], depth_ref, east_ref, north_ref,
+    )
+    set_factor(
+        g, total, factor, grazers_ref, bulk_ref.at[prey_rows : prey_rows + g.tile], others[-1:], prey_rows
+    )
+    unpack_strips(g, strips_ref, yev_ref, yod_ref, y_even, full_ref)
+    prey2_ref[...] = jnp.zeros_like(prey2_ref)
+
+    def one(t, carry):
+        taste = taste_of(groups_ref, pref_ref, t)
+        base = pl.multiple_of(t * g.tile, g.tile)
+        halo = pl.multiple_of(t * 2 * g.L, 2 * g.L)
+        strip_at = pl.ds(pl.multiple_of(t * SUB, SUB), SUB)
+        news = {}
+
+        def emit(r, lh, new):
+            at = (r * g.LH + lh) * SUB
+            out_ref[pl.ds(base + at, SUB), :] = new
+            prey2_ref[at : at + SUB, :] += taste * new
+            news[r, lh] = new
+
+        advance(
+            g, cf, strip_fixes(g, cf, full_ref[strip_at, :]),
+            rows_of(g, field_ref, xev_ref, xod_ref, x_even, t), taste, factor, emit,
+        )
+        for i in range(2):
+            for lh in range(g.LH):
+                at = pl.ds(halo + i * g.L + lh * SUB, SUB)
+                low, high = news[i, lh], news[g.R - 2 + i, lh]
+                xev2_ref[at, :] = jnp.where(x_even, high, low)
+                xod2_ref[at, :] = jnp.where(x_even, low, high)
+        strips2_ref[strip_at, :] = pack_strips(
+            [news[r, lh] for r in range(g.R) for lh in range(g.LH)]
+        )
+        return carry
+
+    lax.fori_loop(0, g.T, one, 0)
+    packed = [strips2_ref[t * SUB : (t + 1) * SUB, :] for t in range(g.T)]
+    for v in range(0, g.T, 4):
+        low = message_strips(packed[v : v + 4], True)
+        high = message_strips(packed[v : v + 4], False)
+        yev2_ref[v * 2 : v * 2 + SUB, :] = jnp.where(y_even, high, low)
+        yod2_ref[v * 2 : v * 2 + SUB, :] = jnp.where(y_even, low, high)
+
+
+def step_two_kernel(
+    g, total, n_other,
+    field_ref, strips_ref, xev_ref, xod_ref, yev_ref, yod_ref, prey_ref, cf,
+    grazers_ref, groups_ref, pref_ref, *rest,
+):
+    others, (out_ref, factor, full_ref) = rest[:n_other], rest[n_other:]
+    x_even, y_even = is_even("gx"), is_even("gy")
+    set_factor(g, total, factor, grazers_ref, prey_ref, others)
+    unpack_strips(g, strips_ref, yev_ref, yod_ref, y_even, full_ref)
+
+    def one(t, carry):
+        taste = taste_of(groups_ref, pref_ref, t)
+        base = pl.multiple_of(t * g.tile, g.tile)
+        strip_at = pl.ds(pl.multiple_of(t * SUB, SUB), SUB)
+
+        def emit(r, lh, new):
+            out_ref[pl.ds(base + lh * SUB * g.R + r, SUB, stride=g.R), :] = new
+
+        advance(
+            g, cf, strip_fixes(g, cf, full_ref[strip_at, :]),
+            rows_of(g, field_ref, xev_ref, xod_ref, x_even, t), taste, factor, emit,
+        )
+        return carry
+
+    lax.fori_loop(0, g.T, one, 0)
+
+
+def call(body, outs, operands, scalars=(), scratch=()):
+    vmem, smem = pl.BlockSpec(memory_space=pltpu.VMEM), pl.BlockSpec(memory_space=pltpu.SMEM)
+    return pl.pallas_call(
+        body,
+        out_shape=[jax.ShapeDtypeStruct((rows, 128), jnp.float32) for rows in outs],
+        in_specs=[smem if i in scalars else vmem for i in range(len(operands))],
+        out_specs=[vmem] * len(outs),
+        scratch_shapes=[pltpu.VMEM((rows, 128), jnp.float32) for rows in scratch],
+        compiler_params=pltpu.CompilerParams(vmem_limit_bytes=LIM),
+    )(*operands)
+
+
+def pair_swap(values, axis, start):
+    pairs = []
+    for i in range(start, lax.axis_size(axis) - 1, 2):
+        pairs += [(i, i + 1), (i + 1, i)]
+    if not pairs:
+        return jnp.zeros_like(values)
+    return lax.ppermute(values, axis, pairs)
+
+
+def tracer_swap(values):
+    return lax.ppermute(values, "tracer", [(0, 1), (1, 0)])
+
+
+def neighbours(x_ev, x_od, y_ev, y_od):
+    x_od = pair_swap(x_od, "gx", 1)
+    y_ev = pair_swap(y_ev, "gy", 0)
+    y_od = pair_swap(y_od, "gy", 1)
+    x_ev = pair_swap(x_ev, "gx", 0)
+    return x_ev, x_od, y_ev, y_od
+
+
+def on_device(tracers, fluxes, diff_east, diff_north, column_depth, grazers, groups, preference):
+    tr_dev, levels, rows, cols = tracers.shape
+    parts = lax.axis_size("tracer")
+    if not (cols == 128 and rows * levels == cols and levels == 2 * SUB and rows % SUB == 0):
+        return plain(
+            tracers, fluxes, diff_east, diff_north, column_depth, grazers, groups, preference
+        )
+    g = Geo(tr_dev, levels, rows, cols)
+    total = float(tr_dev * parts)
+    pair = parts == 2
+    flat = tracers.reshape(-1, cols)
+    grazers = grazers.reshape(-1, cols)
+
+    if pair:
+        halves = [fluxes.reshape(-1, cols)]
+    else:
+        gathered = lax.all_gather(fluxes, "tracer", axis=1, tiled=True)
+        halves = [gathered[:, i : i + SUB].reshape(-1, cols) for i in (0, SUB)]
+    edges = [call(functools.partial(edges_kernel, g), [2 * SUB], [half])[0] for half in halves]
+    if pair:
+        edges.append(tracer_swap(edges[0]))
+    field, strips, prey = call(
+        functools.partial(load_kernel, g),
+        [g.T * g.tile, g.T * SUB, g.tile],
+        [flat, groups, preference],
+        scalars=(1, 2),
+    )
+    if pair:
+        bulk = jnp.concatenate([halves[0], prey])
+        others = [tracer_swap(bulk)]
+    else:
+        bulk = jnp.concatenate([halves[0], lax.psum(prey, "tracer")])
+        others = [jnp.concatenate([halves[1], jnp.zeros_like(prey)])]
+
+    x_rows = g.T * 2 * g.L + g.L + 2 * SUB
+    messages = call(
+        functools.partial(first_messages_kernel, g),
+        [x_rows, x_rows, g.slots * 2, g.slots * 2],
+        [field, strips, *edges, column_depth, diff_east, diff_north],
+    )
+    messages = neighbours(*messages)
+    x_rows = g.T * 2 * g.L
+    *results, coefs = call(
+        functools.partial(step_one_kernel, g, total, len(others)),
+        [g.T * g.tile, x_rows, x_rows, g.slots2 * 2, g.slots2 * 2, g.T * SUB, g.tile, g.coefs],
+        [field, strips, *messages, *edges, bulk, column_depth, diff_east, diff_north, grazers,
+         groups, preference, *others],
+        scalars=(13, 14),
+        scratch=[g.tile, g.T * SUB],
+    )
+    field, *messages, strips, prey = results
+    if pair:
+        others = [tracer_swap(prey)]
+    else:
+        prey, others = lax.psum(prey, "tracer"), []
+    messages = neighbours(*messages)
+    (out,) = call(
+        functools.partial(step_two_kernel, g, total, len(others)),
+        [g.T * g.tile],
+        [field, strips, *messages, prey, coefs, grazers, groups, preference, *others],
+        scalars=(9, 10),
+        scratch=[g.tile, g.T * SUB],
+    )
+    return out.reshape(tracers.shape)
+
+
 def solution(mesh):
     placed = (
         P("tracer", None, "gx", "gy"),

time: 147 us -> 40.9 us (0.28)
  the two profiles are of different devices: /device:TPU:0 before, /device:TPU:9 now
where the time goes in v1:
time: 40.9 us; the launch traced here: 40.5 us
  starting transfers between devices  19.1 us (47%)
  Pallas kernels  17 us (42%)
  waiting for transfers between devices  2.19 us (5%)
  local copies, waits for them, and re-layouts  2.06 us (5%)
    pallas_call x5, Pallas kernels, call(): pl.pallas_call(body, out_shape=[jax.ShapeDtypeStruct((rows, 128), jnp.flo...  17 us
    ppermute x8, starting transfers between devices, pair_swap(): return lax.ppermute(values, axis, pairs)  16.2 us
    ppermute x3, starting transfers between devices, tracer_swap(): return lax.ppermute(values, 'tracer', [(0, 1), (1, 0)])  2.9 us
    ppermute x8, waiting for transfers between devices, pair_swap(): return lax.ppermute(values, axis, pairs)  2.18 us
    unnamed x18, local copies, waits for them, and re-layouts  2.06 us
  transfers between devices with their start and end apart: 11, of which 2 were waited for; matrix products, arithmetic and copies ran while one was open for 0% of the time, Pallas kernels for 4%

profile of v1, /device:TPU:9, one launch (start us, length us, event | category | flops | bytes accessed | tf_op | source)
XLA Modules:
  0.0 40.5 jit_solution(7811096321230418776)
XLA Ops:
  0.0 0.0 copy-start.1
  0.0 0.9 %copy-done.1 = f32[3,8,8,128]{3,2,1,0:T(8,128)S(1)} copy-done((f32[3,8,8,128]{3,2,1,0:T(8,128)S(1)}, f32[3,8,8,128]{3,2,1,0:T(8,128)}, u32[]{:S(2)}) %copy-start.1) | copy-done | bytes 98328
  0.9 0.1 shard_map.83.mine_ref
  1.0 0.0 copy-start.7
  1.0 0.0 copy-start.8
  1.0 1.3 %collective-permute-start = (f32[16,128]{1,0:T(8,128)S(1)}, f32[16,128]{1,0:T(8,128)S(1)}, u32[]{:S(2)}, u32[]{:S(2)}) collective-permute-start(f32[16,128]{1,0:T(8,128)S(1)} %shard_map.83.mine_ref), channel_id=1, source_target_pairs={{0,16},{16,0},{1,17},{17,1},{2,18},{18,2},{3,19},{19,3},{4,20},{20... | collective-permute-start | bytes 24584 | tf_op jit(solution)/shard_map/ppermute | solution.py:608
  2.3 0.0 copy-done.7
  2.3 0.0 copy-done.8
  2.3 0.0 copy-start
  2.3 1.1 %copy-done = f32[12,16,8,128]{3,2,1,0:T(8,128)S(1)} copy-done((f32[12,16,8,128]{3,2,1,0:T(8,128)S(1)}, f32[12,16,8,128]{3,2,1,0:T(8,128)}, u32[]{:S(2)}) %copy-start) | copy-done | bytes 786456
  3.5 0.0 copy-start.4
  3.5 0.0 copy-start.5
  3.5 0.0 copy-start.6
  3.5 1.6 %shard_map.82 = (f32[1536,128]{1,0:T(8,128)S(1)}, f32[96,128]{1,0:T(8,128)S(1)}, f32[128,128]{1,0:T(8,128)S(1)}) custom-call(f32[1536,128]{1,0:T(8,128)S(1)} %bitcast.4, s32[12]{0:T(128)S(1)} %copy-done.7, f32[16]{0:T(128)S(1)} %copy-done.8), custom_call_target="tpu_custom_call" | custom-call | tf_op jit(solution)/shard_map/pallas_call | solution.py:588
  5.1 0.0 collective-permute-done.other_ref
  5.1 0.0 copy-done.4
  5.1 0.0 copy-done.5
  5.1 0.0 copy-done.6
  5.1 0.0 copy-start.2
  5.1 0.3 shard_map.84
  5.4 1.0 %collective-permute-start.1 = (f32[416,128]{1,0:T(8,128)S(1)}, f32[416,128]{1,0:T(8,128)S(1)}, u32[]{:S(2)}, u32[]{:S(2)}) collective-permute-start(f32[416,128]{1,0:T(8,128)S(1)} %get-tuple-element.22), channel_id=1, source_target_pairs={{0,4},{4,0},{8,12},{12,8},{1,5},{5,1},{9,13},{13,9},{2,6},{6,2},{1... | collective-permute-start | bytes 638984 | tf_op jit(solution)/shard_map/ppermute | solution.py:604
  6.4 3.0 %collective-permute-start.2 = (f32[416,128]{1,0:T(8,128)S(1)}, f32[416,128]{1,0:T(8,128)S(1)}, u32[]{:S(2)}, u32[]{:S(2)}) collective-permute-start(f32[416,128]{1,0:T(8,128)S(1)} %get-tuple-element.23), channel_id=1, source_target_pairs={{4,8},{8,4},{5,9},{9,5},{6,10},{10,6},{7,11},{11,7},{20,24},{24,20... | collective-permute-start | bytes 638984 | tf_op jit(solution)/shard_map/ppermute | solution.py:604
  9.4 0.0 copy-done.2
  9.4 0.0 copy-start.3
  9.5 0.6 %collective-permute-start.5 = (f32[320,128]{1,0:T(8,128)S(1)}, f32[320,128]{1,0:T(8,128)S(1)}, u32[]{:S(2)}, u32[]{:S(2)}) collective-permute-start(f32[320,128]{1,0:T(8,128)S(1)} %pad_maximum_fusion.bulk_ref), channel_id=1, source_target_pairs={{0,16},{16,0},{1,17},{17,1},{2,18},{18,2},{3,19},{19,3},{4,20},{20... | collective-permute-start | bytes 491528 | tf_op jit(solution)/shard_map/ppermute | solution.py:608
  10.1 0.2 collective-permute-start.3
  10.3 4.3 %collective-permute-start.4 = (f32[32,128]{1,0:T(8,128)S(1)}, f32[32,128]{1,0:T(8,128)S(1)}, u32[]{:S(2)}, u32[]{:S(2)}) collective-permute-start(f32[32,128]{1,0:T(8,128)S(1)} %get-tuple-element.25), channel_id=1, source_target_pairs={{1,2},{2,1},{5,6},{6,5},{9,10},{10,9},{13,14},{14,13},{17,18},{18,... | collective-permute-start | bytes 49160 | tf_op jit(solution)/shard_map/ppermute | solution.py:604
  14.6 0.0 collective-permute-done.3.yev_ref
  14.6 1.1 %collective-permute-done.4.yod_ref = f32[32,128]{1,0:T(8,128)S(1)} collective-permute-done((f32[32,128]{1,0:T(8,128)S(1)}, f32[32,128]{1,0:T(8,128)S(1)}, u32[]{:S(2)}, u32[]{:S(2)}) %collective-permute-start.4) | collective-permute-done | bytes 16416 | tf_op jit(solution)/shard_map/ppermute | solution.py:604
  15.7 0.0 collective-permute-done.5.rest_0_
  15.7 0.0 collective-permute-done.1.xev_ref
  15.7 0.0 collective-permute-done.2.xod_ref
  15.7 0.0 copy-done.3
  15.7 7.5 %shard_map.85 = (f32[1536,128]{1,0:T(8,128)S(1)}, f32[384,128]{1,0:T(8,128)S(1)}, f32[384,128]{1,0:T(8,128)S(1)}, f32[24,128]{1,0:T(8,128)S(1)}, f32[24,128]{1,0...) custom-call(f32[1536,128]{1,0:T(8,128)S(1)} %get-tuple-element.20.field_ref, ...), custom_call_target="tpu_custom_call" | custom-call | tf_op jit(solution)/shard_map/pallas_call | solution.py:588
  23.3 0.1 collective-permute-start.6
  23.3 4.0 %collective-permute-start.7 = (f32[384,128]{1,0:T(8,128)S(1)}, f32[384,128]{1,0:T(8,128)S(1)}, u32[]{:S(2)}, u32[]{:S(2)}) collective-permute-start(f32[384,128]{1,0:T(8,128)S(1)} %get-tuple-element.30), channel_id=1, source_target_pairs={{4,8},{8,4},{5,9},{9,5},{6,10},{10,6},{7,11},{11,7},{20,24},{24,20... | collective-permute-start | bytes 589832 | tf_op jit(solution)/shard_map/ppermute | solution.py:604
  27.3 1.0 %collective-permute-start.10 = (f32[128,128]{1,0:T(8,128)S(1)}, f32[128,128]{1,0:T(8,128)S(1)}, u32[]{:S(2)}, u32[]{:S(2)}) collective-permute-start(f32[128,128]{1,0:T(8,128)S(1)} %get-tuple-element.33.prey_ref), channel_id=1, source_target_pairs={{0,16},{16,0},{1,17},{17,1},{2,18},{18,2},{3,19},{19,3},{4,20},{20... | collective-permute-start | bytes 196616 | tf_op jit(solution)/shard_map/ppermute | solution.py:608
  28.3 0.0 collective-permute-start.8
  28.3 3.6 %collective-permute-start.9 = (f32[24,128]{1,0:T(8,128)S(1)}, f32[24,128]{1,0:T(8,128)S(1)}, u32[]{:S(2)}, u32[]{:S(2)}) collective-permute-start(f32[24,128]{1,0:T(8,128)S(1)} %get-tuple-element.32), channel_id=1, source_target_pairs={{1,2},{2,1},{5,6},{6,5},{9,10},{10,9},{13,14},{14,13},{17,18},{18,... | collective-permute-start | bytes 36872 | tf_op jit(solution)/shard_map/ppermute | solution.py:604
  31.9 0.0 collective-permute-done.8.yev_ref
  31.9 1.1 %collective-permute-done.9.yod_ref = f32[24,128]{1,0:T(8,128)S(1)} collective-permute-done((f32[24,128]{1,0:T(8,128)S(1)}, f32[24,128]{1,0:T(8,128)S(1)}, u32[]{:S(2)}, u32[]{:S(2)}) %collective-permute-start.9) | collective-permute-done | bytes 12320 | tf_op jit(solution)/shard_map/ppermute | solution.py:604
  33.0 0.0 collective-permute-done.10.rest_0_
  33.0 0.0 collective-permute-done.6.xev_ref
  33.0 0.0 collective-permute-done.7.xod_ref
  33.0 7.5 %shard_map.86 = f32[1536,128]{1,0:T(8,128)} custom-call(f32[1536,128]{1,0:T(8,128)S(1)} %get-tuple-element.27.field_ref, f32[96,128]{1,0:T(8,128)S(1)} %get-tuple-element.28.strips_ref, f32[384,128]{1,0:T(8,128)S(1)} %collective-permute-done.6.xev_ref, f32[384,128]{1,0:T(8,128)S(1)} %collective-permute-done.7.xod_ref, ...), custom_call_target="tpu_custom_call" | custom-call | tf_op jit(solution)/shard_map/pallas_call | solution.py:588
  (1 shorter events, 0.0 us)
Async XLA Ops:
  0.0 0.9 %copy-start.1 = (f32[3,8,8,128]{3,2,1,0:T(8,128)S(1)}, f32[3,8,8,128]{3,2,1,0:T(8,128)}, u32[]{:S(2)}) copy-start(f32[3,8,8,128]{3,2,1,0:T(8,128)} %param.9) | copy-start | bytes 294916
  1.0 1.3 %copy-start.7 = (s32[12]{0:T(128)S(1)}, s32[12]{0:T(128)}, u32[]{:S(2)}) copy-start(s32[12]{0:T(128)} %groups_ref.5) | copy-start | bytes 148
  1.0 1.3 %copy-start.8 = (f32[16]{0:T(128)S(1)}, f32[16]{0:T(128)}, u32[]{:S(2)}) copy-start(f32[16]{0:T(128)} %pref_ref.5) | copy-start | bytes 196
  1.0 4.1 %collective-permute-start = (f32[16,128]{1,0:T(8,128)S(1)}, f32[16,128]{1,0:T(8,128)S(1)}, u32[]{:S(2)}, u32[]{:S(2)}) collective-permute-start(f32[16,128]{1,0:T(8,128)S(1)} %shard_map.83.mine_ref), channel_id=1, source_target_pairs={{0,16},{16,0},{1,17},{17,1},{2,18},{18,2},{3,19},{19,3},{4,20},{20... | collective-permute-start | bytes 24584 | tf_op jit(solution)/shard_map/ppermute | solution.py:608
  2.3 1.1 %copy-start = (f32[12,16,8,128]{3,2,1,0:T(8,128)S(1)}, f32[12,16,8,128]{3,2,1,0:T(8,128)}, u32[]{:S(2)}) copy-start(f32[12,16,8,128]{3,2,1,0:T(8,128)} %param.8) | copy-start | bytes 2359300
  3.5 1.6 %copy-start.4 = (s32[8,128]{1,0:T(8,128)S(1)}, s32[8,128]{1,0:T(8,128)}, u32[]{:S(2)}) copy-start(s32[8,128]{1,0:T(8,128)} %depth_ref.3) | copy-start | bytes 12292
  3.5 1.6 %copy-start.5 = (f32[8,128]{1,0:T(8,128)S(1)}, f32[8,128]{1,0:T(8,128)}, u32[]{:S(2)}) copy-start(f32[8,128]{1,0:T(8,128)} %east_ref.3) | copy-start | bytes 12292
  3.5 1.7 %copy-start.6 = (f32[8,128]{1,0:T(8,128)S(1)}, f32[8,128]{1,0:T(8,128)}, u32[]{:S(2)}) copy-start(f32[8,128]{1,0:T(8,128)} %north_ref.3) | copy-start | bytes 12292
  5.1 4.3 %copy-start.2 = (f32[3,8,8,128]{3,2,1,0:T(8,128)S(1)}, f32[3,8,8,128]{3,2,1,0:T(8,128)}, u32[]{:S(2)}) copy-start(f32[3,8,8,128]{3,2,1,0:T(8,128)} %param.9) | copy-start | bytes 294916
  5.4 10.3 %collective-permute-start.1 = (f32[416,128]{1,0:T(8,128)S(1)}, f32[416,128]{1,0:T(8,128)S(1)}, u32[]{:S(2)}, u32[]{:S(2)}) collective-permute-start(f32[416,128]{1,0:T(8,128)S(1)} %get-tuple-element.22), channel_id=1, source_target_pairs={{0,4},{4,0},{8,12},{12,8},{1,5},{5,1},{9,13},{13,9},{2,6},{6,2},{1... | collective-permute-start | bytes 638984 | tf_op jit(solution)/shard_map/ppermute | solution.py:604
  6.4 9.3 %collective-permute-start.2 = (f32[416,128]{1,0:T(8,128)S(1)}, f32[416,128]{1,0:T(8,128)S(1)}, u32[]{:S(2)}, u32[]{:S(2)}) collective-permute-start(f32[416,128]{1,0:T(8,128)S(1)} %get-tuple-element.23), channel_id=1, source_target_pairs={{4,8},{8,4},{5,9},{9,5},{6,10},{10,6},{7,11},{11,7},{20,24},{24,20... | collective-permute-start | bytes 638984 | tf_op jit(solution)/shard_map/ppermute | solution.py:604
  9.4 6.3 %copy-start.3 = (f32[16,8,128]{2,1,0:T(8,128)S(1)}, f32[16,8,128]{2,1,0:T(8,128)}, u32[]{:S(2)}) copy-start(f32[16,8,128]{2,1,0:T(8,128)} %param.13) | copy-start | bytes 196612
  9.5 6.3 %collective-permute-start.5 = (f32[320,128]{1,0:T(8,128)S(1)}, f32[320,128]{1,0:T(8,128)S(1)}, u32[]{:S(2)}, u32[]{:S(2)}) collective-permute-start(f32[320,128]{1,0:T(8,128)S(1)} %pad_maximum_fusion.bulk_ref), channel_id=1, source_target_pairs={{0,16},{16,0},{1,17},{17,1},{2,18},{18,2},{3,19},{19,3},{4,20},{20... | collective-permute-start | bytes 491528 | tf_op jit(solution)/shard_map/ppermute | solution.py:608
  10.1 4.5 %collective-permute-start.3 = (f32[32,128]{1,0:T(8,128)S(1)}, f32[32,128]{1,0:T(8,128)S(1)}, u32[]{:S(2)}, u32[]{:S(2)}) collective-permute-start(f32[32,128]{1,0:T(8,128)S(1)} %get-tuple-element.24), channel_id=1, source_target_pairs={{0,1},{1,0},{2,3},{3,2},{4,5},{5,4},{6,7},{7,6},{8,9},{9,8},{10,11... | collective-permute-start | bytes 49160 | tf_op jit(solution)/shard_map/ppermute | solution.py:604
  10.3 5.4 %collective-permute-start.4 = (f32[32,128]{1,0:T(8,128)S(1)}, f32[32,128]{1,0:T(8,128)S(1)}, u32[]{:S(2)}, u32[]{:S(2)}) collective-permute-start(f32[32,128]{1,0:T(8,128)S(1)} %get-tuple-element.25), channel_id=1, source_target_pairs={{1,2},{2,1},{5,6},{6,5},{9,10},{10,9},{13,14},{14,13},{17,18},{18,... | collective-permute-start | bytes 49160 | tf_op jit(solution)/shard_map/ppermute | solution.py:604
  23.3 9.7 %collective-permute-start.6 = (f32[384,128]{1,0:T(8,128)S(1)}, f32[384,128]{1,0:T(8,128)S(1)}, u32[]{:S(2)}, u32[]{:S(2)}) collective-permute-start(f32[384,128]{1,0:T(8,128)S(1)} %get-tuple-element.29), channel_id=1, source_target_pairs={{0,4},{4,0},{8,12},{12,8},{1,5},{5,1},{9,13},{13,9},{2,6},{6,2},{1... | collective-permute-start | bytes 589832 | tf_op jit(solution)/shard_map/ppermute | solution.py:604
  23.3 9.6 %collective-permute-start.7 = (f32[384,128]{1,0:T(8,128)S(1)}, f32[384,128]{1,0:T(8,128)S(1)}, u32[]{:S(2)}, u32[]{:S(2)}) collective-permute-start(f32[384,128]{1,0:T(8,128)S(1)} %get-tuple-element.30), channel_id=1, source_target_pairs={{4,8},{8,4},{5,9},{9,5},{6,10},{10,6},{7,11},{11,7},{20,24},{24,20... | collective-permute-start | bytes 589832 | tf_op jit(solution)/shard_map/ppermute | solution.py:604
  27.3 5.7 %collective-permute-start.10 = (f32[128,128]{1,0:T(8,128)S(1)}, f32[128,128]{1,0:T(8,128)S(1)}, u32[]{:S(2)}, u32[]{:S(2)}) collective-permute-start(f32[128,128]{1,0:T(8,128)S(1)} %get-tuple-element.33.prey_ref), channel_id=1, source_target_pairs={{0,16},{16,0},{1,17},{17,1},{2,18},{18,2},{3,19},{19,3},{4,20},{20... | collective-permute-start | bytes 196616 | tf_op jit(solution)/shard_map/ppermute | solution.py:608
  28.3 3.6 %collective-permute-start.8 = (f32[24,128]{1,0:T(8,128)S(1)}, f32[24,128]{1,0:T(8,128)S(1)}, u32[]{:S(2)}, u32[]{:S(2)}) collective-permute-start(f32[24,128]{1,0:T(8,128)S(1)} %get-tuple-element.31), channel_id=1, source_target_pairs={{0,1},{1,0},{2,3},{3,2},{4,5},{5,4},{6,7},{7,6},{8,9},{9,8},{10,11... | collective-permute-start | bytes 36872 | tf_op jit(solution)/shard_map/ppermute | solution.py:604
  28.3 4.7 %collective-permute-start.9 = (f32[24,128]{1,0:T(8,128)S(1)}, f32[24,128]{1,0:T(8,128)S(1)}, u32[]{:S(2)}, u32[]{:S(2)}) collective-permute-start(f32[24,128]{1,0:T(8,128)S(1)} %get-tuple-element.32), channel_id=1, source_target_pairs={{1,2},{2,1},{5,6},{6,5},{9,10},{10,9},{13,14},{14,13},{17,18},{18,... | collective-permute-start | bytes 36872 | tf_op jit(solution)/shard_map/ppermute | solution.py:604

commit v2 on v1

--- a/solution.py
+++ b/solution.py
@@ -10,6 +10,7 @@
 STEPS = 2
 SUB = 8
 LIM = 48 * 1024 * 1024
+AHEAD = 2
 
 
 def with_halo(cells, sides, width):
@@ -182,75 +183,87 @@
     return lax.rem(lax.axis_index(axis), 2) == 0
 
 
-def edges_kernel(g, fluxes_ref, out_ref):
-    base = g.R * SUB
-    out_ref[0:SUB, :] = fluxes_ref[pl.ds(g.R - 1, SUB, stride=g.R), :]
-    parts = []
-    for r in range(g.R):
-        row = fluxes_ref[pl.ds(base + r, SUB, stride=g.R), :]
-        parts += [row] * g.LH
-    out_ref[SUB : 2 * SUB, :] = pack_strips(parts)
-
-
-def load_kernel(g, tracers_ref, groups_ref, pref_ref, field_ref, strips_ref, prey_ref):
-    def one(t, carry):
+def load_kernel(
+    g, tracers_ref, groups_ref, pref_ref, field_ref, strips_ref, prey_ref, landed, sems
+):
+    def arrival(t):
+        at = pl.ds(pl.multiple_of(t * g.tile, g.tile), g.tile)
+        return pltpu.make_async_copy(tracers_ref.at[at, :], landed.at[at, :], sems.at[t])
+
+    for t in range(g.T):
+        arrival(t).start()
+    prey_ref[...] = jnp.zeros_like(prey_ref)
+
+    def one(t):
+        arrival(t).wait()
         taste = taste_of(groups_ref, pref_ref, t)
         base = pl.multiple_of(t * g.tile, g.tile)
         parts = []
         for r in range(g.R):
             for lh in range(g.LH):
                 at = (r * g.LH + lh) * SUB
-                v = tracers_ref[pl.ds(base + lh * SUB * g.R + r, SUB, stride=g.R), :]
+                v = landed[pl.ds(base + lh * SUB * g.R + r, SUB, stride=g.R), :]
                 field_ref[pl.ds(base + at, SUB), :] = v
                 parts.append(v)
                 prey_ref[at : at + SUB, :] += taste * v
         strips_ref[pl.ds(pl.multiple_of(t * SUB, SUB), SUB), :] = pack_strips(parts)
-        return carry
-
-    prey_ref[...] = jnp.zeros_like(prey_ref)
-    lax.fori_loop(0, g.T, one, 0)
+
+    each_tracer(g, one)
+
+
+def flux_reader(g, mine_ref, other_ref):
+    first = lax.axis_index("tracer") == 0
+    single = lax.axis_size("tracer") != 2
+
+    def flux(dim, r, lh):
+        at = pl.ds(dim * g.R * SUB + r, SUB, stride=g.R)
+        a, b = mine_ref[at, :], other_ref[at, :]
+        if single:
+            return (a, b)[lh]
+        return jnp.where(first, (a, b)[lh], (b, a)[lh])
+
+    return flux
 
 
 def first_messages_kernel(
     g, field_ref, strips_ref, mine_ref, other_ref, depth_ref, east_ref, north_ref,
-    xev_ref, xod_ref, yev_ref, yod_ref,
+    xev_ref, xod_ref, yev_ref, yod_ref, extra_ref,
 ):
     x_even, y_even = is_even("gx"), is_even("gy")
-    first = lax.axis_index("tracer") == 0
-    single = lax.axis_size("tracer") != 2
+    flux = flux_reader(g, mine_ref, other_ref)
     zero = jnp.zeros((SUB, 128), jnp.float32)
 
     def put(ref_ev, ref_od, at, even, low, high):
         ref_ev[at, :] = jnp.where(even, high, low)
         ref_od[at, :] = jnp.where(even, low, high)
 
-    def one(t, carry):
+    def one(t):
         base = pl.multiple_of(t * g.tile, g.tile)
         for i in range(2 * g.LH):
             low = field_ref[pl.ds(base + i * SUB, SUB), :]
             high = field_ref[pl.ds(base + g.tile - 2 * g.L + i * SUB, SUB), :]
             at = pl.ds(pl.multiple_of(t * 2 * g.L, SUB) + i * SUB, SUB)
             put(xev_ref, xod_ref, at, x_even, low, high)
-        return carry
-
-    lax.fori_loop(0, g.T, one, 0)
-    mine, other = mine_ref[...], other_ref[...]
-    lower = mine if single else jnp.where(first, mine, other)
-    upper = other if single else jnp.where(first, other, mine)
+
+    each_tracer(g, one)
     at = g.T * 2 * g.L
-    for lh, half in enumerate((lower, upper)):
-        put(xev_ref, xod_ref, slice(at, at + SUB), x_even, zero, half[0:SUB])
+    for lh in range(g.LH):
+        put(xev_ref, xod_ref, slice(at, at + SUB), x_even, zero, flux(0, g.R - 1, lh))
         at += SUB
     depth = depth_ref[...].astype(jnp.float32)
     put(xev_ref, xod_ref, slice(at, at + SUB), x_even, depth, roll(depth, 2, 0))
     at += SUB
     put(xev_ref, xod_ref, slice(at, at + SUB), x_even, zero, roll(east_ref[...], 1, 0))
 
-    half_of = (lanes() // 8) % g.LH
     packed = [strips_ref[t * SUB : (t + 1) * SUB, :] for t in range(g.T)]
-    packed.append(pack_strips(spread_rows(g, depth)))
-    packed.append(jnp.where(half_of == 0, lower[SUB : 2 * SUB], upper[SUB : 2 * SUB]))
-    packed.append(pack_strips(spread_rows(g, north_ref[...])))
+    extras = [
+        pack_strips(spread_rows(g, depth)),
+        pack_strips([flux(1, r, lh) for r in range(g.R) for lh in range(g.LH)]),
+        pack_strips(spread_rows(g, north_ref[...])),
+    ]
+    for i, one_extra in enumerate(extras):
+        extra_ref[i * SUB : (i + 1) * SUB, :] = one_extra
+    packed += extras
     for v in range(0, len(packed), 4):
         low = message_strips(packed[v : v + 4], True)
         high = message_strips(packed[v : v + 4], False)
@@ -264,12 +277,8 @@
     return parts
 
 
-def coefficients(
-    g, cf, xl, yl, yu, mine_ref, other_ref, fluxes_mine, fluxes_other, depth_ref, east_ref, north_ref
-):
+def coefficients(g, cf, xl, yl, yu, flux, extra_ref, depth_ref, east_ref, north_ref):
     lane, sub = lanes(), sublanes()
-    first = lax.axis_index("tracer") == 0
-    single = lax.axis_size("tracer") != 2
     depth = depth_ref[...].astype(jnp.float32)
     depth_low, depth_high = xl(g.LH)
     east = east_ref[...]
@@ -284,13 +293,6 @@
     depths += [spread(depth, r) for r in range(g.R)]
     depths += [spread(depth_high, 0), spread(depth_high, 1)]
     wet = [[level[lh] < d for lh in range(g.LH)] for d in depths]
-
-    def flux(dim, r, lh):
-        at = pl.ds(dim * g.R * SUB + r, SUB, stride=g.R)
-        a, b = fluxes_mine[at, :], fluxes_other[at, :]
-        if single:
-            return (a, b)[lh]
-        return jnp.where(first, (a, b)[lh], (b, a)[lh])
 
     def store(name, index, value):
         at = g.off[name] + index * SUB
@@ -332,14 +334,7 @@
 
     place = lane % 8
     half_of = (lane // 8) % g.LH
-    mine, other = mine_ref[SUB : 2 * SUB, :], other_ref[SUB : 2 * SUB, :]
-    lower = mine if single else jnp.where(first, mine, other)
-    upper = other if single else jnp.where(first, other, mine)
-    own = (
-        pack_strips(spread_rows(g, depth)),
-        jnp.where(half_of == 0, lower, upper),
-        pack_strips(spread_rows(g, north)),
-    )
+    own = [extra_ref[i * SUB : (i + 1) * SUB, :] for i in range(3)]
     full = []
     for i, one in enumerate(own):
         slot = g.T + i
@@ -449,13 +444,13 @@
     return jnp.where(even, od, ev), jnp.where(even, ev, od)
 
 
-def set_factor(g, total, factor, grazers_ref, mine_ref, others, scale_rows=0):
+def set_factor(g, total, factor, grazers_ref, mine_ref, others):
     for r in range(g.R):
         for lh in range(g.LH):
             at = (r * g.LH + lh) * SUB
             prey = mine_ref[at : at + SUB, :]
             for ref in others:
-                prey = prey + ref[scale_rows + at : scale_rows + at + SUB, :]
+                prey = prey + ref[at : at + SUB, :]
             grazers = grazers_ref[pl.ds(lh * SUB * g.R + r, SUB, stride=g.R), :]
             factor[at : at + SUB, :] = grazers / (1.0 + 4.0 * prey / total)
 
@@ -484,24 +479,34 @@
     return split_sides(y_even, yev_ref[at, :], yod_ref[at, :])
 
 
-def unpack_strips(g, strips_ref, yev_ref, yod_ref, y_even, full_ref):
+def all_strip_fixes(g, cf, strips_ref, yev_ref, yod_ref, y_even, slope_ref, carried_ref):
     for t in range(g.T):
         low, high = y_sides(y_even, yev_ref, yod_ref, t // 4)
-        full_ref[t * SUB : (t + 1) * SUB, :] = full_strips(
-            strips_ref[t * SUB : (t + 1) * SUB, :], low, high, t % 4
-        )
+        at = slice(t * SUB, (t + 1) * SUB)
+        full = full_strips(strips_ref[at, :], low, high, t % 4)
+        slope_ref[at, :], carried_ref[at, :] = strip_fixes(g, cf, full)
+
+
+def each_tracer(g, body):
+    def some(i, carry):
+        for ahead in range(AHEAD):
+            body(i * AHEAD + ahead)
+        return carry
+
+    lax.fori_loop(0, g.T // AHEAD, some, 0)
+    for t in range(g.T - g.T % AHEAD, g.T):
+        body(t)
 
 
 def step_one_kernel(
     g, total, n_other,
-    field_ref, strips_ref, xev_ref, xod_ref, yev_ref, yod_ref, mine_ref, other_ref,
-    bulk_ref, depth_ref, east_ref, north_ref, grazers_ref, groups_ref, pref_ref, *rest,
+    field_ref, strips_ref, xev_ref, xod_ref, yev_ref, yod_ref, extra_ref, mine_ref, other_ref,
+    depth_ref, east_ref, north_ref, grazers_ref, groups_ref, pref_ref, prey_ref, *rest,
 ):
     others, rest = rest[:n_other], rest[n_other:]
     (out_ref, xev2_ref, xod2_ref, yev2_ref, yod2_ref, strips2_ref, prey2_ref, cf,
-     factor, full_ref) = rest
+     factor, slope_ref, carried_ref) = rest
     x_even, y_even = is_even("gx"), is_even("gy")
-    prey_rows = 3 * g.R * SUB
 
     def xl(i):
         at = pl.ds(g.T * 2 * g.L + i * SUB, SUB)
@@ -511,15 +516,13 @@
         g, cf, xl,
         lambda v: y_sides(y_even, yev_ref, yod_ref, v)[0],
         lambda v: y_sides(y_even, yev_ref, yod_ref, v)[1],
-        mine_ref, other_ref, bulk_ref, others[0], depth_ref, east_ref, north_ref,
-    )
-    set_factor(
-        g, total, factor, grazers_ref, bulk_ref.at[prey_rows : prey_rows + g.tile], others[-1:], prey_rows
-    )
-    unpack_strips(g, strips_ref, yev_ref, yod_ref, y_even, full_ref)
+        flux_reader(g, mine_ref, other_ref), extra_ref, depth_ref, east_ref, north_ref,
+    )
+    set_factor(g, total, factor, grazers_ref, prey_ref, others)
+    all_strip_fixes(g, cf, strips_ref, yev_ref, yod_ref, y_even, slope_ref, carried_ref)
     prey2_ref[...] = jnp.zeros_like(prey2_ref)
 
-    def one(t, carry):
+    def one(t):
         taste = taste_of(groups_ref, pref_ref, t)
         base = pl.multiple_of(t * g.tile, g.tile)
         halo = pl.multiple_of(t * 2 * g.L, 2 * g.L)
@@ -533,7 +536,7 @@
             news[r, lh] = new
 
         advance(
-            g, cf, strip_fixes(g, cf, full_ref[strip_at, :]),
+            g, cf, (slope_ref[strip_at, :], carried_ref[strip_at, :]),
             rows_of(g, field_ref, xev_ref, xod_ref, x_even, t), taste, factor, emit,
         )
         for i in range(2):
@@ -545,9 +548,8 @@
         strips2_ref[strip_at, :] = pack_strips(
             [news[r, lh] for r in range(g.R) for lh in range(g.LH)]
         )
-        return carry
-
-    lax.fori_loop(0, g.T, one, 0)
+
+    each_tracer(g, one)
     packed = [strips2_ref[t * SUB : (t + 1) * SUB, :] for t in range(g.T)]
     for v in range(0, g.T, 4):
         low = message_strips(packed[v : v + 4], True)
@@ -558,39 +560,51 @@
 
 def step_two_kernel(
     g, total, n_other,
-    field_ref, strips_ref, xev_ref, xod_ref, yev_ref, yod_ref, prey_ref, cf,
-    grazers_ref, groups_ref, pref_ref, *rest,
+    field_ref, strips_ref, xev_ref, xod_ref, yev_ref, yod_ref, cf,
+    grazers_ref, groups_ref, pref_ref, prey_ref, *rest,
 ):
-    others, (out_ref, factor, full_ref) = rest[:n_other], rest[n_other:]
+    others, (out_ref, factor, slope_ref, carried_ref, leaving, sems) = rest[:n_other], rest[n_other:]
     x_even, y_even = is_even("gx"), is_even("gy")
     set_factor(g, total, factor, grazers_ref, prey_ref, others)
-    unpack_strips(g, strips_ref, yev_ref, yod_ref, y_even, full_ref)
-
-    def one(t, carry):
+    all_strip_fixes(g, cf, strips_ref, yev_ref, yod_ref, y_even, slope_ref, carried_ref)
+
+    def departure(t):
+        at = pl.ds(pl.multiple_of(t * g.tile, g.tile), g.tile)
+        return pltpu.make_async_copy(leaving.at[at, :], out_ref.at[at, :], sems.at[t])
+
+    def one(t):
         taste = taste_of(groups_ref, pref_ref, t)
         base = pl.multiple_of(t * g.tile, g.tile)
         strip_at = pl.ds(pl.multiple_of(t * SUB, SUB), SUB)
 
         def emit(r, lh, new):
-            out_ref[pl.ds(base + lh * SUB * g.R + r, SUB, stride=g.R), :] = new
+            leaving[pl.ds(base + lh * SUB * g.R + r, SUB, stride=g.R), :] = new
 
         advance(
-            g, cf, strip_fixes(g, cf, full_ref[strip_at, :]),
+            g, cf, (slope_ref[strip_at, :], carried_ref[strip_at, :]),
             rows_of(g, field_ref, xev_ref, xod_ref, x_even, t), taste, factor, emit,
         )
-        return carry
-
-    lax.fori_loop(0, g.T, one, 0)
-
-
-def call(body, outs, operands, scalars=(), scratch=()):
-    vmem, smem = pl.BlockSpec(memory_space=pltpu.VMEM), pl.BlockSpec(memory_space=pltpu.SMEM)
+        departure(t).start()
+
+    each_tracer(g, one)
+    for t in range(g.T):
+        departure(t).wait()
+
+
+def call(body, outs, operands, scalars=(), far=(), far_out=False, scratch=()):
+    spaces = [
+        pltpu.SMEM if i in scalars else pltpu.HBM if i in far else pltpu.VMEM
+        for i in range(len(operands))
+    ]
     return pl.pallas_call(
         body,
         out_shape=[jax.ShapeDtypeStruct((rows, 128), jnp.float32) for rows in outs],
-        in_specs=[smem if i in scalars else vmem for i in range(len(operands))],
-        out_specs=[vmem] * len(outs),
-        scratch_shapes=[pltpu.VMEM((rows, 128), jnp.float32) for rows in scratch],
+        in_specs=[pl.BlockSpec(memory_space=space) for space in spaces],
+        out_specs=[pl.BlockSpec(memory_space=pltpu.HBM if far_out else pltpu.VMEM)] * len(outs),
+        scratch_shapes=[
+            pltpu.VMEM((rows, 128), jnp.float32) if isinstance(rows, int) else rows
+            for rows in scratch
+        ],
         compiler_params=pltpu.CompilerParams(vmem_limit_bytes=LIM),
     )(*operands)
 
@@ -606,6 +620,12 @@
 
 def tracer_swap(values):
     return lax.ppermute(values, "tracer", [(0, 1), (1, 0)])
+
+
+def all_prey(values):
+    if lax.axis_size("tracer") == 2:
+        return [values, tracer_swap(values)]
+    return [lax.psum(values, "tracer")]
 
 
 def neighbours(x_ev, x_od, y_ev, y_od):
@@ -630,54 +650,47 @@
     grazers = grazers.reshape(-1, cols)
 
     if pair:
-        halves = [fluxes.reshape(-1, cols)]
+        mine = fluxes.reshape(-1, cols)
+        other = tracer_swap(mine)
     else:
         gathered = lax.all_gather(fluxes, "tracer", axis=1, tiled=True)
-        halves = [gathered[:, i : i + SUB].reshape(-1, cols) for i in (0, SUB)]
-    edges = [call(functools.partial(edges_kernel, g), [2 * SUB], [half])[0] for half in halves]
-    if pair:
-        edges.append(tracer_swap(edges[0]))
+        mine, other = (gathered[:, i : i + SUB].reshape(-1, cols) for i in (0, SUB))
+    copies = pltpu.SemaphoreType.DMA((g.T,))
     field, strips, prey = call(
         functools.partial(load_kernel, g),
         [g.T * g.tile, g.T * SUB, g.tile],
-        [flat, groups, preference],
+        [pltpu.with_memory_space_constraint(flat, pltpu.HBM), groups, preference],
         scalars=(1, 2),
-    )
-    if pair:
-        bulk = jnp.concatenate([halves[0], prey])
-        others = [tracer_swap(bulk)]
-    else:
-        bulk = jnp.concatenate([halves[0], lax.psum(prey, "tracer")])
-        others = [jnp.concatenate([halves[1], jnp.zeros_like(prey)])]
-
+        far=(0,),
+        scratch=[g.T * g.tile, copies],
+    )
+    prey = all_prey(prey)
     x_rows = g.T * 2 * g.L + g.L + 2 * SUB
-    messages = call(
+    *messages, extra = call(
         functools.partial(first_messages_kernel, g),
-        [x_rows, x_rows, g.slots * 2, g.slots * 2],
-        [field, strips, *edges, column_depth, diff_east, diff_north],
+        [x_rows, x_rows, g.slots * 2, g.slots * 2, 3 * SUB],
+        [field, strips, mine, other, column_depth, diff_east, diff_north],
     )
     messages = neighbours(*messages)
     x_rows = g.T * 2 * g.L
     *results, coefs = call(
-        functools.partial(step_one_kernel, g, total, len(others)),
+        functools.partial(step_one_kernel, g, total, len(prey) - 1),
         [g.T * g.tile, x_rows, x_rows, g.slots2 * 2, g.slots2 * 2, g.T * SUB, g.tile, g.coefs],
-        [field, strips, *messages, *edges, bulk, column_depth, diff_east, diff_north, grazers,
-         groups, preference, *others],
+        [field, strips, *messages, extra, mine, other, column_depth, diff_east, diff_north,
+         grazers, groups, preference, *prey],
         scalars=(13, 14),
-        scratch=[g.tile, g.T * SUB],
+        scratch=[g.tile, g.T * SUB, g.T * SUB],
     )
     field, *messages, strips, prey = results
-    if pair:
-        others = [tracer_swap(prey)]
-    else:
-        prey, others = lax.psum(prey, "tracer"), []
+    prey = all_prey(prey)
     messages = neighbours(*messages)
     (out,) = call(
-        functools.partial(step_two_kernel, g, total, len(others)),
+        functools.partial(step_two_kernel, g, total, len(prey) - 1),
         [g.T * g.tile],
-        [field, strips, *messages, prey, coefs, grazers, groups, preference, *others],
-        scalars=(9, 10),
-        scratch=[g.tile, g.T * SUB],
+        [field, strips, *messages, coefs, grazers, groups, preference, *prey],
+        scalars=(8, 9),
+        far_out=True,
+        scratch=[g.tile, g.T * SUB, g.T * SUB, g.T * g.tile, copies],
     )
     return out.reshape(tracers.shape)
 

time: 40.9 us -> 34.3 us (0.84)
  Pallas kernels: 17 us -> 11.9 us
  local copies, waits for them, and re-layouts: 2.06 us -> 0.03 us
  starting transfers between devices: 19.1 us -> 19.7 us
    pallas_call x5 -> x4, Pallas kernels: 17 us -> 11.9 us  [call(): pl.pallas_call(body, out_shape=[jax.ShapeDtypeStruct((rows, 128), jnp.flo...]
    unnamed x18 -> x14, local copies, waits for them, and re-layouts: 2.06 us -> 0.03 us
    ppermute x8, starting transfers between devices: 16.2 us -> 16.8 us  [pair_swap(): return lax.ppermute(values, axis, pairs)]
  transfers between devices with their start and end apart: 11 -> 11, of which waited for: 2 -> 2; matrix products, arithmetic and copies ran while one was open for 0% -> 0% of each run, Pallas kernels for 4% -> 8%
where the time goes in v2:
time: 34.3 us; the launch traced here: 33.9 us
  starting transfers between devices  19.7 us (57%)
  Pallas kernels  11.9 us (35%)
  waiting for transfers between devices  2.17 us (6%)
    ppermute x8, starting transfers between devices, pair_swap(): return lax.ppermute(values, axis, pairs)  16.8 us
    pallas_call x4, Pallas kernels, call(): pl.pallas_call(body, out_shape=[jax.ShapeDtypeStruct((rows, 128), jnp.flo...  11.9 us
    ppermute x3, starting transfers between devices, tracer_swap(): return lax.ppermute(values, 'tracer', [(0, 1), (1, 0)])  2.84 us
    ppermute x8, waiting for transfers between devices, pair_swap(): return lax.ppermute(values, axis, pairs)  2.17 us
  transfers between devices with their start and end apart: 11, of which 2 were waited for; matrix products, arithmetic and copies ran while one was open for 0% of the time, Pallas kernels for 8%

profile of v2, /device:TPU:9, one launch (start us, length us, event | category | flops | bytes accessed | tf_op | source)
XLA Modules:
  0.0 33.9 jit_solution(9907247144616025825)
XLA Ops:
  0.0 0.0 copy-start.5
  0.0 0.0 copy-start.6
  0.0 1.2 %collective-permute-start = (f32[192,128]{1,0:T(8,128)}, f32[192,128]{1,0:T(8,128)S(1)}, u32[]{:S(2)}, u32[]{:S(2)}) collective-permute-start(f32[192,128]{1,0:T(8,128)} %bitcast.4), channel_id=1, source_target_pairs={{0,16},{16,0},{1,17},{17,1},{2,18},{18,2},{3,19},{19,3},{4,20},{20... | collective-permute-start | bytes 294920 | tf_op jit(solution)/shard_map/ppermute | solution.py:622
  1.2 0.0 copy-done.5
  1.2 0.0 copy-done.6
  1.2 0.0 copy-start
  1.3 0.0 copy-start.2
  1.3 0.0 copy-start.3
  1.3 0.0 copy-start.4
  1.3 2.5 %shard_map.82 = (f32[1536,128]{1,0:T(8,128)S(1)}, f32[96,128]{1,0:T(8,128)S(1)}, f32[128,128]{1,0:T(8,128)S(1)}) custom-call(f32[1536,128]{1,0:T(8,128)} %bitcast.9, s32[12]{0:T(128)S(1)} %copy-done.5, f32[16]{0:T(128)S(1)} %copy-done.6), custom_call_target="tpu_custom_call" | custom-call | tf_op jit(solution)/shard_map/pallas_call | solution.py:599
  3.8 0.0 collective-permute-done.other_ref
  3.8 0.0 copy-done
  3.9 0.0 copy-done.2
  3.9 0.0 copy-done.3
  3.9 0.0 copy-done.4
  3.9 0.0 copy-start.1
  3.9 0.3 shard_map.83
  4.2 1.7 %collective-permute-start.1 = (f32[416,128]{1,0:T(8,128)S(1)}, f32[416,128]{1,0:T(8,128)S(1)}, u32[]{:S(2)}, u32[]{:S(2)}) collective-permute-start(f32[416,128]{1,0:T(8,128)S(1)} %get-tuple-element.23), channel_id=1, source_target_pairs={{0,4},{4,0},{8,12},{12,8},{1,5},{5,1},{9,13},{13,9},{2,6},{6,2},{1... | collective-permute-start | bytes 638984 | tf_op jit(solution)/shard_map/ppermute | solution.py:618
  5.8 3.0 %collective-permute-start.2 = (f32[416,128]{1,0:T(8,128)S(1)}, f32[416,128]{1,0:T(8,128)S(1)}, u32[]{:S(2)}, u32[]{:S(2)}) collective-permute-start(f32[416,128]{1,0:T(8,128)S(1)} %get-tuple-element.24), channel_id=1, source_target_pairs={{4,8},{8,4},{5,9},{9,5},{6,10},{10,6},{7,11},{11,7},{20,24},{24,20... | collective-permute-start | bytes 638984 | tf_op jit(solution)/shard_map/ppermute | solution.py:618
  8.9 1.3 %collective-permute-start.5 = (f32[128,128]{1,0:T(8,128)S(1)}, f32[128,128]{1,0:T(8,128)S(1)}, u32[]{:S(2)}, u32[]{:S(2)}) collective-permute-start(f32[128,128]{1,0:T(8,128)S(1)} %get-tuple-element.28.prey_ref), channel_id=1, source_target_pairs={{0,16},{16,0},{1,17},{17,1},{2,18},{18,2},{3,19},{19,3},{4,20},{20... | collective-permute-start | bytes 196616 | tf_op jit(solution)/shard_map/ppermute | solution.py:622
  10.2 0.2 collective-permute-start.3
  10.3 4.3 %collective-permute-start.4 = (f32[32,128]{1,0:T(8,128)S(1)}, f32[32,128]{1,0:T(8,128)S(1)}, u32[]{:S(2)}, u32[]{:S(2)}) collective-permute-start(f32[32,128]{1,0:T(8,128)S(1)} %get-tuple-element.26), channel_id=1, source_target_pairs={{1,2},{2,1},{5,6},{6,5},{9,10},{10,9},{13,14},{14,13},{17,18},{18,... | collective-permute-start | bytes 49160 | tf_op jit(solution)/shard_map/ppermute | solution.py:618
  14.7 0.0 collective-permute-done.5.rest_0_
  14.7 0.0 collective-permute-done.3.yev_ref
  14.7 1.1 %collective-permute-done.4.yod_ref = f32[32,128]{1,0:T(8,128)S(1)} collective-permute-done((f32[32,128]{1,0:T(8,128)S(1)}, f32[32,128]{1,0:T(8,128)S(1)}, u32[]{:S(2)}, u32[]{:S(2)}) %collective-permute-start.4) | collective-permute-done | bytes 16416 | tf_op jit(solution)/shard_map/ppermute | solution.py:618
  15.8 0.0 collective-permute-done.1.xev_ref
  15.8 0.0 collective-permute-done.2.xod_ref
  15.8 0.0 copy-done.1
  15.8 4.5 %shard_map.84 = (f32[1536,128]{1,0:T(8,128)S(1)}, f32[384,128]{1,0:T(8,128)S(1)}, f32[384,128]{1,0:T(8,128)S(1)}, f32[24,128]{1,0:T(8,128)S(1)}, f32[24,128]{1,0...) custom-call(f32[1536,128]{1,0:T(8,128)S(1)} %get-tuple-element.21.field_ref, ...), custom_call_target="tpu_custom_call" | custom-call | tf_op jit(solution)/shard_map/pallas_call | solution.py:599
  20.3 0.1 collective-permute-start.6
  20.4 4.0 %collective-permute-start.7 = (f32[384,128]{1,0:T(8,128)S(1)}, f32[384,128]{1,0:T(8,128)S(1)}, u32[]{:S(2)}, u32[]{:S(2)}) collective-permute-start(f32[384,128]{1,0:T(8,128)S(1)} %get-tuple-element.32), channel_id=1, source_target_pairs={{4,8},{8,4},{5,9},{9,5},{6,10},{10,6},{7,11},{11,7},{20,24},{24,20... | collective-permute-start | bytes 589832 | tf_op jit(solution)/shard_map/ppermute | solution.py:618
  24.3 0.3 collective-permute-start.10
  24.6 0.0 collective-permute-start.8
  24.6 3.6 %collective-permute-start.9 = (f32[24,128]{1,0:T(8,128)S(1)}, f32[24,128]{1,0:T(8,128)S(1)}, u32[]{:S(2)}, u32[]{:S(2)}) collective-permute-start(f32[24,128]{1,0:T(8,128)S(1)} %get-tuple-element.34), channel_id=1, source_target_pairs={{1,2},{2,1},{5,6},{6,5},{9,10},{10,9},{13,14},{14,13},{17,18},{18,... | collective-permute-start | bytes 36872 | tf_op jit(solution)/shard_map/ppermute | solution.py:618
  28.3 0.0 collective-permute-done.8.yev_ref
  28.3 1.1 %collective-permute-done.9.yod_ref = f32[24,128]{1,0:T(8,128)S(1)} collective-permute-done((f32[24,128]{1,0:T(8,128)S(1)}, f32[24,128]{1,0:T(8,128)S(1)}, u32[]{:S(2)}, u32[]{:S(2)}) %collective-permute-start.9) | collective-permute-done | bytes 12320 | tf_op jit(solution)/shard_map/ppermute | solution.py:618
  29.3 0.0 collective-permute-done.10.rest_0_
  29.3 0.0 collective-permute-done.6.xev_ref
  29.3 0.0 collective-permute-done.7.xod_ref
  29.3 4.6 %shard_map.85 = f32[1536,128]{1,0:T(8,128)} custom-call(f32[1536,128]{1,0:T(8,128)S(1)} %get-tuple-element.29.field_ref, f32[96,128]{1,0:T(8,128)S(1)} %get-tuple-element.30.strips_ref, f32[384,128]{1,0:T(8,128)S(1)} %collective-permute-done.6.xev_ref, f32[384,128]{1,0:T(8,128)S(1)} %collective-permute-done.7.xod_ref, ...), custom_call_target="tpu_custom_call" | custom-call | tf_op jit(solution)/shard_map/pallas_call | solution.py:599
Async XLA Ops:
  0.0 1.2 %copy-start.5 = (s32[12]{0:T(128)S(1)}, s32[12]{0:T(128)}, u32[]{:S(2)}) copy-start(s32[12]{0:T(128)} %groups_ref.5) | copy-start | bytes 148
  0.0 1.2 %copy-start.6 = (f32[16]{0:T(128)S(1)}, f32[16]{0:T(128)}, u32[]{:S(2)}) copy-start(f32[16]{0:T(128)} %pref_ref.5) | copy-start | bytes 196
  0.0 3.8 %collective-permute-start = (f32[192,128]{1,0:T(8,128)}, f32[192,128]{1,0:T(8,128)S(1)}, u32[]{:S(2)}, u32[]{:S(2)}) collective-permute-start(f32[192,128]{1,0:T(8,128)} %bitcast.4), channel_id=1, source_target_pairs={{0,16},{16,0},{1,17},{17,1},{2,18},{18,2},{3,19},{19,3},{4,20},{20... | collective-permute-start | bytes 294920 | tf_op jit(solution)/shard_map/ppermute | solution.py:622
  1.2 2.6 %copy-start = (f32[3,8,8,128]{3,2,1,0:T(8,128)S(1)}, f32[3,8,8,128]{3,2,1,0:T(8,128)}, u32[]{:S(2)}) copy-start(f32[3,8,8,128]{3,2,1,0:T(8,128)} %param.9) | copy-start | bytes 294916
  1.3 2.6 %copy-start.2 = (s32[8,128]{1,0:T(8,128)S(1)}, s32[8,128]{1,0:T(8,128)}, u32[]{:S(2)}) copy-start(s32[8,128]{1,0:T(8,128)} %depth_ref.3) | copy-start | bytes 12292
  1.3 2.6 %copy-start.3 = (f32[8,128]{1,0:T(8,128)S(1)}, f32[8,128]{1,0:T(8,128)}, u32[]{:S(2)}) copy-start(f32[8,128]{1,0:T(8,128)} %east_ref.3) | copy-start | bytes 12292
  1.3 2.6 %copy-start.4 = (f32[8,128]{1,0:T(8,128)S(1)}, f32[8,128]{1,0:T(8,128)}, u32[]{:S(2)}) copy-start(f32[8,128]{1,0:T(8,128)} %north_ref.3) | copy-start | bytes 12292
  3.9 11.9 %copy-start.1 = (f32[16,8,128]{2,1,0:T(8,128)S(1)}, f32[16,8,128]{2,1,0:T(8,128)}, u32[]{:S(2)}) copy-start(f32[16,8,128]{2,1,0:T(8,128)} %param.13) | copy-start | bytes 196612
  4.2 11.6 %collective-permute-start.1 = (f32[416,128]{1,0:T(8,128)S(1)}, f32[416,128]{1,0:T(8,128)S(1)}, u32[]{:S(2)}, u32[]{:S(2)}) collective-permute-start(f32[416,128]{1,0:T(8,128)S(1)} %get-tuple-element.23), channel_id=1, source_target_pairs={{0,4},{4,0},{8,12},{12,8},{1,5},{5,1},{9,13},{13,9},{2,6},{6,2},{1... | collective-permute-start | bytes 638984 | tf_op jit(solution)/shard_map/ppermute | solution.py:618
  5.8 9.9 %collective-permute-start.2 = (f32[416,128]{1,0:T(8,128)S(1)}, f32[416,128]{1,0:T(8,128)S(1)}, u32[]{:S(2)}, u32[]{:S(2)}) collective-permute-start(f32[416,128]{1,0:T(8,128)S(1)} %get-tuple-element.24), channel_id=1, source_target_pairs={{4,8},{8,4},{5,9},{9,5},{6,10},{10,6},{7,11},{11,7},{20,24},{24,20... | collective-permute-start | bytes 638984 | tf_op jit(solution)/shard_map/ppermute | solution.py:618
  8.9 5.8 %collective-permute-start.5 = (f32[128,128]{1,0:T(8,128)S(1)}, f32[128,128]{1,0:T(8,128)S(1)}, u32[]{:S(2)}, u32[]{:S(2)}) collective-permute-start(f32[128,128]{1,0:T(8,128)S(1)} %get-tuple-element.28.prey_ref), channel_id=1, source_target_pairs={{0,16},{16,0},{1,17},{17,1},{2,18},{18,2},{3,19},{19,3},{4,20},{20... | collective-permute-start | bytes 196616 | tf_op jit(solution)/shard_map/ppermute | solution.py:622
  10.2 4.5 %collective-permute-start.3 = (f32[32,128]{1,0:T(8,128)S(1)}, f32[32,128]{1,0:T(8,128)S(1)}, u32[]{:S(2)}, u32[]{:S(2)}) collective-permute-start(f32[32,128]{1,0:T(8,128)S(1)} %get-tuple-element.25), channel_id=1, source_target_pairs={{0,1},{1,0},{2,3},{3,2},{4,5},{5,4},{6,7},{7,6},{8,9},{9,8},{10,11... | collective-permute-start | bytes 49160 | tf_op jit(solution)/shard_map/ppermute | solution.py:618
  10.3 5.4 %collective-permute-start.4 = (f32[32,128]{1,0:T(8,128)S(1)}, f32[32,128]{1,0:T(8,128)S(1)}, u32[]{:S(2)}, u32[]{:S(2)}) collective-permute-start(f32[32,128]{1,0:T(8,128)S(1)} %get-tuple-element.26), channel_id=1, source_target_pairs={{1,2},{2,1},{5,6},{6,5},{9,10},{10,9},{13,14},{14,13},{17,18},{18,... | collective-permute-start | bytes 49160 | tf_op jit(solution)/shard_map/ppermute | solution.py:618
  20.3 9.1 %collective-permute-start.6 = (f32[384,128]{1,0:T(8,128)S(1)}, f32[384,128]{1,0:T(8,128)S(1)}, u32[]{:S(2)}, u32[]{:S(2)}) collective-permute-start(f32[384,128]{1,0:T(8,128)S(1)} %get-tuple-element.31), channel_id=1, source_target_pairs={{0,4},{4,0},{8,12},{12,8},{1,5},{5,1},{9,13},{13,9},{2,6},{6,2},{1... | collective-permute-start | bytes 589832 | tf_op jit(solution)/shard_map/ppermute | solution.py:618
  20.4 9.0 %collective-permute-start.7 = (f32[384,128]{1,0:T(8,128)S(1)}, f32[384,128]{1,0:T(8,128)S(1)}, u32[]{:S(2)}, u32[]{:S(2)}) collective-permute-start(f32[384,128]{1,0:T(8,128)S(1)} %get-tuple-element.32), channel_id=1, source_target_pairs={{4,8},{8,4},{5,9},{9,5},{6,10},{10,6},{7,11},{11,7},{20,24},{24,20... | collective-permute-start | bytes 589832 | tf_op jit(solution)/shard_map/ppermute | solution.py:618
  24.3 5.0 %collective-permute-start.10 = (f32[128,128]{1,0:T(8,128)S(1)}, f32[128,128]{1,0:T(8,128)S(1)}, u32[]{:S(2)}, u32[]{:S(2)}) collective-permute-start(f32[128,128]{1,0:T(8,128)S(1)} %get-tuple-element.36.prey_ref), channel_id=1, source_target_pairs={{0,16},{16,0},{1,17},{17,1},{2,18},{18,2},{3,19},{19,3},{4,20},{20... | collective-permute-start | bytes 196616 | tf_op jit(solution)/shard_map/ppermute | solution.py:622
  24.6 3.6 %collective-permute-start.8 = (f32[24,128]{1,0:T(8,128)S(1)}, f32[24,128]{1,0:T(8,128)S(1)}, u32[]{:S(2)}, u32[]{:S(2)}) collective-permute-start(f32[24,128]{1,0:T(8,128)S(1)} %get-tuple-element.33), channel_id=1, source_target_pairs={{0,1},{1,0},{2,3},{3,2},{4,5},{5,4},{6,7},{7,6},{8,9},{9,8},{10,11... | collective-permute-start | bytes 36872 | tf_op jit(solution)/shard_map/ppermute | solution.py:618
  24.6 4.7 %collective-permute-start.9 = (f32[24,128]{1,0:T(8,128)S(1)}, f32[24,128]{1,0:T(8,128)S(1)}, u32[]{:S(2)}, u32[]{:S(2)}) collective-permute-start(f32[24,128]{1,0:T(8,128)S(1)} %get-tuple-element.34), channel_id=1, source_target_pairs={{1,2},{2,1},{5,6},{6,5},{9,10},{10,9},{13,14},{14,13},{17,18},{18,... | collective-permute-start | bytes 36872 | tf_op jit(solution)/shard_map/ppermute | solution.py:618

commit v3 on v0

--- a/solution.py
+++ b/solution.py
@@ -1,9 +1,16 @@
+import functools
+
 import jax
 import jax.numpy as jnp
 from jax import lax
+from jax.experimental import pallas as pl
+from jax.experimental.pallas import tpu as pltpu
 from jax.sharding import PartitionSpec as P
 
 STEPS = 2
+SUB = 8
+LIM = 48 * 1024 * 1024
+INSIDE, FINISH = 2, 2
 
 
 def with_halo(cells, sides, width):
@@ -54,7 +61,7 @@
     return window(carried, 0, length, direction) - window(carried, 1, length + 1, direction)
 
 
-def on_device(tracers, fluxes, diff_east, diff_north, column_depth, grazers, groups, preference):
+def plain(tracers, fluxes, diff_east, diff_north, column_depth, grazers, groups, preference):
     tr_dev, levels, rows_dev, cols_dev = tracers.shape
     total_tracers = tr_dev * lax.axis_size("tracer")
     level_index = lax.broadcasted_iota(jnp.int32, (levels, rows_dev, cols_dev), 0)
@@ -99,6 +106,607 @@
     return tracer_field
 
 
+WIDE = 16
+EACH = 128 // WIDE
+
+
+class Geo:
+    def __init__(self, tr_dev, levels, rows, cols):
+        self.T, self.L, self.R, self.C = tr_dev, levels, rows, cols
+        self.LH = levels // SUB
+        self.tile = rows * levels
+        self.K = rows * self.LH
+        self.NV = self.K // EACH
+        self.SR = self.NV * SUB
+        self.my1 = -(-(tr_dev + 3) * self.NV // EACH)
+        self.my2 = -(-tr_dev * self.NV // EACH)
+        self.inner = Table(
+            hx=(rows + 1) * self.LH, px=(rows + 1) * self.LH, mx=(rows + 1) * self.LH,
+            kx=rows + 1, hy=self.K, py=self.K, my=self.K, ky=rows,
+            hz=self.K, pz=self.K, mz=self.K,
+        )
+        self.outer = Table(
+            hx=4 * self.LH, px=2 * self.LH, mx=2 * self.LH, kx=1,
+            hs=self.NV, ps=self.NV, ms=self.NV, ks=self.NV,
+        )
+
+
+class Table:
+    def __init__(self, **counts):
+        self.at, self.rows = {}, 0
+        for name, count in counts.items():
+            self.at[name] = self.rows
+            self.rows += count * SUB
+
+    def get(self, ref, name, index):
+        at = self.at[name] + index * SUB
+        return ref[at : at + SUB, :]
+
+    def set(self, ref, name, index, value):
+        at = self.at[name] + index * SUB
+        ref[at : at + SUB, :] = value
+
+    def set_flux(self, ref, axis, index, opened, flux):
+        flux = jnp.where(opened, flux, 0.0)
+        self.set(ref, "p" + axis, index, jnp.maximum(flux, 0.0))
+        self.set(ref, "m" + axis, index, jnp.minimum(flux, 0.0))
+
+    def set_open(self, ref, axis, index, opened):
+        self.set(ref, "h" + axis, index, jnp.where(opened, 0.5, 0.0))
+
+
+def lanes():
+    return lax.broadcasted_iota(jnp.int32, (SUB, 128), 1)
+
+
+def sublanes():
+    return lax.broadcasted_iota(jnp.int32, (SUB, 128), 0)
+
+
+def roll(v, by, axis):
+    by = by % v.shape[axis]
+    return v if by == 0 else pltpu.roll(v, by, axis)
+
+
+def registers(ref):
+    return [ref[i : i + SUB, :] for i in range(0, ref.shape[0], SUB)]
+
+
+def rows8(index):
+    return pl.ds(pl.multiple_of(index * SUB, SUB), SUB)
+
+
+def pack_strips(parts):
+    lane = lanes()
+    out = []
+    for v in range(0, len(parts), EACH):
+        packed = jnp.zeros((SUB, 128), jnp.float32)
+        for k, part in enumerate(parts[v : v + EACH]):
+            inside = (lane >= WIDE * k + 8) & (lane < WIDE * k + 16)
+            packed = jnp.where(inside, roll(part, WIDE * k + 12, 1), packed)
+        out.append(packed)
+    return out
+
+
+def message_strips(packed, low):
+    place = lanes() % WIDE
+    out = jnp.zeros((SUB, 128), jnp.float32)
+    for m, one in enumerate(packed):
+        moved = roll(one, 2 * m - (12 if low else 10), 1)
+        out = jnp.where((place == 2 * m) | (place == 2 * m + 1), moved, out)
+    return out
+
+
+def put_messages(packed, even, ev_ref, od_ref):
+    for v in range(0, len(packed), EACH):
+        low = message_strips(packed[v : v + EACH], True)
+        high = message_strips(packed[v : v + EACH], False)
+        at = rows8(v // EACH)
+        ev_ref[at, :] = jnp.where(even, high, low)
+        od_ref[at, :] = jnp.where(even, low, high)
+
+
+def full_strips(own, from_lower, from_upper, m):
+    place = lanes() % WIDE
+    out = jnp.where(place < 2, roll(from_lower, -2 * m, 1), 0.0)
+    out = jnp.where((place >= 2) & (place < 6), roll(own, -10, 1), out)
+    out = jnp.where((place >= 8) & (place < 12), own, out)
+    return jnp.where((place >= 12) & (place < 14), roll(from_upper, 12 - 2 * m, 1), out)
+
+
+def spread(rows, r):
+    return jnp.broadcast_to(rows[r : r + 1, :], (SUB, 128))
+
+
+def spread_rows(g, rows):
+    return [spread(rows, r) for r in range(g.R) for _ in range(g.LH)]
+
+
+def taste_of(groups_ref, pref_ref, t):
+    return pref_ref[groups_ref[t]]
+
+
+def is_even(axis):
+    return lax.rem(lax.axis_index(axis), 2) == 0
+
+
+def split_sides(even, ev, od):
+    return jnp.where(even, od, ev), jnp.where(even, ev, od)
+
+
+def limited(a, b):
+    least, most = jnp.minimum(a, b), jnp.maximum(a, b)
+    return jnp.maximum(least, jnp.minimum(most, 0.0))
+
+
+def each_tracer(g, ahead, body):
+    def some(i, carry):
+        for more in range(ahead):
+            body(i * ahead + more)
+        return carry
+
+    lax.fori_loop(0, g.T // ahead, some, 0)
+    for t in range(g.T - g.T % ahead, g.T):
+        body(t)
+
+
+def flux_reader(g, mine_ref, other_ref):
+    first = lax.axis_index("tracer") == 0
+    single = lax.axis_size("tracer") != 2
+
+    def flux(dim, r, lh):
+        at = pl.ds(dim * g.R * SUB + r, SUB, stride=g.R)
+        a, b = mine_ref[at, :], other_ref[at, :]
+        if single:
+            return (a, b)[lh]
+        return jnp.where(first, (a, b)[lh], (b, a)[lh])
+
+    return flux
+
+
+def load_kernel(
+    g, tracers_ref, groups_ref, pref_ref, field_ref, strips_ref, prey_ref, landed, sems
+):
+    def arrival(t):
+        at = pl.ds(pl.multiple_of(t * g.tile, g.tile), g.tile)
+        return pltpu.make_async_copy(tracers_ref.at[at, :], landed.at[at, :], sems.at[t])
+
+    for t in range(g.T):
+        arrival(t).start()
+    prey_ref[...] = jnp.zeros_like(prey_ref)
+
+    def one(t):
+        arrival(t).wait()
+        taste = taste_of(groups_ref, pref_ref, t)
+        base = pl.multiple_of(t * g.tile, g.tile)
+        parts = []
+        for r in range(g.R):
+            for lh in range(g.LH):
+                at = (r * g.LH + lh) * SUB
+                v = landed[pl.ds(base + lh * SUB * g.R + r, SUB, stride=g.R), :]
+                field_ref[pl.ds(base + at, SUB), :] = v
+                parts.append(v)
+                prey_ref[at : at + SUB, :] += taste * v
+        for i, packed in enumerate(pack_strips(parts)):
+            strips_ref[rows8(t * g.NV + i), :] = packed
+
+    each_tracer(g, 2, one)
+
+
+def first_messages_kernel(
+    g, field_ref, strips_ref, mine_ref, other_ref, depth_ref, east_ref, north_ref,
+    xev_ref, xod_ref, yev_ref, yod_ref, extra_ref,
+):
+    x_even, y_even = is_even("gx"), is_even("gy")
+    flux = flux_reader(g, mine_ref, other_ref)
+    zero = jnp.zeros((SUB, 128), jnp.float32)
+
+    def put(at, low, high):
+        xev_ref[at, :] = jnp.where(x_even, high, low)
+        xod_ref[at, :] = jnp.where(x_even, low, high)
+
+    def one(t):
+        base = pl.multiple_of(t * g.tile, g.tile)
+        for i in range(2 * g.LH):
+            low = field_ref[pl.ds(base + i * SUB, SUB), :]
+            high = field_ref[pl.ds(base + g.tile - 2 * g.L + i * SUB, SUB), :]
+            put(rows8(t * 2 * g.LH + i), low, high)
+
+    each_tracer(g, 2, one)
+    at = g.T * 2 * g.LH
+    for lh in range(g.LH):
+        put(rows8(at + lh), zero, flux(0, g.R - 1, lh))
+    depth = depth_ref[...].astype(jnp.float32)
+    put(rows8(at + g.LH), depth, roll(depth, 2, 0))
+    put(rows8(at + g.LH + 1), zero, roll(east_ref[...], 1, 0))
+    extras = pack_strips(spread_rows(g, depth))
+    extras += pack_strips([flux(1, r, lh) for r in range(g.R) for lh in range(g.LH)])
+    extras += pack_strips(spread_rows(g, north_ref[...]))
+    for i, packed in enumerate(extras):
+        extra_ref[rows8(i), :] = packed
+    put_messages(registers(strips_ref) + extras, y_even, yev_ref, yod_ref)
+
+
+def wet_levels(g, depths):
+    level = [(sublanes() + SUB * lh).astype(jnp.float32) for lh in range(g.LH)]
+    return [[level[lh] < d for lh in range(g.LH)] for d in depths]
+
+
+def inner_coefficients(g, cf, flux, depth, east, north):
+    tab, sub = g.inner, sublanes()
+    depths = [spread(depth, r) for r in range(g.R)]
+    wet = wet_levels(g, depths)
+    wet_before = wet_levels(g, [roll(d, 1, 1) for d in depths])
+    for r in range(g.R):
+        tab.set(cf, "kx", r + 1, 2.0 * spread(east, r))
+        tab.set(cf, "ky", r, 2.0 * roll(spread(north, r), 1, 1))
+        flux_z = [roll(flux(2, r, lh), 1, 0) for lh in range(g.LH)]
+        for lh in range(g.LH):
+            k, here = r * g.LH + lh, wet[r][lh]
+            if r:
+                opened = here & wet[r - 1][lh]
+                tab.set_open(cf, "x", k, opened)
+                tab.set_flux(cf, "x", k, opened, flux(0, r - 1, lh))
+            opened = here & wet_before[r][lh]
+            tab.set_open(cf, "y", k, opened)
+            tab.set_flux(cf, "y", k, opened, roll(flux(1, r, lh), 1, 1))
+            opened = here if lh else here & (sub > 0)
+            above = jnp.where(sub == 0, flux_z[lh - 1], flux_z[lh]) if lh else flux_z[lh]
+            tab.set_open(cf, "z", k, opened)
+            tab.set_flux(cf, "z", k, opened, above)
+
+
+def outer_coefficients(g, cf, extra_x, extra_y, flux, extra_ref, depth, east):
+    tab, lane = g.outer, lanes()
+    depth_low, depth_high = extra_x(g.LH)
+    depths = [spread(depth_low, 0), spread(depth_low, 1), spread(depth, 0), spread(depth, g.R - 1)]
+    depths += [spread(depth_high, 0), spread(depth_high, 1)]
+    wet = wet_levels(g, depths)
+    tab.set(cf, "kx", 0, 2.0 * spread(extra_x(g.LH + 1)[0], 0))
+    for lh in range(g.LH):
+        for face, row in enumerate((0, 1, 3, 4)):
+            tab.set_open(cf, "x", face * g.LH + lh, wet[row][lh] & wet[row + 1][lh])
+        tab.set_flux(cf, "x", lh, wet[1][lh] & wet[2][lh], extra_x(lh)[0])
+        tab.set_flux(cf, "x", g.LH + lh, wet[3][lh] & wet[4][lh], flux(0, g.R - 1, lh))
+    place, half = lane % WIDE, (lane // WIDE) % g.LH
+    for i in range(g.NV):
+        full = []
+        for which in range(3):
+            own = which * g.NV + i
+            slot = g.T * g.NV + own
+            full.append(full_strips(extra_ref[rows8(own), :], *extra_y(slot // EACH), slot % EACH))
+        wet_s = jnp.where((sublanes() + SUB * half).astype(jnp.float32) < full[0], 1.0, 0.0)
+        opened = (wet_s * roll(wet_s, 1, 1) > 0.0) & (place != 0) & (place != 8)
+        tab.set_open(cf, "s", i, opened)
+        tab.set_flux(cf, "s", i, opened, roll(full[1], 1, 1))
+        tab.set(cf, "ks", i, 2.0 * roll(full[2], 1, 1))
+
+
+def end_lanes():
+    lane = lanes()
+    return (lane < 2) | (lane >= 126)
+
+
+def inside_kernel(g, ahead, first, field_ref, *refs):
+    if first:
+        mine_ref, other_ref, depth_ref, east_ref, north_ref, part_ref, cf = refs
+        inner_coefficients(
+            g, cf, flux_reader(g, mine_ref, other_ref), depth_ref[...].astype(jnp.float32),
+            east_ref[...], north_ref[...],
+        )
+    else:
+        cf, part_ref = refs
+    sub = sublanes()
+    ends, top, bottom = end_lanes(), sub == 0, sub == SUB - 1
+
+    def coef(name, index):
+        return g.inner.get(cf, name, index)
+
+    def shift_down(v):
+        rolled = [roll(x, 1, 0) for x in v]
+        return rolled[:1] + [
+            jnp.where(top, rolled[i - 1], rolled[i]) for i in range(1, g.LH)
+        ]
+
+    def shift_up(v):
+        rolled = [roll(x, -1, 0) for x in v]
+        return [jnp.where(bottom, rolled[(i + 1) % g.LH], rolled[i]) for i in range(g.LH)]
+
+    def one(t):
+        base = pl.multiple_of(t * g.tile, g.tile)
+        for r in range(g.R):
+            index = [r * g.LH + lh for lh in range(g.LH)]
+            at = [pl.ds(base + k * SUB, SUB) for k in index]
+            cells = [field_ref[a, :] for a in at]
+            news = []
+            for k, c in zip(index, cells):
+                j = coef("hy", k) * (c - roll(c, 1, 1))
+                s = limited(j, roll(j, -1, 1))
+                flow = coef("py", k) * roll(c + s, 1, 1) + coef("my", k) * (c - s)
+                flow = flow - coef("ky", r) * j
+                news.append(c + jnp.where(ends, 0.0, flow - roll(flow, -1, 1)))
+            j = [coef("hz", k) * (c - a) for k, c, a in zip(index, cells, shift_down(cells))]
+            s = [limited(a, b) for a, b in zip(j, shift_up(j))]
+            above = shift_down([c + v for c, v in zip(cells, s)])
+            flow = [
+                coef("pz", k) * a + coef("mz", k) * (c - v)
+                for k, a, c, v in zip(index, above, cells, s)
+            ]
+            for a, new, high, low in zip(at, news, flow, shift_up(flow)):
+                part_ref[a, :] = new + (high - low)
+
+    each_tracer(g, ahead, one)
+
+
+def strip_tendency(g, cf, full, i):
+    def coef(name):
+        return g.outer.get(cf, name, i)
+
+    j = coef("hs") * (full - roll(full, 1, 1))
+    s = limited(j, roll(j, -1, 1))
+    flow = coef("ps") * roll(full + s, 1, 1) + coef("ms") * (full - s) - coef("ks") * j
+    tend = flow - roll(flow, -1, 1)
+    return jnp.where(lanes() % WIDE < 12, tend, roll(tend, 10, 1))
+
+
+def all_strip_tendencies(g, cf, strips_ref, sides, tend_ref):
+    for n in range(g.T * g.NV):
+        full = full_strips(strips_ref[rows8(n), :], *sides(n // EACH), n % EACH)
+        tend_ref[rows8(n), :] = strip_tendency(g, cf, full, n % g.NV)
+
+
+def set_factor(g, total, factor, grazers_ref, prey_refs):
+    for r in range(g.R):
+        for lh in range(g.LH):
+            at = rows8(r * g.LH + lh)
+            prey = sum(ref[at, :] for ref in prey_refs)
+            grazers = grazers_ref[pl.ds(lh * SUB * g.R + r, SUB, stride=g.R), :]
+            factor[at, :] = grazers / (1.0 + 4.0 * prey / total)
+
+
+def finish(g, inner, outer, t, field_ref, part_ref, tend_ref, sides, taste, factor, emit):
+    base = pl.multiple_of(t * g.tile, g.tile)
+    ends = end_lanes()
+
+    def cell(r, lh):
+        if 0 <= r < g.R:
+            return field_ref[pl.ds(base + (r * g.LH + lh) * SUB, SUB), :]
+        i = r + 2 if r < 0 else r - g.R
+        return sides(t * 2 * g.LH + i * g.LH + lh)[0 if r < 0 else 1]
+
+    def coef(name, f, lh):
+        if 0 < f < g.R:
+            return g.inner.get(inner, name, f * g.LH + lh)
+        if name == "hx":
+            return g.outer.get(outer, name, {-1: 0, 0: 1, g.R: 2, g.R + 1: 3}[f] * g.LH + lh)
+        return g.outer.get(outer, name, (g.LH if f else 0) + lh)
+
+    state = [None] * g.LH
+    tends = [tend_ref[rows8(t * g.NV + i), :] for i in range(g.NV)]
+    for f in range(-1, g.R + 2):
+        kappa = g.inner.get(inner, "kx", f) if f > 0 else g.outer.get(outer, "kx", 0)
+        for lh in range(g.LH):
+            if f < 0:
+                below = cell(-2, lh)
+                here = cell(-1, lh)
+                state[lh] = (here, coef("hx", f, lh) * (here - below), None, None)
+                continue
+            c, j, left, carried = state[lh]
+            up = cell(f, lh)
+            j_up = coef("hx", f, lh) * (up - c)
+            s = limited(j, j_up)
+            if f > 0:
+                kap = g.inner.get(inner, "kx", f - 1) if f > 1 else g.outer.get(outer, "kx", 0)
+                flow = coef("px", f - 1, lh) * left + coef("mx", f - 1, lh) * (c - s) - kap * j
+                if f > 1:
+                    r = f - 2
+                    k = r * g.LH + lh
+                    v, n = divmod(k, EACH)
+                    old = cell(r, lh)
+                    new = part_ref[pl.ds(base + k * SUB, SUB), :] + (carried - flow)
+                    new = new + jnp.where(ends, roll(tends[v], -(WIDE * n + 12), 1), 0.0)
+                    new = new - (taste * factor[rows8(k), :]) * old
+                    emit(r, lh, new)
+                carried = flow
+            state[lh] = (up, j_up, c + s, carried)
+
+
+def reader(even, ev_ref, od_ref):
+    def sides(i):
+        at = rows8(i)
+        return split_sides(even, ev_ref[at, :], od_ref[at, :])
+
+    return sides
+
+
+def step_one_kernel(
+    g, total, ahead,
+    field_ref, part_ref, strips_ref, xev_ref, xod_ref, yev_ref, yod_ref, inner, extra_ref,
+    mine_ref, other_ref, depth_ref, east_ref, grazers_ref, groups_ref, pref_ref, *rest,
+):
+    prey_refs, rest = rest[:-10], rest[-10:]
+    (out_ref, xev2_ref, xod2_ref, yev2_ref, yod2_ref, strips2_ref, prey2_ref, outer,
+     factor, tend_ref) = rest
+    x_even, y_even = is_even("gx"), is_even("gy")
+    x_sides, y_sides = reader(x_even, xev_ref, xod_ref), reader(y_even, yev_ref, yod_ref)
+    outer_coefficients(
+        g, outer, lambda i: x_sides(g.T * 2 * g.LH + i), y_sides,
+        flux_reader(g, mine_ref, other_ref), extra_ref,
+        depth_ref[...].astype(jnp.float32), east_ref[...],
+    )
+    set_factor(g, total, factor, grazers_ref, prey_refs)
+    all_strip_tendencies(g, outer, strips_ref, y_sides, tend_ref)
+    prey2_ref[...] = jnp.zeros_like(prey2_ref)
+
+    def one(t):
+        taste = taste_of(groups_ref, pref_ref, t)
+        base = pl.multiple_of(t * g.tile, g.tile)
+        news = {}
+
+        def emit(r, lh, new):
+            at = (r * g.LH + lh) * SUB
+            out_ref[pl.ds(base + at, SUB), :] = new
+            prey2_ref[at : at + SUB, :] += taste * new
+            news[r, lh] = new
+
+        finish(g, inner, outer, t, field_ref, part_ref, tend_ref, x_sides, taste, factor, emit)
+        for i in range(2):
+            for lh in range(g.LH):
+                at = rows8(t * 2 * g.LH + i * g.LH + lh)
+                low, high = news[i, lh], news[g.R - 2 + i, lh]
+                xev2_ref[at, :] = jnp.where(x_even, high, low)
+                xod2_ref[at, :] = jnp.where(x_even, low, high)
+        parts = [news[r, lh] for r in range(g.R) for lh in range(g.LH)]
+        for i, packed in enumerate(pack_strips(parts)):
+            strips2_ref[rows8(t * g.NV + i), :] = packed
+
+    each_tracer(g, ahead, one)
+    put_messages(registers(strips2_ref), y_even, yev2_ref, yod2_ref)
+
+
+def step_two_kernel(
+    g, total, ahead,
+    field_ref, part_ref, strips_ref, xev_ref, xod_ref, yev_ref, yod_ref, inner, outer,
+    grazers_ref, groups_ref, pref_ref, *rest,
+):
+    prey_refs, (out_ref, factor, tend_ref, leaving, sems) = rest[:-5], rest[-5:]
+    x_sides = reader(is_even("gx"), xev_ref, xod_ref)
+    y_sides = reader(is_even("gy"), yev_ref, yod_ref)
+    set_factor(g, total, factor, grazers_ref, prey_refs)
+    all_strip_tendencies(g, outer, strips_ref, y_sides, tend_ref)
+
+    def departure(t):
+        at = pl.ds(pl.multiple_of(t * g.tile, g.tile), g.tile)
+        return pltpu.make_async_copy(leaving.at[at, :], out_ref.at[at, :], sems.at[t])
+
+    def one(t):
+        taste = taste_of(groups_ref, pref_ref, t)
+        base = pl.multiple_of(t * g.tile, g.tile)
+
+        def emit(r, lh, new):
+            leaving[pl.ds(base + lh * SUB * g.R + r, SUB, stride=g.R), :] = new
+
+        finish(g, inner, outer, t, field_ref, part_ref, tend_ref, x_sides, taste, factor, emit)
+        departure(t).start()
+
+    each_tracer(g, ahead, one)
+    for t in range(g.T):
+        departure(t).wait()
+
+
+def call(body, outs, operands, scalars=(), far_out=False, scratch=(), cost=0):
+    spaces = [pltpu.SMEM if i in scalars else pltpu.VMEM for i in range(len(operands))]
+    if far_out is None:
+        spaces[0] = pltpu.HBM
+        operands = [pltpu.with_memory_space_constraint(operands[0], pltpu.HBM), *operands[1:]]
+    return pl.pallas_call(
+        body,
+        out_shape=[jax.ShapeDtypeStruct((rows, 128), jnp.float32) for rows in outs],
+        in_specs=[pl.BlockSpec(memory_space=space) for space in spaces],
+        out_specs=[pl.BlockSpec(memory_space=pltpu.HBM if far_out else pltpu.VMEM)] * len(outs),
+        scratch_shapes=[
+            pltpu.VMEM((rows, 128), jnp.float32) if isinstance(rows, int) else rows
+            for rows in scratch
+        ],
+        compiler_params=pltpu.CompilerParams(vmem_limit_bytes=LIM),
+        cost_estimate=pl.CostEstimate(flops=cost, bytes_accessed=0, transcendentals=0)
+        if cost
+        else None,
+    )(*operands)
+
+
+def pair_swap(values, axis, start):
+    pairs = []
+    for i in range(start, lax.axis_size(axis) - 1, 2):
+        pairs += [(i, i + 1), (i + 1, i)]
+    if not pairs:
+        return jnp.zeros_like(values)
+    return lax.ppermute(values, axis, pairs)
+
+
+def tracer_swap(values):
+    return lax.ppermute(values, "tracer", [(0, 1), (1, 0)])
+
+
+def all_prey(values):
+    if lax.axis_size("tracer") == 2:
+        return [values, tracer_swap(values)]
+    return [lax.psum(values, "tracer")]
+
+
+def neighbours(x_ev, x_od, y_ev, y_od):
+    x_od = pair_swap(x_od, "gx", 1)
+    y_ev = pair_swap(y_ev, "gy", 0)
+    y_od = pair_swap(y_od, "gy", 1)
+    x_ev = pair_swap(x_ev, "gx", 0)
+    return x_ev, x_od, y_ev, y_od
+
+
+def on_device(tracers, fluxes, diff_east, diff_north, column_depth, grazers, groups, preference):
+    tr_dev, levels, rows, cols = tracers.shape
+    parts = lax.axis_size("tracer")
+    if not (cols == 128 and rows * levels == cols and levels == 2 * SUB and rows % SUB == 0):
+        return plain(
+            tracers, fluxes, diff_east, diff_north, column_depth, grazers, groups, preference
+        )
+    g = Geo(tr_dev, levels, rows, cols)
+    total = float(tr_dev * parts)
+    flat = tracers.reshape(-1, cols)
+    grazers = grazers.reshape(-1, cols)
+    cells = g.T * g.tile
+    copies = pltpu.SemaphoreType.DMA((g.T,))
+
+    if parts == 2:
+        mine = fluxes.reshape(-1, cols)
+        other = tracer_swap(mine)
+    else:
+        gathered = lax.all_gather(fluxes, "tracer", axis=1, tiled=True)
+        mine, other = (gathered[:, i : i + SUB].reshape(-1, cols) for i in (0, SUB))
+    field, strips, prey = call(
+        functools.partial(load_kernel, g),
+        [cells, g.T * g.SR, g.tile],
+        [flat, groups, preference],
+        scalars=(1, 2),
+        far_out=None,
+        scratch=[cells, copies],
+    )
+    prey = all_prey(prey)
+    x_rows = g.T * 2 * g.L
+    x_more = x_rows + g.L + 2 * SUB
+    *messages, extra = call(
+        functools.partial(first_messages_kernel, g),
+        [x_more, x_more, g.my1 * SUB, g.my1 * SUB, 3 * g.SR],
+        [field, strips, mine, other, column_depth, diff_east, diff_north],
+    )
+    messages = neighbours(*messages)
+    part, inner = call(
+        functools.partial(inside_kernel, g, INSIDE, True),
+        [cells, g.inner.rows],
+        [field, mine, other, column_depth, diff_east, diff_north],
+    )
+    *results, outer = call(
+        functools.partial(step_one_kernel, g, total, FINISH),
+        [cells, x_rows, x_rows, g.my2 * SUB, g.my2 * SUB, g.T * g.SR, g.tile, g.outer.rows],
+        [field, part, strips, *messages, inner, extra, mine, other, column_depth, diff_east,
+         grazers, groups, preference, *prey],
+        scalars=(14, 15),
+        scratch=[g.tile, g.T * g.SR],
+    )
+    field, *messages, strips, prey = results
+    prey = all_prey(prey)
+    messages = neighbours(*messages)
+    (part,) = call(functools.partial(inside_kernel, g, INSIDE, False), [cells], [field, inner])
+    (out,) = call(
+        functools.partial(step_two_kernel, g, total, FINISH),
+        [cells],
+        [field, part, strips, *messages, inner, outer, grazers, groups, preference, *prey],
+        scalars=(10, 11),
+        far_out=True,
+        scratch=[g.tile, g.T * g.SR, cells, copies],
+    )
+    return out.reshape(tracers.shape)
+
+
 def solution(mesh):
     placed = (
         P("tracer", None, "gx", "gy"),

time: 147 us -> 31.2 us (0.21)
  the two profiles are of different devices: /device:TPU:0 before, /device:TPU:9 now
where the time goes in v3:
time: 31.2 us; the launch traced here: 30.9 us
  starting transfers between devices  18.9 us (61%)
  Pallas kernels  11.7 us (38%)
    ppermute x8, starting transfers between devices, pair_swap(): return lax.ppermute(values, axis, pairs)  16.1 us
    pallas_call x6, Pallas kernels, call(): pl.pallas_call(body, out_shape=[jax.ShapeDtypeStruct((rows, 128), jnp.flo...  11.7 us
    ppermute x3, starting transfers between devices, tracer_swap(): return lax.ppermute(values, 'tracer', [(0, 1), (1, 0)])  2.84 us
  transfers between devices with their start and end apart: 11, of which 0 were waited for; matrix products, arithmetic and copies ran while one was open for 0% of the time, Pallas kernels for 21%

profile of v3, /device:TPU:9, one launch (start us, length us, event | category | flops | bytes accessed | tf_op | source)
XLA Modules:
  0.0 30.9 jit_solution(6696528647345725144)
XLA Ops:
  0.0 0.0 copy-start.5
  0.0 0.0 copy-start.6
  0.0 1.2 %collective-permute-start = (f32[192,128]{1,0:T(8,128)}, f32[192,128]{1,0:T(8,128)S(1)}, u32[]{:S(2)}, u32[]{:S(2)}) collective-permute-start(f32[192,128]{1,0:T(8,128)} %bitcast.4), channel_id=1, source_target_pairs={{0,16},{16,0},{1,17},{17,1},{2,18},{18,2},{3,19},{19,3},{4,20},{20... | collective-permute-start | bytes 294920 | tf_op jit(solution)/shard_map/ppermute | solution.py:628
  1.2 0.0 copy-done.5
  1.2 0.0 copy-done.6
  1.2 0.0 copy-start
  1.3 0.0 copy-start.2
  1.3 0.0 copy-start.3
  1.3 0.0 copy-start.4
  1.3 2.5 %shard_map.82 = (f32[1536,128]{1,0:T(8,128)S(1)}, f32[192,128]{1,0:T(8,128)S(1)}, f32[128,128]{1,0:T(8,128)S(1)}) custom-call(f32[1536,128]{1,0:T(8,128)} %bitcast.10, s32[12]{0:T(128)S(1)} %copy-done.5, f32[16]{0:T(128)S(1)} %copy-done.6), custom_call_target="tpu_custom_call" | custom-call | tf_op jit(solution)/shard_map/pallas_call | solution.py:602
  3.8 0.0 collective-permute-done.refs_1_.other_ref
  3.8 0.0 copy-done
  3.9 0.0 copy-done.2
  3.9 0.0 copy-done.3
  3.9 0.0 copy-done.4
  3.9 0.3 shard_map.84
  4.1 1.7 %collective-permute-start.1 = (f32[416,128]{1,0:T(8,128)S(1)}, f32[416,128]{1,0:T(8,128)S(1)}, u32[]{:S(2)}, u32[]{:S(2)}) collective-permute-start(f32[416,128]{1,0:T(8,128)S(1)} %get-tuple-element.26), channel_id=1, source_target_pairs={{0,4},{4,0},{8,12},{12,8},{1,5},{5,1},{9,13},{13,9},{2,6},{6,2},{1... | collective-permute-start | bytes 638984 | tf_op jit(solution)/shard_map/ppermute | solution.py:624
  5.9 3.0 %collective-permute-start.2 = (f32[416,128]{1,0:T(8,128)S(1)}, f32[416,128]{1,0:T(8,128)S(1)}, u32[]{:S(2)}, u32[]{:S(2)}) collective-permute-start(f32[416,128]{1,0:T(8,128)S(1)} %get-tuple-element.27), channel_id=1, source_target_pairs={{4,8},{8,4},{5,9},{9,5},{6,10},{10,6},{7,11},{11,7},{20,24},{24,20... | collective-permute-start | bytes 638984 | tf_op jit(solution)/shard_map/ppermute | solution.py:624
  8.9 1.3 %collective-permute-start.5 = (f32[128,128]{1,0:T(8,128)S(1)}, f32[128,128]{1,0:T(8,128)S(1)}, u32[]{:S(2)}, u32[]{:S(2)}) collective-permute-start(f32[128,128]{1,0:T(8,128)S(1)} %get-tuple-element.32.rest_0_), channel_id=1, source_target_pairs={{0,16},{16,0},{1,17},{17,1},{2,18},{18,2},{3,19},{19,3},{4,20},{20... | collective-permute-start | bytes 196616 | tf_op jit(solution)/shard_map/ppermute | solution.py:628
  10.2 0.2 collective-permute-start.3
  10.4 0.0 copy-start.1
  10.4 4.5 %collective-permute-start.4 = (f32[32,128]{1,0:T(8,128)S(1)}, f32[32,128]{1,0:T(8,128)S(1)}, u32[]{:S(2)}, u32[]{:S(2)}) collective-permute-start(f32[32,128]{1,0:T(8,128)S(1)} %get-tuple-element.29), channel_id=1, source_target_pairs={{1,2},{2,1},{5,6},{6,5},{9,10},{10,9},{13,14},{14,13},{17,18},{18,... | collective-permute-start | bytes 49160 | tf_op jit(solution)/shard_map/ppermute | solution.py:624
  14.8 2.0 %shard_map.83 = (f32[1536,128]{1,0:T(8,128)S(1)}, f32[1336,128]{1,0:T(8,128)S(1)}) custom-call(f32[1536,128]{1,0:T(8,128)S(1)} %get-tuple-element.23.field_ref, f32[192,128]{1,0:T(8,128)S(1)} %bitcast.6, f32[192,128]{1,0:T(8,128)S(1)} %collective-permute-done.refs_1_.other_ref, s32[8,128]{1,0:T(8,128)S(1)} %copy-done.2, f32[8,128]{1,0:T(8,128)S(1)} %copy-done.3, ...), custom_call_target="tpu_custom_call" | custom-call | tf_op jit(solution)/shard_map/pallas_call | solution.py:602
  16.8 0.0 collective-permute-done.5.rest_1_
  16.9 0.0 collective-permute-done.3.yev_ref
  16.9 0.0 collective-permute-done.4.yod_ref
  16.9 0.0 collective-permute-done.1.xev_ref
  16.9 0.0 collective-permute-done.2.xod_ref
  16.9 0.0 copy-done.1
  16.9 2.4 %shard_map.85 = (f32[1536,128]{1,0:T(8,128)S(1)}, f32[384,128]{1,0:T(8,128)S(1)}, f32[384,128]{1,0:T(8,128)S(1)}, f32[24,128]{1,0:T(8,128)S(1)}, f32[24,128]{1,0...) custom-call(f32[1536,128]{1,0:T(8,128)S(1)} %get-tuple-element.23.field_ref, ...), custom_call_target="tpu_custom_call" | custom-call | tf_op jit(solution)/shard_map/pallas_call | solution.py:602
  19.3 0.1 collective-permute-start.6
  19.4 3.4 %collective-permute-start.7 = (f32[384,128]{1,0:T(8,128)S(1)}, f32[384,128]{1,0:T(8,128)S(1)}, u32[]{:S(2)}, u32[]{:S(2)}) collective-permute-start(f32[384,128]{1,0:T(8,128)S(1)} %get-tuple-element.36), channel_id=1, source_target_pairs={{4,8},{8,4},{5,9},{9,5},{6,10},{10,6},{7,11},{11,7},{20,24},{24,20... | collective-permute-start | bytes 589832 | tf_op jit(solution)/shard_map/ppermute | solution.py:624
  22.8 0.3 collective-permute-start.10
  23.1 0.0 collective-permute-start.8
  23.1 3.3 %collective-permute-start.9 = (f32[24,128]{1,0:T(8,128)S(1)}, f32[24,128]{1,0:T(8,128)S(1)}, u32[]{:S(2)}, u32[]{:S(2)}) collective-permute-start(f32[24,128]{1,0:T(8,128)S(1)} %get-tuple-element.38), channel_id=1, source_target_pairs={{1,2},{2,1},{5,6},{6,5},{9,10},{10,9},{13,14},{14,13},{17,18},{18,... | collective-permute-start | bytes 36872 | tf_op jit(solution)/shard_map/ppermute | solution.py:624
  26.3 1.9 %shard_map.86.part_ref = f32[1536,128]{1,0:T(8,128)S(1)} custom-call(f32[1536,128]{1,0:T(8,128)S(1)} %get-tuple-element.33.field_ref, f32[1336,128]{1,0:T(8,128)S(1)} %get-tuple-element.30.inner.refs_0_), custom_call_target="tpu_custom_call" | custom-call | tf_op jit(solution)/shard_map/pallas_call | solution.py:602
  28.3 0.0 collective-permute-done.8.yev_ref
  28.3 0.0 collective-permute-done.9.yod_ref
  28.3 0.0 collective-permute-done.10.rest_1_
  28.3 0.0 collective-permute-done.6.xev_ref
  28.3 0.0 collective-permute-done.7.xod_ref
  28.3 2.6 %shard_map.87 = f32[1536,128]{1,0:T(8,128)} custom-call(f32[1536,128]{1,0:T(8,128)S(1)} %get-tuple-element.33.field_ref, f32[1536,128]{1,0:T(8,128)S(1)} %shard_map.86.part_ref, f32[192,128]{1,0:T(8,128)S(1)} %get-tuple-element.34.strips_ref, f32[384,128]{1,0:T(8,128)S(1)} %collective-permute-done.6.xev_ref, f32[384,128]{1,0:T(8,128)S(1)} %collective-permute-done.7.xod_ref, ...), custom_call_target="tpu_custom_call" | custom-call | tf_op jit(solution)/shard_map/pallas_call | solution.py:602
Async XLA Ops:
  0.0 1.2 %copy-start.5 = (s32[12]{0:T(128)S(1)}, s32[12]{0:T(128)}, u32[]{:S(2)}) copy-start(s32[12]{0:T(128)} %groups_ref.5) | copy-start | bytes 148
  0.0 1.2 %copy-start.6 = (f32[16]{0:T(128)S(1)}, f32[16]{0:T(128)}, u32[]{:S(2)}) copy-start(f32[16]{0:T(128)} %pref_ref.5) | copy-start | bytes 196
  0.0 3.8 %collective-permute-start = (f32[192,128]{1,0:T(8,128)}, f32[192,128]{1,0:T(8,128)S(1)}, u32[]{:S(2)}, u32[]{:S(2)}) collective-permute-start(f32[192,128]{1,0:T(8,128)} %bitcast.4), channel_id=1, source_target_pairs={{0,16},{16,0},{1,17},{17,1},{2,18},{18,2},{3,19},{19,3},{4,20},{20... | collective-permute-start | bytes 294920 | tf_op jit(solution)/shard_map/ppermute | solution.py:628
  1.2 2.6 %copy-start = (f32[3,8,8,128]{3,2,1,0:T(8,128)S(1)}, f32[3,8,8,128]{3,2,1,0:T(8,128)}, u32[]{:S(2)}) copy-start(f32[3,8,8,128]{3,2,1,0:T(8,128)} %param.9) | copy-start | bytes 294916
  1.3 2.6 %copy-start.2 = (s32[8,128]{1,0:T(8,128)S(1)}, s32[8,128]{1,0:T(8,128)}, u32[]{:S(2)}) copy-start(s32[8,128]{1,0:T(8,128)} %depth_ref.3) | copy-start | bytes 12292
  1.3 2.6 %copy-start.3 = (f32[8,128]{1,0:T(8,128)S(1)}, f32[8,128]{1,0:T(8,128)}, u32[]{:S(2)}) copy-start(f32[8,128]{1,0:T(8,128)} %east_ref.3) | copy-start | bytes 12292
  1.3 2.6 %copy-start.4 = (f32[8,128]{1,0:T(8,128)S(1)}, f32[8,128]{1,0:T(8,128)}, u32[]{:S(2)}) copy-start(f32[8,128]{1,0:T(8,128)} %north_ref.1) | copy-start | bytes 12292
  4.1 12.7 %collective-permute-start.1 = (f32[416,128]{1,0:T(8,128)S(1)}, f32[416,128]{1,0:T(8,128)S(1)}, u32[]{:S(2)}, u32[]{:S(2)}) collective-permute-start(f32[416,128]{1,0:T(8,128)S(1)} %get-tuple-element.26), channel_id=1, source_target_pairs={{0,4},{4,0},{8,12},{12,8},{1,5},{5,1},{9,13},{13,9},{2,6},{6,2},{1... | collective-permute-start | bytes 638984 | tf_op jit(solution)/shard_map/ppermute | solution.py:624
  5.9 11.0 %collective-permute-start.2 = (f32[416,128]{1,0:T(8,128)S(1)}, f32[416,128]{1,0:T(8,128)S(1)}, u32[]{:S(2)}, u32[]{:S(2)}) collective-permute-start(f32[416,128]{1,0:T(8,128)S(1)} %get-tuple-element.27), channel_id=1, source_target_pairs={{4,8},{8,4},{5,9},{9,5},{6,10},{10,6},{7,11},{11,7},{20,24},{24,20... | collective-permute-start | bytes 638984 | tf_op jit(solution)/shard_map/ppermute | solution.py:624
  8.9 8.0 %collective-permute-start.5 = (f32[128,128]{1,0:T(8,128)S(1)}, f32[128,128]{1,0:T(8,128)S(1)}, u32[]{:S(2)}, u32[]{:S(2)}) collective-permute-start(f32[128,128]{1,0:T(8,128)S(1)} %get-tuple-element.32.rest_0_), channel_id=1, source_target_pairs={{0,16},{16,0},{1,17},{17,1},{2,18},{18,2},{3,19},{19,3},{4,20},{20... | collective-permute-start | bytes 196616 | tf_op jit(solution)/shard_map/ppermute | solution.py:628
  10.2 6.7 %collective-permute-start.3 = (f32[32,128]{1,0:T(8,128)S(1)}, f32[32,128]{1,0:T(8,128)S(1)}, u32[]{:S(2)}, u32[]{:S(2)}) collective-permute-start(f32[32,128]{1,0:T(8,128)S(1)} %get-tuple-element.28), channel_id=1, source_target_pairs={{0,1},{1,0},{2,3},{3,2},{4,5},{5,4},{6,7},{7,6},{8,9},{9,8},{10,11... | collective-permute-start | bytes 49160 | tf_op jit(solution)/shard_map/ppermute | solution.py:624
  10.4 6.5 %copy-start.1 = (f32[16,8,128]{2,1,0:T(8,128)S(1)}, f32[16,8,128]{2,1,0:T(8,128)}, u32[]{:S(2)}) copy-start(f32[16,8,128]{2,1,0:T(8,128)} %param.13) | copy-start | bytes 196612
  10.4 6.5 %collective-permute-start.4 = (f32[32,128]{1,0:T(8,128)S(1)}, f32[32,128]{1,0:T(8,128)S(1)}, u32[]{:S(2)}, u32[]{:S(2)}) collective-permute-start(f32[32,128]{1,0:T(8,128)S(1)} %get-tuple-element.29), channel_id=1, source_target_pairs={{1,2},{2,1},{5,6},{6,5},{9,10},{10,9},{13,14},{14,13},{17,18},{18,... | collective-permute-start | bytes 49160 | tf_op jit(solution)/shard_map/ppermute | solution.py:624
  19.3 9.0 %collective-permute-start.6 = (f32[384,128]{1,0:T(8,128)S(1)}, f32[384,128]{1,0:T(8,128)S(1)}, u32[]{:S(2)}, u32[]{:S(2)}) collective-permute-start(f32[384,128]{1,0:T(8,128)S(1)} %get-tuple-element.35), channel_id=1, source_target_pairs={{0,4},{4,0},{8,12},{12,8},{1,5},{5,1},{9,13},{13,9},{2,6},{6,2},{1... | collective-permute-start | bytes 589832 | tf_op jit(solution)/shard_map/ppermute | solution.py:624
  19.4 8.9 %collective-permute-start.7 = (f32[384,128]{1,0:T(8,128)S(1)}, f32[384,128]{1,0:T(8,128)S(1)}, u32[]{:S(2)}, u32[]{:S(2)}) collective-permute-start(f32[384,128]{1,0:T(8,128)S(1)} %get-tuple-element.36), channel_id=1, source_target_pairs={{4,8},{8,4},{5,9},{9,5},{6,10},{10,6},{7,11},{11,7},{20,24},{24,20... | collective-permute-start | bytes 589832 | tf_op jit(solution)/shard_map/ppermute | solution.py:624
  22.8 5.5 %collective-permute-start.10 = (f32[128,128]{1,0:T(8,128)S(1)}, f32[128,128]{1,0:T(8,128)S(1)}, u32[]{:S(2)}, u32[]{:S(2)}) collective-permute-start(f32[128,128]{1,0:T(8,128)S(1)} %get-tuple-element.40.rest_0_), channel_id=1, source_target_pairs={{0,16},{16,0},{1,17},{17,1},{2,18},{18,2},{3,19},{19,3},{4,20},{20... | collective-permute-start | bytes 196616 | tf_op jit(solution)/shard_map/ppermute | solution.py:628
  23.1 5.2 %collective-permute-start.8 = (f32[24,128]{1,0:T(8,128)S(1)}, f32[24,128]{1,0:T(8,128)S(1)}, u32[]{:S(2)}, u32[]{:S(2)}) collective-permute-start(f32[24,128]{1,0:T(8,128)S(1)} %get-tuple-element.37), channel_id=1, source_target_pairs={{0,1},{1,0},{2,3},{3,2},{4,5},{5,4},{6,7},{7,6},{8,9},{9,8},{10,11... | collective-permute-start | bytes 36872 | tf_op jit(solution)/shard_map/ppermute | solution.py:624
  23.1 5.2 %collective-permute-start.9 = (f32[24,128]{1,0:T(8,128)S(1)}, f32[24,128]{1,0:T(8,128)S(1)}, u32[]{:S(2)}, u32[]{:S(2)}) collective-permute-start(f32[24,128]{1,0:T(8,128)S(1)} %get-tuple-element.38), channel_id=1, source_target_pairs={{1,2},{2,1},{5,6},{6,5},{9,10},{10,9},{13,14},{14,13},{17,18},{18,... | collective-permute-start | bytes 36872 | tf_op jit(solution)/shard_map/ppermute | solution.py:624

commit v4 on v3

--- a/solution.py
+++ b/solution.py
@@ -10,7 +10,7 @@
 STEPS = 2
 SUB = 8
 LIM = 48 * 1024 * 1024
-INSIDE, FINISH = 2, 2
+INSIDE, FINISH = 3, 3
 
 
 def with_halo(cells, sides, width):
@@ -521,7 +521,7 @@
 
 def step_one_kernel(
     g, total, ahead,
-    field_ref, part_ref, strips_ref, xev_ref, xod_ref, yev_ref, yod_ref, inner, extra_ref,
+    field_ref, part_ref, strips_ref, xev_ref, xod_ref, yod_ref, yev_ref, inner, extra_ref,
     mine_ref, other_ref, depth_ref, east_ref, grazers_ref, groups_ref, pref_ref, *rest,
 ):
     prey_refs, rest = rest[:-10], rest[-10:]
@@ -664,7 +664,7 @@
         mine, other = (gathered[:, i : i + SUB].reshape(-1, cols) for i in (0, SUB))
     field, strips, prey = call(
         functools.partial(load_kernel, g),
-        [cells, g.T * g.SR, g.tile],
+        [cells, g.T * g.SR, g.T * 2 * g.L + g.L + 3 * SUB],
         [flat, groups, preference],
         scalars=(1, 2),
         far_out=None,
@@ -679,6 +679,7 @@
         [field, strips, mine, other, column_depth, diff_east, diff_north],
     )
     messages = neighbours(*messages)
+    messages = messages[0], messages[1], messages[3], messages[2]
     part, inner = call(
         functools.partial(inside_kernel, g, INSIDE, True),
         [cells, g.inner.rows],

time: 31.2 us -> 29.9 us (0.958)
  starting transfers between devices: 18.9 us -> 16.7 us
  waiting for transfers between devices: 0.03 us -> 1.54 us
  Pallas kernels: 11.7 us -> 11 us
    ppermute x8, starting transfers between devices: 16.1 us -> 13.4 us  [pair_swap(): return lax.ppermute(values, axis, pairs)]
    ppermute x8, waiting for transfers between devices: 0.02 us -> 1.54 us  [pair_swap(): return lax.ppermute(values, axis, pairs)]
    pallas_call x6, Pallas kernels: 11.7 us -> 11 us  [call(): pl.pallas_call(body, out_shape=[jax.ShapeDtypeStruct((rows, 128), jnp.flo...]
    ppermute x3, starting transfers between devices: 2.84 us -> 3.25 us  [tracer_swap(): return lax.ppermute(values, 'tracer', [(0, 1), (1, 0)])]
  transfers between devices with their start and end apart: 11 -> 11, of which waited for: 0 -> 2; matrix products, arithmetic and copies ran while one was open for 0% -> 0% of each run, Pallas kernels for 21% -> 21%
where the time goes in v4:
time: 29.9 us; the launch traced here: 29.4 us
  starting transfers between devices  16.7 us (56%)
  Pallas kernels  11 us (37%)
  waiting for transfers between devices  1.54 us (5%)
    ppermute x8, starting transfers between devices, pair_swap(): return lax.ppermute(values, axis, pairs)  13.4 us
    pallas_call x6, Pallas kernels, call(): pl.pallas_call(body, out_shape=[jax.ShapeDtypeStruct((rows, 128), jnp.flo...  11 us
    ppermute x3, starting transfers between devices, tracer_swap(): return lax.ppermute(values, 'tracer', [(0, 1), (1, 0)])  3.25 us
    ppermute x8, waiting for transfers between devices, pair_swap(): return lax.ppermute(values, axis, pairs)  1.54 us
  transfers between devices with their start and end apart: 11, of which 2 were waited for; matrix products, arithmetic and copies ran while one was open for 0% of the time, Pallas kernels for 21%

profile of v4, /device:TPU:9, one launch (start us, length us, event | category | flops | bytes accessed | tf_op | source)
XLA Modules:
  0.0 29.4 jit_solution(15484886335696327025)
XLA Ops:
  0.0 0.0 copy-start.5
  0.0 0.0 copy-start.6
  0.0 1.2 %collective-permute-start = (f32[192,128]{1,0:T(8,128)}, f32[192,128]{1,0:T(8,128)S(1)}, u32[]{:S(2)}, u32[]{:S(2)}) collective-permute-start(f32[192,128]{1,0:T(8,128)} %bitcast.4), channel_id=1, source_target_pairs={{0,16},{16,0},{1,17},{17,1},{2,18},{18,2},{3,19},{19,3},{4,20},{20... | collective-permute-start | bytes 294920 | tf_op jit(solution)/shard_map/ppermute | solution.py:628
  1.2 0.0 copy-done.5
  1.2 0.0 copy-done.6
  1.2 0.0 copy-start
  1.3 0.0 copy-start.3
  1.3 0.0 copy-start.4
  1.3 2.5 %shard_map.82 = (f32[1536,128]{1,0:T(8,128)S(1)}, f32[192,128]{1,0:T(8,128)S(1)}, f32[424,128]{1,0:T(8,128)S(1)}) custom-call(f32[1536,128]{1,0:T(8,128)} %bitcast.10, s32[12]{0:T(128)S(1)} %copy-done.5, f32[16]{0:T(128)S(1)} %copy-done.6), custom_call_target="tpu_custom_call" | custom-call | tf_op jit(solution)/shard_map/pallas_call | solution.py:602
  3.8 0.0 copy-start.2
  3.8 0.7 %collective-permute-start.5 = (f32[424,128]{1,0:T(8,128)S(1)}, f32[424,128]{1,0:T(8,128)S(1)}, u32[]{:S(2)}, u32[]{:S(2)}) collective-permute-start(f32[424,128]{1,0:T(8,128)S(1)} %get-tuple-element.32.rest_0_), channel_id=1, source_target_pairs={{0,16},{16,0},{1,17},{17,1},{2,18},{18,2},{3,19},{19,3},{4,20},{20... | collective-permute-start | bytes 651272 | tf_op jit(solution)/shard_map/ppermute | solution.py:628
  4.5 0.0 collective-permute-done.refs_1_.other_ref
  4.6 0.0 copy-done
  4.6 0.0 copy-done.3
  4.6 0.0 copy-done.4
  4.6 0.0 copy-done.2
  4.6 0.3 shard_map.84
  4.8 1.0 %collective-permute-start.1 = (f32[416,128]{1,0:T(8,128)S(1)}, f32[416,128]{1,0:T(8,128)S(1)}, u32[]{:S(2)}, u32[]{:S(2)}) collective-permute-start(f32[416,128]{1,0:T(8,128)S(1)} %get-tuple-element.26), channel_id=1, source_target_pairs={{0,4},{4,0},{8,12},{12,8},{1,5},{5,1},{9,13},{13,9},{2,6},{6,2},{1... | collective-permute-start | bytes 638984 | tf_op jit(solution)/shard_map/ppermute | solution.py:624
  5.9 3.0 %collective-permute-start.2 = (f32[416,128]{1,0:T(8,128)S(1)}, f32[416,128]{1,0:T(8,128)S(1)}, u32[]{:S(2)}, u32[]{:S(2)}) collective-permute-start(f32[416,128]{1,0:T(8,128)S(1)} %get-tuple-element.27), channel_id=1, source_target_pairs={{4,8},{8,4},{5,9},{9,5},{6,10},{10,6},{7,11},{11,7},{20,24},{24,20... | collective-permute-start | bytes 638984 | tf_op jit(solution)/shard_map/ppermute | solution.py:624
  8.9 3.2 %collective-permute-start.3 = (f32[32,128]{1,0:T(8,128)S(1)}, f32[32,128]{1,0:T(8,128)S(1)}, u32[]{:S(2)}, u32[]{:S(2)}) collective-permute-start(f32[32,128]{1,0:T(8,128)S(1)} %get-tuple-element.28), channel_id=1, source_target_pairs={{1,2},{2,1},{5,6},{6,5},{9,10},{10,9},{13,14},{14,13},{17,18},{18,... | collective-permute-start | bytes 49160 | tf_op jit(solution)/shard_map/ppermute | solution.py:624
  12.1 0.0 copy-start.1
  12.1 0.1 collective-permute-start.4
  12.2 1.7 %shard_map.83 = (f32[1536,128]{1,0:T(8,128)S(1)}, f32[1336,128]{1,0:T(8,128)S(1)}) custom-call(f32[1536,128]{1,0:T(8,128)S(1)} %get-tuple-element.23.field_ref, f32[192,128]{1,0:T(8,128)S(1)} %bitcast.6, f32[192,128]{1,0:T(8,128)S(1)} %collective-permute-done.refs_1_.other_ref, s32[8,128]{1,0:T(8,128)S(1)} %copy-done.2, f32[8,128]{1,0:T(8,128)S(1)} %copy-done.3, ...), custom_call_target="tpu_custom_call" | custom-call | tf_op jit(solution)/shard_map/pallas_call | solution.py:602
  13.9 0.0 collective-permute-done.3.yod_ref
  13.9 0.8 %collective-permute-done.4.yev_ref = f32[32,128]{1,0:T(8,128)S(1)} collective-permute-done((f32[32,128]{1,0:T(8,128)S(1)}, f32[32,128]{1,0:T(8,128)S(1)}, u32[]{:S(2)}, u32[]{:S(2)}) %collective-permute-start.4) | collective-permute-done | bytes 16416 | tf_op jit(solution)/shard_map/ppermute | solution.py:624
  14.8 0.0 collective-permute-done.5.rest_1_
  14.8 0.0 collective-permute-done.1.xev_ref
  14.8 0.0 collective-permute-done.2.xod_ref
  14.8 0.0 copy-done.1
  14.8 2.3 %shard_map.85 = (f32[1536,128]{1,0:T(8,128)S(1)}, f32[384,128]{1,0:T(8,128)S(1)}, f32[384,128]{1,0:T(8,128)S(1)}, f32[24,128]{1,0:T(8,128)S(1)}, f32[24,128]{1,0...) custom-call(f32[1536,128]{1,0:T(8,128)S(1)} %get-tuple-element.23.field_ref, ...), custom_call_target="tpu_custom_call" | custom-call | tf_op jit(solution)/shard_map/pallas_call | solution.py:602
  17.1 0.1 collective-permute-start.6
  17.1 4.0 %collective-permute-start.7 = (f32[384,128]{1,0:T(8,128)S(1)}, f32[384,128]{1,0:T(8,128)S(1)}, u32[]{:S(2)}, u32[]{:S(2)}) collective-permute-start(f32[384,128]{1,0:T(8,128)S(1)} %get-tuple-element.36), channel_id=1, source_target_pairs={{4,8},{8,4},{5,9},{9,5},{6,10},{10,6},{7,11},{11,7},{20,24},{24,20... | collective-permute-start | bytes 589832 | tf_op jit(solution)/shard_map/ppermute | solution.py:624
  21.1 1.3 %collective-permute-start.10 = (f32[128,128]{1,0:T(8,128)S(1)}, f32[128,128]{1,0:T(8,128)S(1)}, u32[]{:S(2)}, u32[]{:S(2)}) collective-permute-start(f32[128,128]{1,0:T(8,128)S(1)} %get-tuple-element.40.rest_0_), channel_id=1, source_target_pairs={{0,16},{16,0},{1,17},{17,1},{2,18},{18,2},{3,19},{19,3},{4,20},{20... | collective-permute-start | bytes 196616 | tf_op jit(solution)/shard_map/ppermute | solution.py:628
  22.4 0.0 collective-permute-start.8
  22.4 2.1 %collective-permute-start.9 = (f32[24,128]{1,0:T(8,128)S(1)}, f32[24,128]{1,0:T(8,128)S(1)}, u32[]{:S(2)}, u32[]{:S(2)}) collective-permute-start(f32[24,128]{1,0:T(8,128)S(1)} %get-tuple-element.38), channel_id=1, source_target_pairs={{1,2},{2,1},{5,6},{6,5},{9,10},{10,9},{13,14},{14,13},{17,18},{18,... | collective-permute-start | bytes 36872 | tf_op jit(solution)/shard_map/ppermute | solution.py:624
  24.5 1.6 %shard_map.86.part_ref = f32[1536,128]{1,0:T(8,128)S(1)} custom-call(f32[1536,128]{1,0:T(8,128)S(1)} %get-tuple-element.33.field_ref, f32[1336,128]{1,0:T(8,128)S(1)} %get-tuple-element.30.inner.refs_0_), custom_call_target="tpu_custom_call" | custom-call | tf_op jit(solution)/shard_map/pallas_call | solution.py:602
  26.1 0.0 collective-permute-done.8.yev_ref
  26.2 0.7 %collective-permute-done.9.yod_ref = f32[24,128]{1,0:T(8,128)S(1)} collective-permute-done((f32[24,128]{1,0:T(8,128)S(1)}, f32[24,128]{1,0:T(8,128)S(1)}, u32[]{:S(2)}, u32[]{:S(2)}) %collective-permute-start.9) | collective-permute-done | bytes 12320 | tf_op jit(solution)/shard_map/ppermute | solution.py:624
  26.8 0.0 collective-permute-done.10.rest_1_
  26.9 0.0 collective-permute-done.6.xev_ref
  26.9 0.0 collective-permute-done.7.xod_ref
  26.9 2.6 %shard_map.87 = f32[1536,128]{1,0:T(8,128)} custom-call(f32[1536,128]{1,0:T(8,128)S(1)} %get-tuple-element.33.field_ref, f32[1536,128]{1,0:T(8,128)S(1)} %shard_map.86.part_ref, f32[192,128]{1,0:T(8,128)S(1)} %get-tuple-element.34.strips_ref, f32[384,128]{1,0:T(8,128)S(1)} %collective-permute-done.6.xev_ref, f32[384,128]{1,0:T(8,128)S(1)} %collective-permute-done.7.xod_ref, ...), custom_call_target="tpu_custom_call" | custom-call | tf_op jit(solution)/shard_map/pallas_call | solution.py:602
Async XLA Ops:
  0.0 1.2 %copy-start.5 = (s32[12]{0:T(128)S(1)}, s32[12]{0:T(128)}, u32[]{:S(2)}) copy-start(s32[12]{0:T(128)} %groups_ref.5) | copy-start | bytes 148
  0.0 1.2 %copy-start.6 = (f32[16]{0:T(128)S(1)}, f32[16]{0:T(128)}, u32[]{:S(2)}) copy-start(f32[16]{0:T(128)} %pref_ref.5) | copy-start | bytes 196
  0.0 4.5 %collective-permute-start = (f32[192,128]{1,0:T(8,128)}, f32[192,128]{1,0:T(8,128)S(1)}, u32[]{:S(2)}, u32[]{:S(2)}) collective-permute-start(f32[192,128]{1,0:T(8,128)} %bitcast.4), channel_id=1, source_target_pairs={{0,16},{16,0},{1,17},{17,1},{2,18},{18,2},{3,19},{19,3},{4,20},{20... | collective-permute-start | bytes 294920 | tf_op jit(solution)/shard_map/ppermute | solution.py:628
  1.2 3.3 %copy-start = (f32[3,8,8,128]{3,2,1,0:T(8,128)S(1)}, f32[3,8,8,128]{3,2,1,0:T(8,128)}, u32[]{:S(2)}) copy-start(f32[3,8,8,128]{3,2,1,0:T(8,128)} %param.9) | copy-start | bytes 294916
  1.3 3.3 %copy-start.3 = (f32[8,128]{1,0:T(8,128)S(1)}, f32[8,128]{1,0:T(8,128)}, u32[]{:S(2)}) copy-start(f32[8,128]{1,0:T(8,128)} %east_ref.3) | copy-start | bytes 12292
  1.3 3.3 %copy-start.4 = (f32[8,128]{1,0:T(8,128)S(1)}, f32[8,128]{1,0:T(8,128)}, u32[]{:S(2)}) copy-start(f32[8,128]{1,0:T(8,128)} %north_ref.1) | copy-start | bytes 12292
  3.8 0.7 %copy-start.2 = (s32[8,128]{1,0:T(8,128)S(1)}, s32[8,128]{1,0:T(8,128)}, u32[]{:S(2)}) copy-start(s32[8,128]{1,0:T(8,128)} %depth_ref.3) | copy-start | bytes 12292
  3.8 10.9 %collective-permute-start.5 = (f32[424,128]{1,0:T(8,128)S(1)}, f32[424,128]{1,0:T(8,128)S(1)}, u32[]{:S(2)}, u32[]{:S(2)}) collective-permute-start(f32[424,128]{1,0:T(8,128)S(1)} %get-tuple-element.32.rest_0_), channel_id=1, source_target_pairs={{0,16},{16,0},{1,17},{17,1},{2,18},{18,2},{3,19},{19,3},{4,20},{20... | collective-permute-start | bytes 651272 | tf_op jit(solution)/shard_map/ppermute | solution.py:628
  4.8 9.9 %collective-permute-start.1 = (f32[416,128]{1,0:T(8,128)S(1)}, f32[416,128]{1,0:T(8,128)S(1)}, u32[]{:S(2)}, u32[]{:S(2)}) collective-permute-start(f32[416,128]{1,0:T(8,128)S(1)} %get-tuple-element.26), channel_id=1, source_target_pairs={{0,4},{4,0},{8,12},{12,8},{1,5},{5,1},{9,13},{13,9},{2,6},{6,2},{1... | collective-permute-start | bytes 638984 | tf_op jit(solution)/shard_map/ppermute | solution.py:624
  5.9 8.9 %collective-permute-start.2 = (f32[416,128]{1,0:T(8,128)S(1)}, f32[416,128]{1,0:T(8,128)S(1)}, u32[]{:S(2)}, u32[]{:S(2)}) collective-permute-start(f32[416,128]{1,0:T(8,128)S(1)} %get-tuple-element.27), channel_id=1, source_target_pairs={{4,8},{8,4},{5,9},{9,5},{6,10},{10,6},{7,11},{11,7},{20,24},{24,20... | collective-permute-start | bytes 638984 | tf_op jit(solution)/shard_map/ppermute | solution.py:624
  8.9 5.0 %collective-permute-start.3 = (f32[32,128]{1,0:T(8,128)S(1)}, f32[32,128]{1,0:T(8,128)S(1)}, u32[]{:S(2)}, u32[]{:S(2)}) collective-permute-start(f32[32,128]{1,0:T(8,128)S(1)} %get-tuple-element.28), channel_id=1, source_target_pairs={{1,2},{2,1},{5,6},{6,5},{9,10},{10,9},{13,14},{14,13},{17,18},{18,... | collective-permute-start | bytes 49160 | tf_op jit(solution)/shard_map/ppermute | solution.py:624
  12.1 2.7 %copy-start.1 = (f32[16,8,128]{2,1,0:T(8,128)S(1)}, f32[16,8,128]{2,1,0:T(8,128)}, u32[]{:S(2)}) copy-start(f32[16,8,128]{2,1,0:T(8,128)} %param.13) | copy-start | bytes 196612
  12.1 2.7 %collective-permute-start.4 = (f32[32,128]{1,0:T(8,128)S(1)}, f32[32,128]{1,0:T(8,128)S(1)}, u32[]{:S(2)}, u32[]{:S(2)}) collective-permute-start(f32[32,128]{1,0:T(8,128)S(1)} %get-tuple-element.29), channel_id=1, source_target_pairs={{0,1},{1,0},{2,3},{3,2},{4,5},{5,4},{6,7},{7,6},{8,9},{9,8},{10,11... | collective-permute-start | bytes 49160 | tf_op jit(solution)/shard_map/ppermute | solution.py:624
  17.1 9.8 %collective-permute-start.6 = (f32[384,128]{1,0:T(8,128)S(1)}, f32[384,128]{1,0:T(8,128)S(1)}, u32[]{:S(2)}, u32[]{:S(2)}) collective-permute-start(f32[384,128]{1,0:T(8,128)S(1)} %get-tuple-element.35), channel_id=1, source_target_pairs={{0,4},{4,0},{8,12},{12,8},{1,5},{5,1},{9,13},{13,9},{2,6},{6,2},{1... | collective-permute-start | bytes 589832 | tf_op jit(solution)/shard_map/ppermute | solution.py:624
  17.1 9.7 %collective-permute-start.7 = (f32[384,128]{1,0:T(8,128)S(1)}, f32[384,128]{1,0:T(8,128)S(1)}, u32[]{:S(2)}, u32[]{:S(2)}) collective-permute-start(f32[384,128]{1,0:T(8,128)S(1)} %get-tuple-element.36), channel_id=1, source_target_pairs={{4,8},{8,4},{5,9},{9,5},{6,10},{10,6},{7,11},{11,7},{20,24},{24,20... | collective-permute-start | bytes 589832 | tf_op jit(solution)/shard_map/ppermute | solution.py:624
  21.1 5.7 %collective-permute-start.10 = (f32[128,128]{1,0:T(8,128)S(1)}, f32[128,128]{1,0:T(8,128)S(1)}, u32[]{:S(2)}, u32[]{:S(2)}) collective-permute-start(f32[128,128]{1,0:T(8,128)S(1)} %get-tuple-element.40.rest_0_), channel_id=1, source_target_pairs={{0,16},{16,0},{1,17},{17,1},{2,18},{18,2},{3,19},{19,3},{4,20},{20... | collective-permute-start | bytes 196616 | tf_op jit(solution)/shard_map/ppermute | solution.py:628
  22.4 3.7 %collective-permute-start.8 = (f32[24,128]{1,0:T(8,128)S(1)}, f32[24,128]{1,0:T(8,128)S(1)}, u32[]{:S(2)}, u32[]{:S(2)}) collective-permute-start(f32[24,128]{1,0:T(8,128)S(1)} %get-tuple-element.37), channel_id=1, source_target_pairs={{0,1},{1,0},{2,3},{3,2},{4,5},{5,4},{6,7},{7,6},{8,9},{9,8},{10,11... | collective-permute-start | bytes 36872 | tf_op jit(solution)/shard_map/ppermute | solution.py:624
  22.4 4.4 %collective-permute-start.9 = (f32[24,128]{1,0:T(8,128)S(1)}, f32[24,128]{1,0:T(8,128)S(1)}, u32[]{:S(2)}, u32[]{:S(2)}) collective-permute-start(f32[24,128]{1,0:T(8,128)S(1)} %get-tuple-element.38), channel_id=1, source_target_pairs={{1,2},{2,1},{5,6},{6,5},{9,10},{10,9},{13,14},{14,13},{17,18},{18,... | collective-permute-start | bytes 36872 | tf_op jit(solution)/shard_map/ppermute | solution.py:624

commit v5 on v4

--- a/solution.py
+++ b/solution.py
@@ -126,8 +126,10 @@
             hz=self.K, pz=self.K, mz=self.K,
         )
         self.outer = Table(
-            hx=4 * self.LH, px=2 * self.LH, mx=2 * self.LH, kx=1,
-            hs=self.NV, ps=self.NV, ms=self.NV, ks=self.NV,
+            hx=4 * self.LH, px=2 * self.LH, mx=2 * self.LH, kx=1
+        )
+        self.ends = Table(
+            hs=4 * self.NV, ps=2 * self.NV, ms=2 * self.NV, ks=2 * self.NV
         )
 
 
@@ -222,8 +224,8 @@
     return [spread(rows, r) for r in range(g.R) for _ in range(g.LH)]
 
 
-def taste_of(groups_ref, pref_ref, t):
-    return pref_ref[groups_ref[t]]
+def taste_of(taste_ref, t):
+    return taste_ref[rows8(t), :]
 
 
 def is_even(axis):
@@ -265,19 +267,31 @@
 
 
 def load_kernel(
-    g, tracers_ref, groups_ref, pref_ref, field_ref, strips_ref, prey_ref, landed, sems
+    g, tracers_ref, groups_far, pref_far, field_ref, strips_ref, prey_ref, taste_ref,
+    landed, sems, groups_ref, pref_ref, small_sems,
 ):
     def arrival(t):
         at = pl.ds(pl.multiple_of(t * g.tile, g.tile), g.tile)
         return pltpu.make_async_copy(tracers_ref.at[at, :], landed.at[at, :], sems.at[t])
 
+    small = [
+        pltpu.make_async_copy(a, b, small_sems.at[i])
+        for i, (a, b) in enumerate(((groups_far, groups_ref), (pref_far, pref_ref)))
+    ]
+    for copy in small:
+        copy.start()
     for t in range(g.T):
         arrival(t).start()
     prey_ref[...] = jnp.zeros_like(prey_ref)
 
+    for copy in small:
+        copy.wait()
+    for t in range(g.T):
+        taste_ref[rows8(t), :] = jnp.full((SUB, 128), pref_ref[groups_ref[t]], jnp.float32)
+
     def one(t):
         arrival(t).wait()
-        taste = taste_of(groups_ref, pref_ref, t)
+        taste = taste_of(taste_ref, t)
         base = pl.multiple_of(t * g.tile, g.tile)
         parts = []
         for r in range(g.R):
@@ -356,8 +370,8 @@
             tab.set_flux(cf, "z", k, opened, above)
 
 
-def outer_coefficients(g, cf, extra_x, extra_y, flux, extra_ref, depth, east):
-    tab, lane = g.outer, lanes()
+def outer_coefficients(g, cf, extra_x, flux, depth, east):
+    tab = g.outer
     depth_low, depth_high = extra_x(g.LH)
     depths = [spread(depth_low, 0), spread(depth_low, 1), spread(depth, 0), spread(depth, g.R - 1)]
     depths += [spread(depth_high, 0), spread(depth_high, 1)]
@@ -368,18 +382,26 @@
             tab.set_open(cf, "x", face * g.LH + lh, wet[row][lh] & wet[row + 1][lh])
         tab.set_flux(cf, "x", lh, wet[1][lh] & wet[2][lh], extra_x(lh)[0])
         tab.set_flux(cf, "x", g.LH + lh, wet[3][lh] & wet[4][lh], flux(0, g.R - 1, lh))
-    place, half = lane % WIDE, (lane // WIDE) % g.LH
+
+
+def strip_coefficients(g, cf, extra_y, extra_ref):
+    tab, lane = g.ends, lanes()
+    half = (lane // WIDE) % g.LH
+    level = (sublanes() + SUB * half).astype(jnp.float32)
     for i in range(g.NV):
         full = []
         for which in range(3):
             own = which * g.NV + i
             slot = g.T * g.NV + own
             full.append(full_strips(extra_ref[rows8(own), :], *extra_y(slot // EACH), slot % EACH))
-        wet_s = jnp.where((sublanes() + SUB * half).astype(jnp.float32) < full[0], 1.0, 0.0)
-        opened = (wet_s * roll(wet_s, 1, 1) > 0.0) & (place != 0) & (place != 8)
-        tab.set_open(cf, "s", i, opened)
-        tab.set_flux(cf, "s", i, opened, roll(full[1], 1, 1))
-        tab.set(cf, "ks", i, 2.0 * roll(full[2], 1, 1))
+        wet = [level < roll(full[0], -away, 1) for away in (-2, -1, 0, 1, 2)]
+        opened = [a & b for a, b in zip(wet, wet[1:])]
+        for face in range(4):
+            tab.set_open(cf, "s", face * g.NV + i, opened[face])
+        for face in range(2):
+            flux, kappa = (roll(v, 1 - face, 1) for v in full[1:])
+            tab.set_flux(cf, "s", face * g.NV + i, opened[1 + face], flux)
+            tab.set(cf, "ks", face * g.NV + i, 2.0 * kappa)
 
 
 def end_lanes():
@@ -395,7 +417,7 @@
             east_ref[...], north_ref[...],
         )
     else:
-        cf, part_ref = refs
+        tend_ref, cf, whole_ref, part_ref = refs
     sub = sublanes()
     ends, top, bottom = end_lanes(), sub == 0, sub == SUB - 1
 
@@ -418,6 +440,10 @@
             index = [r * g.LH + lh for lh in range(g.LH)]
             at = [pl.ds(base + k * SUB, SUB) for k in index]
             cells = [field_ref[a, :] for a in at]
+            if not first:
+                cells = [c + end_columns(g, tend_ref, t, k) for k, c in zip(index, cells)]
+                for a, c in zip(at, cells):
+                    whole_ref[a, :] = c
             news = []
             for k, c in zip(index, cells):
                 j = coef("hy", k) * (c - roll(c, 1, 1))
@@ -439,20 +465,33 @@
 
 
 def strip_tendency(g, cf, full, i):
-    def coef(name):
-        return g.outer.get(cf, name, i)
-
-    j = coef("hs") * (full - roll(full, 1, 1))
-    s = limited(j, roll(j, -1, 1))
-    flow = coef("ps") * roll(full + s, 1, 1) + coef("ms") * (full - s) - coef("ks") * j
-    tend = flow - roll(flow, -1, 1)
-    return jnp.where(lanes() % WIDE < 12, tend, roll(tend, 10, 1))
+    def coef(name, face):
+        return g.ends.get(cf, name, face * g.NV + i)
+
+    cell = [roll(full, -away, 1) for away in (-2, -1, 0, 1, 2)]
+    j = [coef("hs", face) * (cell[face + 1] - cell[face]) for face in range(4)]
+    s = [limited(a, b) for a, b in zip(j, j[1:])]
+    flow = [
+        coef("ps", f) * (cell[f + 1] + s[f])
+        + coef("ms", f) * (cell[f + 2] - s[f + 1])
+        - coef("ks", f) * j[f + 1]
+        for f in range(2)
+    ]
+    tend = flow[0] - flow[1]
+    place = lanes() % WIDE
+    tend = jnp.where(place < 12, tend, roll(tend, 10, 1))
+    return jnp.where((place >= 10) & (place < 14), tend, 0.0)
 
 
 def all_strip_tendencies(g, cf, strips_ref, sides, tend_ref):
     for n in range(g.T * g.NV):
         full = full_strips(strips_ref[rows8(n), :], *sides(n // EACH), n % EACH)
         tend_ref[rows8(n), :] = strip_tendency(g, cf, full, n % g.NV)
+
+
+def end_columns(g, tend_ref, t, k):
+    v, n = divmod(k, EACH)
+    return jnp.where(end_lanes(), roll(tend_ref[rows8(t * g.NV + v), :], -(WIDE * n + 12), 1), 0.0)
 
 
 def set_factor(g, total, factor, grazers_ref, prey_refs):
@@ -464,9 +503,8 @@
             factor[at, :] = grazers / (1.0 + 4.0 * prey / total)
 
 
-def finish(g, inner, outer, t, field_ref, part_ref, tend_ref, sides, taste, factor, emit):
+def finish(g, inner, outer, t, field_ref, part_ref, sides, taste, factor, emit):
     base = pl.multiple_of(t * g.tile, g.tile)
-    ends = end_lanes()
 
     def cell(r, lh):
         if 0 <= r < g.R:
@@ -482,9 +520,7 @@
         return g.outer.get(outer, name, (g.LH if f else 0) + lh)
 
     state = [None] * g.LH
-    tends = [tend_ref[rows8(t * g.NV + i), :] for i in range(g.NV)]
     for f in range(-1, g.R + 2):
-        kappa = g.inner.get(inner, "kx", f) if f > 0 else g.outer.get(outer, "kx", 0)
         for lh in range(g.LH):
             if f < 0:
                 below = cell(-2, lh)
@@ -501,10 +537,8 @@
                 if f > 1:
                     r = f - 2
                     k = r * g.LH + lh
-                    v, n = divmod(k, EACH)
                     old = cell(r, lh)
                     new = part_ref[pl.ds(base + k * SUB, SUB), :] + (carried - flow)
-                    new = new + jnp.where(ends, roll(tends[v], -(WIDE * n + 12), 1), 0.0)
                     new = new - (taste * factor[rows8(k), :]) * old
                     emit(r, lh, new)
                 carried = flow
@@ -519,74 +553,108 @@
     return sides
 
 
-def step_one_kernel(
+def border_kernel(
     g, total, ahead,
-    field_ref, part_ref, strips_ref, xev_ref, xod_ref, yod_ref, yev_ref, inner, extra_ref,
-    mine_ref, other_ref, depth_ref, east_ref, grazers_ref, groups_ref, pref_ref, *rest,
+    field_ref, part_ref, xev_ref, xod_ref, inner, mine_ref, other_ref, depth_ref, east_ref,
+    grazers_ref, taste_ref, *rest,
 ):
-    prey_refs, rest = rest[:-10], rest[-10:]
-    (out_ref, xev2_ref, xod2_ref, yev2_ref, yod2_ref, strips2_ref, prey2_ref, outer,
-     factor, tend_ref) = rest
-    x_even, y_even = is_even("gx"), is_even("gy")
-    x_sides, y_sides = reader(x_even, xev_ref, xod_ref), reader(y_even, yev_ref, yod_ref)
+    prey_refs, (out_ref, strips_ref, prey_ref, outer, factor) = rest[:-5], rest[-5:]
+    x_sides = reader(is_even("gx"), xev_ref, xod_ref)
     outer_coefficients(
-        g, outer, lambda i: x_sides(g.T * 2 * g.LH + i), y_sides,
-        flux_reader(g, mine_ref, other_ref), extra_ref,
+        g, outer, lambda i: x_sides(g.T * 2 * g.LH + i), flux_reader(g, mine_ref, other_ref),
         depth_ref[...].astype(jnp.float32), east_ref[...],
     )
     set_factor(g, total, factor, grazers_ref, prey_refs)
-    all_strip_tendencies(g, outer, strips_ref, y_sides, tend_ref)
-    prey2_ref[...] = jnp.zeros_like(prey2_ref)
+    prey_ref[...] = jnp.zeros_like(prey_ref)
 
     def one(t):
-        taste = taste_of(groups_ref, pref_ref, t)
+        taste = taste_of(taste_ref, t)
         base = pl.multiple_of(t * g.tile, g.tile)
         news = {}
 
         def emit(r, lh, new):
             at = (r * g.LH + lh) * SUB
             out_ref[pl.ds(base + at, SUB), :] = new
-            prey2_ref[at : at + SUB, :] += taste * new
+            prey_ref[at : at + SUB, :] += taste * new
             news[r, lh] = new
 
-        finish(g, inner, outer, t, field_ref, part_ref, tend_ref, x_sides, taste, factor, emit)
-        for i in range(2):
-            for lh in range(g.LH):
-                at = rows8(t * 2 * g.LH + i * g.LH + lh)
-                low, high = news[i, lh], news[g.R - 2 + i, lh]
-                xev2_ref[at, :] = jnp.where(x_even, high, low)
-                xod2_ref[at, :] = jnp.where(x_even, low, high)
+        finish(g, inner, outer, t, field_ref, part_ref, x_sides, taste, factor, emit)
         parts = [news[r, lh] for r in range(g.R) for lh in range(g.LH)]
         for i, packed in enumerate(pack_strips(parts)):
-            strips2_ref[rows8(t * g.NV + i), :] = packed
+            strips_ref[rows8(t * g.NV + i), :] = packed
 
     each_tracer(g, ahead, one)
-    put_messages(registers(strips2_ref), y_even, yev2_ref, yod2_ref)
-
-
-def step_two_kernel(
+
+
+def second_messages_kernel(
+    g, field_ref, strips_ref, next_ref, prey_ref, extra_ref, yod_ref, yev_ref, taste_ref,
+    xev2_ref, xod2_ref, yev2_ref, yod2_ref, strips2_ref, prey2_ref, tend_ref, ends, grazed,
+):
+    x_even, y_even = is_even("gx"), is_even("gy")
+    y_sides = reader(y_even, yev_ref, yod_ref)
+    strip_coefficients(g, ends, y_sides, extra_ref)
+    all_strip_tendencies(g, ends, strips_ref, y_sides, tend_ref)
+    packed = [next_ref[rows8(n), :] + tend_ref[rows8(n), :] for n in range(g.T * g.NV)]
+    for n, one_packed in enumerate(packed):
+        strips2_ref[rows8(n), :] = one_packed
+    put_messages(packed, y_even, yev2_ref, yod2_ref)
+    for i in range(g.NV):
+        grazed[rows8(i), :] = sum(
+            taste_of(taste_ref, t) * tend_ref[rows8(t * g.NV + i), :] for t in range(g.T)
+        )
+    for k in range(g.K):
+        prey2_ref[rows8(k), :] = prey_ref[rows8(k), :] + end_columns(g, grazed, 0, k)
+
+    def one(t):
+        for i in range(2 * g.LH):
+            j = i + (g.R - 2) * g.LH
+            low, high = (
+                field_ref[rows8(t * g.K + k), :] + end_columns(g, tend_ref, t, k) for k in (i, j)
+            )
+            at = rows8(t * 2 * g.LH + i)
+            xev2_ref[at, :] = jnp.where(x_even, high, low)
+            xod2_ref[at, :] = jnp.where(x_even, low, high)
+
+    each_tracer(g, 4, one)
+
+
+def border_two_kernel(
     g, total, ahead,
-    field_ref, part_ref, strips_ref, xev_ref, xod_ref, yev_ref, yod_ref, inner, outer,
-    grazers_ref, groups_ref, pref_ref, *rest,
+    field_ref, part_ref, xev_ref, xod_ref, inner, outer, grazers_ref, taste_ref, *rest,
 ):
-    prey_refs, (out_ref, factor, tend_ref, leaving, sems) = rest[:-5], rest[-5:]
+    prey_refs, (out_ref, factor) = rest[:-2], rest[-2:]
     x_sides = reader(is_even("gx"), xev_ref, xod_ref)
+    set_factor(g, total, factor, grazers_ref, prey_refs)
+
+    def one(t):
+        base = pl.multiple_of(t * g.tile, g.tile)
+
+        def emit(r, lh, new):
+            out_ref[pl.ds(base + (r * g.LH + lh) * SUB, SUB), :] = new
+
+        taste = taste_of(taste_ref, t)
+        finish(g, inner, outer, t, field_ref, part_ref, x_sides, taste, factor, emit)
+
+    each_tracer(g, ahead, one)
+
+
+def result_kernel(
+    g, ahead, field_ref, strips_ref, yev_ref, yod_ref, ends, out_ref, tend_ref, leaving, sems
+):
     y_sides = reader(is_even("gy"), yev_ref, yod_ref)
-    set_factor(g, total, factor, grazers_ref, prey_refs)
-    all_strip_tendencies(g, outer, strips_ref, y_sides, tend_ref)
+    all_strip_tendencies(g, ends, strips_ref, y_sides, tend_ref)
 
     def departure(t):
         at = pl.ds(pl.multiple_of(t * g.tile, g.tile), g.tile)
         return pltpu.make_async_copy(leaving.at[at, :], out_ref.at[at, :], sems.at[t])
 
     def one(t):
-        taste = taste_of(groups_ref, pref_ref, t)
         base = pl.multiple_of(t * g.tile, g.tile)
-
-        def emit(r, lh, new):
-            leaving[pl.ds(base + lh * SUB * g.R + r, SUB, stride=g.R), :] = new
-
-        finish(g, inner, outer, t, field_ref, part_ref, tend_ref, x_sides, taste, factor, emit)
+        for r in range(g.R):
+            for lh in range(g.LH):
+                k = r * g.LH + lh
+                new = field_ref[rows8(t * g.K + k), :] + end_columns(g, tend_ref, t, k)
+                leaving[pl.ds(base + lh * SUB * g.R + r, SUB, stride=g.R), :] = new
         departure(t).start()
 
     each_tracer(g, ahead, one)
@@ -594,11 +662,12 @@
         departure(t).wait()
 
 
-def call(body, outs, operands, scalars=(), far_out=False, scratch=(), cost=0):
-    spaces = [pltpu.SMEM if i in scalars else pltpu.VMEM for i in range(len(operands))]
-    if far_out is None:
-        spaces[0] = pltpu.HBM
-        operands = [pltpu.with_memory_space_constraint(operands[0], pltpu.HBM), *operands[1:]]
+def call(body, outs, operands, far=0, far_out=False, scratch=()):
+    spaces = [pltpu.HBM if i < far else pltpu.VMEM for i in range(len(operands))]
+    operands = [
+        pltpu.with_memory_space_constraint(a, space) if space == pltpu.HBM else a
+        for a, space in zip(operands, spaces)
+    ]
     return pl.pallas_call(
         body,
         out_shape=[jax.ShapeDtypeStruct((rows, 128), jnp.float32) for rows in outs],
@@ -609,9 +678,6 @@
             for rows in scratch
         ],
         compiler_params=pltpu.CompilerParams(vmem_limit_bytes=LIM),
-        cost_estimate=pl.CostEstimate(flops=cost, bytes_accessed=0, transcendentals=0)
-        if cost
-        else None,
     )(*operands)
 
 
@@ -662,13 +728,13 @@
     else:
         gathered = lax.all_gather(fluxes, "tracer", axis=1, tiled=True)
         mine, other = (gathered[:, i : i + SUB].reshape(-1, cols) for i in (0, SUB))
-    field, strips, prey = call(
+    field, strips, prey, taste = call(
         functools.partial(load_kernel, g),
-        [cells, g.T * g.SR, g.T * 2 * g.L + g.L + 3 * SUB],
+        [cells, g.T * g.SR, g.T * 2 * g.L + g.L + 3 * SUB, g.T * SUB],
         [flat, groups, preference],
-        scalars=(1, 2),
-        far_out=None,
-        scratch=[cells, copies],
+        far=3,
+        scratch=[cells, copies, pltpu.SMEM(groups.shape, groups.dtype),
+                 pltpu.SMEM(preference.shape, preference.dtype), pltpu.SemaphoreType.DMA((2,))],
     )
     prey = all_prey(prey)
     x_rows = g.T * 2 * g.L
@@ -685,25 +751,36 @@
         [cells, g.inner.rows],
         [field, mine, other, column_depth, diff_east, diff_north],
     )
-    *results, outer = call(
-        functools.partial(step_one_kernel, g, total, FINISH),
-        [cells, x_rows, x_rows, g.my2 * SUB, g.my2 * SUB, g.T * g.SR, g.tile, g.outer.rows],
-        [field, part, strips, *messages, inner, extra, mine, other, column_depth, diff_east,
-         grazers, groups, preference, *prey],
-        scalars=(14, 15),
-        scratch=[g.tile, g.T * g.SR],
-    )
-    field, *messages, strips, prey = results
+    field, next_strips, next_prey, outer = call(
+        functools.partial(border_kernel, g, total, FINISH),
+        [cells, g.T * g.SR, g.tile, g.outer.rows],
+        [field, part, *messages[:2], inner, mine, other, column_depth, diff_east, grazers, taste,
+         *prey],
+        scratch=[g.tile],
+    )
+    *messages, strips, prey, tend, ends = call(
+        functools.partial(second_messages_kernel, g),
+        [x_rows, x_rows, g.my2 * SUB, g.my2 * SUB, g.T * g.SR, g.tile, g.T * g.SR, g.ends.rows],
+        [field, strips, next_strips, next_prey, extra, *messages[2:], taste],
+        scratch=[g.SR],
+    )
     prey = all_prey(prey)
     messages = neighbours(*messages)
-    (part,) = call(functools.partial(inside_kernel, g, INSIDE, False), [cells], [field, inner])
+    field, part = call(
+        functools.partial(inside_kernel, g, INSIDE, False), [cells, cells], [field, tend, inner]
+    )
+    (field,) = call(
+        functools.partial(border_two_kernel, g, total, FINISH),
+        [cells],
+        [field, part, *messages[:2], inner, outer, grazers, taste, *prey],
+        scratch=[g.tile],
+    )
     (out,) = call(
-        functools.partial(step_two_kernel, g, total, FINISH),
+        functools.partial(result_kernel, g, FINISH),
         [cells],
-        [field, part, strips, *messages, inner, outer, grazers, groups, preference, *prey],
-        scalars=(10, 11),
+        [field, strips, *messages[2:], ends],
         far_out=True,
-        scratch=[g.tile, g.T * g.SR, cells, copies],
+        scratch=[g.T * g.SR, cells, copies],
     )
     return out.reshape(tracers.shape)
 

time: 29.9 us -> 28.9 us (0.967)
  waiting for transfers between devices: 1.54 us -> 0.08 us
  starting transfers between devices: 16.7 us -> 17.5 us
  Pallas kernels: 11 us -> 10.4 us
  local copies, waits for them, and re-layouts: 0.03 us -> 0.34 us
    ppermute x8, waiting for transfers between devices: 1.54 us -> 0.02 us  [pair_swap(): return lax.ppermute(values, axis, pairs)]
    ppermute x8, starting transfers between devices: 13.4 us -> 14.6 us  [pair_swap(): return lax.ppermute(values, axis, pairs)]
    pallas_call x6 -> x8, Pallas kernels: 11 us -> 10.4 us  [call(): pl.pallas_call(body, out_shape=[jax.ShapeDtypeStruct((rows, 128), jnp.flo...]
    ppermute x3, starting transfers between devices: 3.25 us -> 2.85 us  [tracer_swap(): return lax.ppermute(values, 'tracer', [(0, 1), (1, 0)])]
    unnamed x14 -> x10, local copies, waits for them, and re-layouts: 0.03 us -> 0.34 us
  transfers between devices with their start and end apart: 11 -> 11, of which waited for: 2 -> 1; matrix products, arithmetic and copies ran while one was open for 0% -> 0% of each run, Pallas kernels for 21% -> 26%
where the time goes in v5:
time: 28.9 us; the launch traced here: 28.5 us
  starting transfers between devices  17.5 us (61%)
  Pallas kernels  10.4 us (36%)
  local copies, waits for them, and re-layouts  0.34 us (1%)
    ppermute x8, starting transfers between devices, pair_swap(): return lax.ppermute(values, axis, pairs)  14.6 us
    pallas_call x8, Pallas kernels, call(): pl.pallas_call(body, out_shape=[jax.ShapeDtypeStruct((rows, 128), jnp.flo...  10.4 us
    ppermute x3, starting transfers between devices, tracer_swap(): return lax.ppermute(values, 'tracer', [(0, 1), (1, 0)])  2.85 us
  transfers between devices with their start and end apart: 11, of which 1 were waited for; matrix products, arithmetic and copies ran while one was open for 0% of the time, Pallas kernels for 26%

profile of v5, /device:TPU:9, one launch (start us, length us, event | category | flops | bytes accessed | tf_op | source)
XLA Modules:
  0.0 28.5 jit_solution(6921033059477931305)
XLA Ops:
  0.0 1.2 %collective-permute-start = (f32[192,128]{1,0:T(8,128)}, f32[192,128]{1,0:T(8,128)S(1)}, u32[]{:S(2)}, u32[]{:S(2)}) collective-permute-start(f32[192,128]{1,0:T(8,128)} %bitcast.4), channel_id=1, source_target_pairs={{0,16},{16,0},{1,17},{17,1},{2,18},{18,2},{3,19},{19,3},{4,20},{20... | collective-permute-start | bytes 294920 | tf_op jit(solution)/shard_map/ppermute | solution.py:694
  1.2 0.0 copy-start
  1.2 0.0 copy-start.3
  1.2 0.0 copy-start.4
  1.2 2.1 %shard_map.82 = (f32[1536,128]{1,0:T(8,128)S(1)}, f32[192,128]{1,0:T(8,128)S(1)}, f32[424,128]{1,0:T(8,128)S(1)}, f32[96,128]{1,0:T(8,128)S(1)}) custom-call(f32[1536,128]{1,0:T(8,128)} %bitcast.10, s32[12]{0:T(128)} %groups_far.1, f32[16]{0:T(128)} %pref_far.1), custom_call_target="tpu_custom_call" | custom-call | tf_op jit(solution)/shard_map/pallas_call | solution.py:671
  3.3 0.0 copy-start.2
  3.3 0.3 %collective-permute-start.3 = (f32[424,128]{1,0:T(8,128)S(1)}, f32[424,128]{1,0:T(8,128)S(1)}, u32[]{:S(2)}, u32[]{:S(2)}) collective-permute-start(f32[424,128]{1,0:T(8,128)S(1)} %get-tuple-element.37.rest_0_), channel_id=1, source_target_pairs={{0,16},{16,0},{1,17},{17,1},{2,18},{18,2},{3,19},{19,3},{4,20},{20... | collective-permute-start | bytes 651272 | tf_op jit(solution)/shard_map/ppermute | solution.py:694
  3.6 0.1 collective-permute-done.refs_1_.other_ref
  3.7 0.0 copy-done
  3.7 0.0 copy-done.3
  3.7 0.0 copy-done.4
  3.7 0.3 %copy-done.2 = s32[8,128]{1,0:T(8,128)S(1)} copy-done((s32[8,128]{1,0:T(8,128)S(1)}, s32[8,128]{1,0:T(8,128)}, u32[]{:S(2)}) %copy-start.2) | copy-done | bytes 4120
  4.0 0.2 shard_map.84
  4.2 1.6 %collective-permute-start.1 = (f32[416,128]{1,0:T(8,128)S(1)}, f32[416,128]{1,0:T(8,128)S(1)}, u32[]{:S(2)}, u32[]{:S(2)}) collective-permute-start(f32[416,128]{1,0:T(8,128)S(1)} %get-tuple-element.33), channel_id=1, source_target_pairs={{0,4},{4,0},{8,12},{12,8},{1,5},{5,1},{9,13},{13,9},{2,6},{6,2},{1... | collective-permute-start | bytes 638984 | tf_op jit(solution)/shard_map/ppermute | solution.py:690
  5.9 3.0 %collective-permute-start.2 = (f32[416,128]{1,0:T(8,128)S(1)}, f32[416,128]{1,0:T(8,128)S(1)}, u32[]{:S(2)}, u32[]{:S(2)}) collective-permute-start(f32[416,128]{1,0:T(8,128)S(1)} %get-tuple-element.34), channel_id=1, source_target_pairs={{4,8},{8,4},{5,9},{9,5},{6,10},{10,6},{7,11},{11,7},{20,24},{24,20... | collective-permute-start | bytes 638984 | tf_op jit(solution)/shard_map/ppermute | solution.py:690
  8.9 3.2 %collective-permute-start.4 = (f32[32,128]{1,0:T(8,128)S(1)}, f32[32,128]{1,0:T(8,128)S(1)}, u32[]{:S(2)}, u32[]{:S(2)}) collective-permute-start(f32[32,128]{1,0:T(8,128)S(1)} %get-tuple-element.42), channel_id=1, source_target_pairs={{1,2},{2,1},{5,6},{6,5},{9,10},{10,9},{13,14},{14,13},{17,18},{18,... | collective-permute-start | bytes 49160 | tf_op jit(solution)/shard_map/ppermute | solution.py:690
  12.1 0.0 copy-start.1
  12.1 0.1 collective-permute-start.5
  12.2 1.7 %shard_map.83 = (f32[1536,128]{1,0:T(8,128)S(1)}, f32[1336,128]{1,0:T(8,128)S(1)}) custom-call(f32[1536,128]{1,0:T(8,128)S(1)} %get-tuple-element.30.field_ref, f32[192,128]{1,0:T(8,128)S(1)} %bitcast.6, f32[192,128]{1,0:T(8,128)S(1)} %collective-permute-done.refs_1_.other_ref, s32[8,128]{1,0:T(8,128)S(1)} %copy-done.2, f32[8,128]{1,0:T(8,128)S(1)} %copy-done.3, ...), custom_call_target="tpu_custom_call" | custom-call | tf_op jit(solution)/shard_map/pallas_call | solution.py:671
  13.8 0.0 collective-permute-done.3.rest_1_
  13.9 0.0 collective-permute-done.1.xev_ref
  13.9 0.0 collective-permute-done.2.xod_ref
  13.9 0.0 copy-done.1
  13.9 1.0 %shard_map.85 = (f32[1536,128]{1,0:T(8,128)S(1)}, f32[192,128]{1,0:T(8,128)S(1)}, f32[128,128]{1,0:T(8,128)S(1)}, f32[136,128]{1,0:T(8,128)S(1)}) custom-call(f32[1536,128]{1,0:T(8,128)S(1)} %get-tuple-element.30.field_ref, f32[1536,128]{1,0:T(8,128)S(1)} %get-tuple-element.31.part_ref, f32[416,128]{1,0:T(8,128)S(1)} %collective-permute-done.1.xev_ref, ...), custom_call_target="tpu_custom_call" | custom-call | tf_op jit(solution)/shard_map/pallas_call | solution.py:671
  14.9 0.0 collective-permute-done.4.yod_ref
  14.9 0.0 collective-permute-done.5.yev_ref
  14.9 1.2 %shard_map.86 = (f32[384,128]{1,0:T(8,128)S(1)}, f32[384,128]{1,0:T(8,128)S(1)}, f32[24,128]{1,0:T(8,128)S(1)}, f32[24,128]{1,0:T(8,128)S(1)}, f32[192,128]{1,0:...) custom-call(f32[1536,128]{1,0:T(8,128)S(1)} %get-tuple-element.38.field_ref, ...), custom_call_target="tpu_custom_call" | custom-call | tf_op jit(solution)/shard_map/pallas_call | solution.py:671
  16.1 0.1 collective-permute-start.6
  16.2 3.8 %collective-permute-start.7 = (f32[384,128]{1,0:T(8,128)S(1)}, f32[384,128]{1,0:T(8,128)S(1)}, u32[]{:S(2)}, u32[]{:S(2)}) collective-permute-start(f32[384,128]{1,0:T(8,128)S(1)} %get-tuple-element.48), channel_id=1, source_target_pairs={{4,8},{8,4},{5,9},{9,5},{6,10},{10,6},{7,11},{11,7},{20,24},{24,20... | collective-permute-start | bytes 589832 | tf_op jit(solution)/shard_map/ppermute | solution.py:690
  20.0 1.3 %collective-permute-start.8 = (f32[128,128]{1,0:T(8,128)S(1)}, f32[128,128]{1,0:T(8,128)S(1)}, u32[]{:S(2)}, u32[]{:S(2)}) collective-permute-start(f32[128,128]{1,0:T(8,128)S(1)} %get-tuple-element.50.rest_0_), channel_id=1, source_target_pairs={{0,16},{16,0},{1,17},{17,1},{2,18},{18,2},{3,19},{19,3},{4,20},{20... | collective-permute-start | bytes 196616 | tf_op jit(solution)/shard_map/ppermute | solution.py:694
  21.3 0.7 %collective-permute-start.9 = (f32[24,128]{1,0:T(8,128)S(1)}, f32[24,128]{1,0:T(8,128)S(1)}, u32[]{:S(2)}, u32[]{:S(2)}) collective-permute-start(f32[24,128]{1,0:T(8,128)S(1)} %get-tuple-element.52), channel_id=1, source_target_pairs={{0,1},{1,0},{2,3},{3,2},{4,5},{5,4},{6,7},{7,6},{8,9},{9,8},{10,11... | collective-permute-start | bytes 36872 | tf_op jit(solution)/shard_map/ppermute | solution.py:690
  22.1 2.1 %collective-permute-start.10 = (f32[24,128]{1,0:T(8,128)S(1)}, f32[24,128]{1,0:T(8,128)S(1)}, u32[]{:S(2)}, u32[]{:S(2)}) collective-permute-start(f32[24,128]{1,0:T(8,128)S(1)} %get-tuple-element.53), channel_id=1, source_target_pairs={{1,2},{2,1},{5,6},{6,5},{9,10},{10,9},{13,14},{14,13},{17,18},{18,... | collective-permute-start | bytes 36872 | tf_op jit(solution)/shard_map/ppermute | solution.py:690
  24.2 1.9 %shard_map.87 = (f32[1536,128]{1,0:T(8,128)S(1)}, f32[1536,128]{1,0:T(8,128)S(1)}) custom-call(f32[1536,128]{1,0:T(8,128)S(1)} %get-tuple-element.38.field_ref, f32[192,128]{1,0:T(8,128)S(1)} %get-tuple-element.44.refs_0_, f32[1336,128]{1,0:T(8,128)S(1)} %get-tuple-element.35.inner.refs_1_), custom_call_target="tpu_custom_call" | custom-call | tf_op jit(solution)/shard_map/pallas_call | solution.py:671
  26.1 0.0 collective-permute-done.8.rest_1_
  26.1 0.0 collective-permute-done.6.xev_ref
  26.1 0.0 collective-permute-done.7.xod_ref
  26.1 0.7 %shard_map.88.field_ref = f32[1536,128]{1,0:T(8,128)S(1)} custom-call(f32[1536,128]{1,0:T(8,128)S(1)} %get-tuple-element.45.field_ref, f32[1536,128]{1,0:T(8,128)S(1)} %get-tuple-element.46.part_ref, f32[384,128]{1,0:T(8,128)S(1)} %collective-permute-done.6.xev_ref, f32[384,128]{1,0:T(8,128)S(1)} %collective-permute-done.7.xod_ref, ...), custom_call_target="tpu_custom_call" | custom-call | tf_op jit(solution)/shard_map/pallas_call | solution.py:671
  26.8 0.0 collective-permute-done.9.yev_ref
  26.8 0.0 collective-permute-done.10.yod_ref
  26.8 1.7 %shard_map.89 = f32[1536,128]{1,0:T(8,128)} custom-call(f32[1536,128]{1,0:T(8,128)S(1)} %shard_map.88.field_ref, f32[192,128]{1,0:T(8,128)S(1)} %get-tuple-element.51.strips_ref, f32[24,128]{1,0:T(8,128)S(1)} %collective-permute-done.9.yev_ref, f32[24,128]{1,0:T(8,128)S(1)} %collective-permute-done.10.yod_ref, f32[160,128]{1,0:T(8,128)S(1)} %get-tuple-element.54.ends), custom_call_target="tpu_custom_call" | custom-call | tf_op jit(solution)/shard_map/pallas_call | solution.py:671
Async XLA Ops:
  0.0 3.7 %collective-permute-start = (f32[192,128]{1,0:T(8,128)}, f32[192,128]{1,0:T(8,128)S(1)}, u32[]{:S(2)}, u32[]{:S(2)}) collective-permute-start(f32[192,128]{1,0:T(8,128)} %bitcast.4), channel_id=1, source_target_pairs={{0,16},{16,0},{1,17},{17,1},{2,18},{18,2},{3,19},{19,3},{4,20},{20... | collective-permute-start | bytes 294920 | tf_op jit(solution)/shard_map/ppermute | solution.py:694
  1.2 2.4 %copy-start = (f32[3,8,8,128]{3,2,1,0:T(8,128)S(1)}, f32[3,8,8,128]{3,2,1,0:T(8,128)}, u32[]{:S(2)}) copy-start(f32[3,8,8,128]{3,2,1,0:T(8,128)} %param.9) | copy-start | bytes 294916
  1.2 2.4 %copy-start.3 = (f32[8,128]{1,0:T(8,128)S(1)}, f32[8,128]{1,0:T(8,128)}, u32[]{:S(2)}) copy-start(f32[8,128]{1,0:T(8,128)} %east_ref.3) | copy-start | bytes 12292
  1.2 2.4 %copy-start.4 = (f32[8,128]{1,0:T(8,128)S(1)}, f32[8,128]{1,0:T(8,128)}, u32[]{:S(2)}) copy-start(f32[8,128]{1,0:T(8,128)} %north_ref.1) | copy-start | bytes 12292
  3.3 0.7 %copy-start.2 = (s32[8,128]{1,0:T(8,128)S(1)}, s32[8,128]{1,0:T(8,128)}, u32[]{:S(2)}) copy-start(s32[8,128]{1,0:T(8,128)} %depth_ref.3) | copy-start | bytes 12292
  3.3 10.5 %collective-permute-start.3 = (f32[424,128]{1,0:T(8,128)S(1)}, f32[424,128]{1,0:T(8,128)S(1)}, u32[]{:S(2)}, u32[]{:S(2)}) collective-permute-start(f32[424,128]{1,0:T(8,128)S(1)} %get-tuple-element.37.rest_0_), channel_id=1, source_target_pairs={{0,16},{16,0},{1,17},{17,1},{2,18},{18,2},{3,19},{19,3},{4,20},{20... | collective-permute-start | bytes 651272 | tf_op jit(solution)/shard_map/ppermute | solution.py:694
  4.2 9.6 %collective-permute-start.1 = (f32[416,128]{1,0:T(8,128)S(1)}, f32[416,128]{1,0:T(8,128)S(1)}, u32[]{:S(2)}, u32[]{:S(2)}) collective-permute-start(f32[416,128]{1,0:T(8,128)S(1)} %get-tuple-element.33), channel_id=1, source_target_pairs={{0,4},{4,0},{8,12},{12,8},{1,5},{5,1},{9,13},{13,9},{2,6},{6,2},{1... | collective-permute-start | bytes 638984 | tf_op jit(solution)/shard_map/ppermute | solution.py:690
  5.9 8.0 %collective-permute-start.2 = (f32[416,128]{1,0:T(8,128)S(1)}, f32[416,128]{1,0:T(8,128)S(1)}, u32[]{:S(2)}, u32[]{:S(2)}) collective-permute-start(f32[416,128]{1,0:T(8,128)S(1)} %get-tuple-element.34), channel_id=1, source_target_pairs={{4,8},{8,4},{5,9},{9,5},{6,10},{10,6},{7,11},{11,7},{20,24},{24,20... | collective-permute-start | bytes 638984 | tf_op jit(solution)/shard_map/ppermute | solution.py:690
  8.9 6.0 %collective-permute-start.4 = (f32[32,128]{1,0:T(8,128)S(1)}, f32[32,128]{1,0:T(8,128)S(1)}, u32[]{:S(2)}, u32[]{:S(2)}) collective-permute-start(f32[32,128]{1,0:T(8,128)S(1)} %get-tuple-element.42), channel_id=1, source_target_pairs={{1,2},{2,1},{5,6},{6,5},{9,10},{10,9},{13,14},{14,13},{17,18},{18,... | collective-permute-start | bytes 49160 | tf_op jit(solution)/shard_map/ppermute | solution.py:690
  12.1 1.8 %copy-start.1 = (f32[16,8,128]{2,1,0:T(8,128)S(1)}, f32[16,8,128]{2,1,0:T(8,128)}, u32[]{:S(2)}) copy-start(f32[16,8,128]{2,1,0:T(8,128)} %param.13) | copy-start | bytes 196612
  12.1 2.8 %collective-permute-start.5 = (f32[32,128]{1,0:T(8,128)S(1)}, f32[32,128]{1,0:T(8,128)S(1)}, u32[]{:S(2)}, u32[]{:S(2)}) collective-permute-start(f32[32,128]{1,0:T(8,128)S(1)} %get-tuple-element.43), channel_id=1, source_target_pairs={{0,1},{1,0},{2,3},{3,2},{4,5},{5,4},{6,7},{7,6},{8,9},{9,8},{10,11... | collective-permute-start | bytes 49160 | tf_op jit(solution)/shard_map/ppermute | solution.py:690
  16.1 10.0 %collective-permute-start.6 = (f32[384,128]{1,0:T(8,128)S(1)}, f32[384,128]{1,0:T(8,128)S(1)}, u32[]{:S(2)}, u32[]{:S(2)}) collective-permute-start(f32[384,128]{1,0:T(8,128)S(1)} %get-tuple-element.47), channel_id=1, source_target_pairs={{0,4},{4,0},{8,12},{12,8},{1,5},{5,1},{9,13},{13,9},{2,6},{6,2},{1... | collective-permute-start | bytes 589832 | tf_op jit(solution)/shard_map/ppermute | solution.py:690
  16.2 9.9 %collective-permute-start.7 = (f32[384,128]{1,0:T(8,128)S(1)}, f32[384,128]{1,0:T(8,128)S(1)}, u32[]{:S(2)}, u32[]{:S(2)}) collective-permute-start(f32[384,128]{1,0:T(8,128)S(1)} %get-tuple-element.48), channel_id=1, source_target_pairs={{4,8},{8,4},{5,9},{9,5},{6,10},{10,6},{7,11},{11,7},{20,24},{24,20... | collective-permute-start | bytes 589832 | tf_op jit(solution)/shard_map/ppermute | solution.py:690
  20.0 6.1 %collective-permute-start.8 = (f32[128,128]{1,0:T(8,128)S(1)}, f32[128,128]{1,0:T(8,128)S(1)}, u32[]{:S(2)}, u32[]{:S(2)}) collective-permute-start(f32[128,128]{1,0:T(8,128)S(1)} %get-tuple-element.50.rest_0_), channel_id=1, source_target_pairs={{0,16},{16,0},{1,17},{17,1},{2,18},{18,2},{3,19},{19,3},{4,20},{20... | collective-permute-start | bytes 196616 | tf_op jit(solution)/shard_map/ppermute | solution.py:694
  21.3 5.4 %collective-permute-start.9 = (f32[24,128]{1,0:T(8,128)S(1)}, f32[24,128]{1,0:T(8,128)S(1)}, u32[]{:S(2)}, u32[]{:S(2)}) collective-permute-start(f32[24,128]{1,0:T(8,128)S(1)} %get-tuple-element.52), channel_id=1, source_target_pairs={{0,1},{1,0},{2,3},{3,2},{4,5},{5,4},{6,7},{7,6},{8,9},{9,8},{10,11... | collective-permute-start | bytes 36872 | tf_op jit(solution)/shard_map/ppermute | solution.py:690
  22.1 4.7 %collective-permute-start.10 = (f32[24,128]{1,0:T(8,128)S(1)}, f32[24,128]{1,0:T(8,128)S(1)}, u32[]{:S(2)}, u32[]{:S(2)}) collective-permute-start(f32[24,128]{1,0:T(8,128)S(1)} %get-tuple-element.53), channel_id=1, source_target_pairs={{1,2},{2,1},{5,6},{6,5},{9,10},{10,9},{13,14},{14,13},{17,18},{18,... | collective-permute-start | bytes 36872 | tf_op jit(solution)/shard_map/ppermute | solution.py:690

commit v6 on v5

--- a/solution.py
+++ b/solution.py
@@ -8,9 +8,10 @@
 from jax.sharding import PartitionSpec as P
 
 STEPS = 2
+LONG = pl.CostEstimate(flops=2_000_000_000, bytes_accessed=400_000_000, transcendentals=0)
 SUB = 8
 LIM = 48 * 1024 * 1024
-INSIDE, FINISH = 3, 3
+INSIDE, FINISH, LAST = 3, 3, 3
 
 
 def with_halo(cells, sides, width):
@@ -108,6 +109,7 @@
 
 WIDE = 16
 EACH = 128 // WIDE
+SLOTS = WIDE // 4
 
 
 class Geo:
@@ -118,8 +120,8 @@
         self.K = rows * self.LH
         self.NV = self.K // EACH
         self.SR = self.NV * SUB
-        self.my1 = -(-(tr_dev + 3) * self.NV // EACH)
-        self.my2 = -(-tr_dev * self.NV // EACH)
+        self.my1 = -(-(tr_dev + 3) * self.NV // SLOTS)
+        self.my2 = -(-tr_dev * self.NV // SLOTS)
         self.inner = Table(
             hx=(rows + 1) * self.LH, px=(rows + 1) * self.LH, mx=(rows + 1) * self.LH,
             kx=rows + 1, hy=self.K, py=self.K, my=self.K, ky=rows,
@@ -184,36 +186,27 @@
     for v in range(0, len(parts), EACH):
         packed = jnp.zeros((SUB, 128), jnp.float32)
         for k, part in enumerate(parts[v : v + EACH]):
-            inside = (lane >= WIDE * k + 8) & (lane < WIDE * k + 16)
-            packed = jnp.where(inside, roll(part, WIDE * k + 12, 1), packed)
+            inside = (lane >= WIDE * k + 6) & (lane < WIDE * k + 14)
+            packed = jnp.where(inside, roll(part, WIDE * k + 10, 1), packed)
         out.append(packed)
     return out
 
 
-def message_strips(packed, low):
-    place = lanes() % WIDE
-    out = jnp.zeros((SUB, 128), jnp.float32)
-    for m, one in enumerate(packed):
-        moved = roll(one, 2 * m - (12 if low else 10), 1)
-        out = jnp.where((place == 2 * m) | (place == 2 * m + 1), moved, out)
-    return out
-
-
-def put_messages(packed, even, ev_ref, od_ref):
-    for v in range(0, len(packed), EACH):
-        low = message_strips(packed[v : v + EACH], True)
-        high = message_strips(packed[v : v + EACH], False)
-        at = rows8(v // EACH)
-        ev_ref[at, :] = jnp.where(even, high, low)
-        od_ref[at, :] = jnp.where(even, low, high)
+def put_messages(packed, out_ref):
+    slot = (lanes() % WIDE) // 4
+    for v in range(0, len(packed), SLOTS):
+        out = jnp.zeros((SUB, 128), jnp.float32)
+        for m, one in enumerate(packed[v : v + SLOTS]):
+            out = jnp.where(slot == m, roll(one, 4 * m - 8, 1), out)
+        out_ref[rows8(v // SLOTS), :] = out
 
 
 def full_strips(own, from_lower, from_upper, m):
     place = lanes() % WIDE
-    out = jnp.where(place < 2, roll(from_lower, -2 * m, 1), 0.0)
-    out = jnp.where((place >= 2) & (place < 6), roll(own, -10, 1), out)
-    out = jnp.where((place >= 8) & (place < 12), own, out)
-    return jnp.where((place >= 12) & (place < 14), roll(from_upper, 12 - 2 * m, 1), out)
+    out = jnp.where(place < 2, roll(from_lower, -4 * m, 1), roll(own, -8, 1))
+    out = jnp.where(place < 6, out, own)
+    out = jnp.where(place < 10, out, roll(from_upper, 8 - 4 * m, 1))
+    return jnp.where(place < 12, out, 0.0)
 
 
 def spread(rows, r):
@@ -309,9 +302,9 @@
 
 def first_messages_kernel(
     g, field_ref, strips_ref, mine_ref, other_ref, depth_ref, east_ref, north_ref,
-    xev_ref, xod_ref, yev_ref, yod_ref, extra_ref,
+    xev_ref, xod_ref, y_ref, extra_ref,
 ):
-    x_even, y_even = is_even("gx"), is_even("gy")
+    x_even = is_even("gx")
     flux = flux_reader(g, mine_ref, other_ref)
     zero = jnp.zeros((SUB, 128), jnp.float32)
 
@@ -338,7 +331,7 @@
     extras += pack_strips(spread_rows(g, north_ref[...]))
     for i, packed in enumerate(extras):
         extra_ref[rows8(i), :] = packed
-    put_messages(registers(strips_ref) + extras, y_even, yev_ref, yod_ref)
+    put_messages(registers(strips_ref) + extras, y_ref)
 
 
 def wet_levels(g, depths):
@@ -393,7 +386,7 @@
         for which in range(3):
             own = which * g.NV + i
             slot = g.T * g.NV + own
-            full.append(full_strips(extra_ref[rows8(own), :], *extra_y(slot // EACH), slot % EACH))
+            full.append(full_strips(extra_ref[rows8(own), :], *extra_y(slot // SLOTS), slot % SLOTS))
         wet = [level < roll(full[0], -away, 1) for away in (-2, -1, 0, 1, 2)]
         opened = [a & b for a, b in zip(wet, wet[1:])]
         for face in range(4):
@@ -479,19 +472,19 @@
     ]
     tend = flow[0] - flow[1]
     place = lanes() % WIDE
-    tend = jnp.where(place < 12, tend, roll(tend, 10, 1))
-    return jnp.where((place >= 10) & (place < 14), tend, 0.0)
+    tend = jnp.where(place < 10, tend, roll(tend, 8, 1))
+    return jnp.where((place >= 8) & (place < 12), tend, 0.0)
 
 
 def all_strip_tendencies(g, cf, strips_ref, sides, tend_ref):
     for n in range(g.T * g.NV):
-        full = full_strips(strips_ref[rows8(n), :], *sides(n // EACH), n % EACH)
+        full = full_strips(strips_ref[rows8(n), :], *sides(n // SLOTS), n % SLOTS)
         tend_ref[rows8(n), :] = strip_tendency(g, cf, full, n % g.NV)
 
 
 def end_columns(g, tend_ref, t, k):
     v, n = divmod(k, EACH)
-    return jnp.where(end_lanes(), roll(tend_ref[rows8(t * g.NV + v), :], -(WIDE * n + 12), 1), 0.0)
+    return jnp.where(end_lanes(), roll(tend_ref[rows8(t * g.NV + v), :], -(WIDE * n + 10), 1), 0.0)
 
 
 def set_factor(g, total, factor, grazers_ref, prey_refs):
@@ -503,7 +496,7 @@
             factor[at, :] = grazers / (1.0 + 4.0 * prey / total)
 
 
-def finish(g, inner, outer, t, field_ref, part_ref, sides, taste, factor, emit):
+def finish(g, inner, outer, t, field_ref, part_ref, sides, emit):
     base = pl.multiple_of(t * g.tile, g.tile)
 
     def cell(r, lh):
@@ -539,8 +532,7 @@
                     k = r * g.LH + lh
                     old = cell(r, lh)
                     new = part_ref[pl.ds(base + k * SUB, SUB), :] + (carried - flow)
-                    new = new - (taste * factor[rows8(k), :]) * old
-                    emit(r, lh, new)
+                    emit(r, lh, old, new)
                 carried = flow
             state[lh] = (up, j_up, c + s, carried)
 
@@ -572,13 +564,14 @@
         base = pl.multiple_of(t * g.tile, g.tile)
         news = {}
 
-        def emit(r, lh, new):
+        def emit(r, lh, old, new):
             at = (r * g.LH + lh) * SUB
+            new = new - (taste * factor[at : at + SUB, :]) * old
             out_ref[pl.ds(base + at, SUB), :] = new
             prey_ref[at : at + SUB, :] += taste * new
             news[r, lh] = new
 
-        finish(g, inner, outer, t, field_ref, part_ref, x_sides, taste, factor, emit)
+        finish(g, inner, outer, t, field_ref, part_ref, x_sides, emit)
         parts = [news[r, lh] for r in range(g.R) for lh in range(g.LH)]
         for i, packed in enumerate(pack_strips(parts)):
             strips_ref[rows8(t * g.NV + i), :] = packed
@@ -588,16 +581,16 @@
 
 def second_messages_kernel(
     g, field_ref, strips_ref, next_ref, prey_ref, extra_ref, yod_ref, yev_ref, taste_ref,
-    xev2_ref, xod2_ref, yev2_ref, yod2_ref, strips2_ref, prey2_ref, tend_ref, ends, grazed,
+    xev2_ref, xod2_ref, y2_ref, strips2_ref, prey2_ref, tend_ref, ends, grazed,
 ):
-    x_even, y_even = is_even("gx"), is_even("gy")
-    y_sides = reader(y_even, yev_ref, yod_ref)
+    x_even = is_even("gx")
+    y_sides = reader(is_even("gy"), yev_ref, yod_ref)
     strip_coefficients(g, ends, y_sides, extra_ref)
     all_strip_tendencies(g, ends, strips_ref, y_sides, tend_ref)
     packed = [next_ref[rows8(n), :] + tend_ref[rows8(n), :] for n in range(g.T * g.NV)]
     for n, one_packed in enumerate(packed):
         strips2_ref[rows8(n), :] = one_packed
-    put_messages(packed, y_even, yev2_ref, yod2_ref)
+    put_messages(packed, y2_ref)
     for i in range(g.NV):
         grazed[rows8(i), :] = sum(
             taste_of(taste_ref, t) * tend_ref[rows8(t * g.NV + i), :] for t in range(g.T)
@@ -615,34 +608,31 @@
             xev2_ref[at, :] = jnp.where(x_even, high, low)
             xod2_ref[at, :] = jnp.where(x_even, low, high)
 
-    each_tracer(g, 4, one)
-
-
-def border_two_kernel(
-    g, total, ahead,
-    field_ref, part_ref, xev_ref, xod_ref, inner, outer, grazers_ref, taste_ref, *rest,
-):
-    prey_refs, (out_ref, factor) = rest[:-2], rest[-2:]
+    each_tracer(g, 6, one)
+
+
+def border_two_kernel(g, ahead, field_ref, part_ref, xev_ref, xod_ref, inner, outer, out_ref):
     x_sides = reader(is_even("gx"), xev_ref, xod_ref)
-    set_factor(g, total, factor, grazers_ref, prey_refs)
 
     def one(t):
         base = pl.multiple_of(t * g.tile, g.tile)
 
-        def emit(r, lh, new):
+        def emit(r, lh, old, new):
             out_ref[pl.ds(base + (r * g.LH + lh) * SUB, SUB), :] = new
 
-        taste = taste_of(taste_ref, t)
-        finish(g, inner, outer, t, field_ref, part_ref, x_sides, taste, factor, emit)
+        finish(g, inner, outer, t, field_ref, part_ref, x_sides, emit)
 
     each_tracer(g, ahead, one)
 
 
 def result_kernel(
-    g, ahead, field_ref, strips_ref, yev_ref, yod_ref, ends, out_ref, tend_ref, leaving, sems
+    g, total, ahead, field_ref, part_ref, strips_ref, yev_ref, yod_ref, ends, grazers_ref, taste_ref,
+    *rest,
 ):
+    prey_refs, (out_ref, factor, tend_ref, leaving, sems) = rest[:-5], rest[-5:]
     y_sides = reader(is_even("gy"), yev_ref, yod_ref)
     all_strip_tendencies(g, ends, strips_ref, y_sides, tend_ref)
+    set_factor(g, total, factor, grazers_ref, prey_refs)
 
     def departure(t):
         at = pl.ds(pl.multiple_of(t * g.tile, g.tile), g.tile)
@@ -650,10 +640,13 @@
 
     def one(t):
         base = pl.multiple_of(t * g.tile, g.tile)
+        taste = taste_of(taste_ref, t)
         for r in range(g.R):
             for lh in range(g.LH):
                 k = r * g.LH + lh
-                new = field_ref[rows8(t * g.K + k), :] + end_columns(g, tend_ref, t, k)
+                at = rows8(t * g.K + k)
+                new = part_ref[at, :] + end_columns(g, tend_ref, t, k)
+                new = new - (taste * factor[rows8(k), :]) * field_ref[at, :]
                 leaving[pl.ds(base + lh * SUB * g.R + r, SUB, stride=g.R), :] = new
         departure(t).start()
 
@@ -662,7 +655,7 @@
         departure(t).wait()
 
 
-def call(body, outs, operands, far=0, far_out=False, scratch=()):
+def call(body, outs, operands, far=0, far_out=False, scratch=(), cost=None):
     spaces = [pltpu.HBM if i < far else pltpu.VMEM for i in range(len(operands))]
     operands = [
         pltpu.with_memory_space_constraint(a, space) if space == pltpu.HBM else a
@@ -678,6 +671,7 @@
             for rows in scratch
         ],
         compiler_params=pltpu.CompilerParams(vmem_limit_bytes=LIM),
+        cost_estimate=cost,
     )(*operands)
 
 
@@ -700,12 +694,9 @@
     return [lax.psum(values, "tracer")]
 
 
-def neighbours(x_ev, x_od, y_ev, y_od):
-    x_od = pair_swap(x_od, "gx", 1)
-    y_ev = pair_swap(y_ev, "gy", 0)
-    y_od = pair_swap(y_od, "gy", 1)
-    x_ev = pair_swap(x_ev, "gx", 0)
-    return x_ev, x_od, y_ev, y_od
+def neighbours(x_ev, x_od, y):
+    y_ev, y_od = pair_swap(y, "gy", 0), pair_swap(y, "gy", 1)
+    return pair_swap(x_ev, "gx", 0), pair_swap(x_od, "gx", 1), y_ev, y_od
 
 
 def on_device(tracers, fluxes, diff_east, diff_north, column_depth, grazers, groups, preference):
@@ -741,7 +732,7 @@
     x_more = x_rows + g.L + 2 * SUB
     *messages, extra = call(
         functools.partial(first_messages_kernel, g),
-        [x_more, x_more, g.my1 * SUB, g.my1 * SUB, 3 * g.SR],
+        [x_more, x_more, g.my1 * SUB, 3 * g.SR],
         [field, strips, mine, other, column_depth, diff_east, diff_north],
     )
     messages = neighbours(*messages)
@@ -760,27 +751,28 @@
     )
     *messages, strips, prey, tend, ends = call(
         functools.partial(second_messages_kernel, g),
-        [x_rows, x_rows, g.my2 * SUB, g.my2 * SUB, g.T * g.SR, g.tile, g.T * g.SR, g.ends.rows],
+        [x_rows, x_rows, g.my2 * SUB, g.T * g.SR, g.tile, g.T * g.SR, g.ends.rows],
         [field, strips, next_strips, next_prey, extra, *messages[2:], taste],
         scratch=[g.SR],
     )
     prey = all_prey(prey)
     messages = neighbours(*messages)
     field, part = call(
-        functools.partial(inside_kernel, g, INSIDE, False), [cells, cells], [field, tend, inner]
-    )
-    (field,) = call(
-        functools.partial(border_two_kernel, g, total, FINISH),
+        functools.partial(inside_kernel, g, INSIDE, False), [cells, cells], [field, tend, inner],
+        cost=LONG,
+    )
+    (part,) = call(
+        functools.partial(border_two_kernel, g, FINISH),
         [cells],
-        [field, part, *messages[:2], inner, outer, grazers, taste, *prey],
-        scratch=[g.tile],
+        [field, part, *messages[:2], inner, outer],
+        cost=LONG,
     )
     (out,) = call(
-        functools.partial(result_kernel, g, FINISH),
+        functools.partial(result_kernel, g, total, LAST),
         [cells],
-        [field, strips, *messages[2:], ends],
+        [field, part, strips, *messages[2:], ends, grazers, taste, *prey],
         far_out=True,
-        scratch=[g.T * g.SR, cells, copies],
+        scratch=[g.tile, g.T * g.SR, cells, copies],
     )
     return out.reshape(tracers.shape)
 

time: 28.9 us -> 28.4 us (0.983)
  Pallas kernels: 10.4 us -> 9.82 us
    pallas_call x8, Pallas kernels: 10.4 us -> 9.82 us  [call(): pl.pallas_call(body, out_shape=[jax.ShapeDtypeStruct((rows, 128), jnp.flo...]
where the time goes in v6:
time: 28.4 us; the launch traced here: 28 us
  starting transfers between devices  17.6 us (62%)
  Pallas kernels  9.82 us (35%)
  local copies, waits for them, and re-layouts  0.34 us (1%)
    ppermute x8, starting transfers between devices, pair_swap(): return lax.ppermute(values, axis, pairs)  14.7 us
    pallas_call x8, Pallas kernels, call(): pl.pallas_call(body, out_shape=[jax.ShapeDtypeStruct((rows, 128), jnp.flo...  9.82 us
    ppermute x3, starting transfers between devices, tracer_swap(): return lax.ppermute(values, 'tracer', [(0, 1), (1, 0)])  2.85 us
  transfers between devices with their start and end apart: 11, of which 1 were waited for; matrix products, arithmetic and copies ran while one was open for 0% of the time, Pallas kernels for 26%

profile of v6, /device:TPU:9, one launch (start us, length us, event | category | flops | bytes accessed | tf_op | source)
XLA Modules:
  0.0 28.0 jit_solution(8406340354772469452)
XLA Ops:
  0.0 1.2 %collective-permute-start = (f32[192,128]{1,0:T(8,128)}, f32[192,128]{1,0:T(8,128)S(1)}, u32[]{:S(2)}, u32[]{:S(2)}) collective-permute-start(f32[192,128]{1,0:T(8,128)} %bitcast.4), channel_id=1, source_target_pairs={{0,16},{16,0},{1,17},{17,1},{2,18},{18,2},{3,19},{19,3},{4,20},{20... | collective-permute-start | bytes 294920 | tf_op jit(solution)/shard_map/ppermute | solution.py:688
  1.2 0.0 copy-start
  1.2 0.0 copy-start.3
  1.2 0.0 copy-start.4
  1.2 2.1 %shard_map.82 = (f32[1536,128]{1,0:T(8,128)S(1)}, f32[192,128]{1,0:T(8,128)S(1)}, f32[424,128]{1,0:T(8,128)S(1)}, f32[96,128]{1,0:T(8,128)S(1)}) custom-call(f32[1536,128]{1,0:T(8,128)} %bitcast.10, s32[12]{0:T(128)} %groups_far.1, f32[16]{0:T(128)} %pref_far.1), custom_call_target="tpu_custom_call" | custom-call | tf_op jit(solution)/shard_map/pallas_call | solution.py:664
  3.3 0.0 copy-start.2
  3.3 0.3 %collective-permute-start.3 = (f32[424,128]{1,0:T(8,128)S(1)}, f32[424,128]{1,0:T(8,128)S(1)}, u32[]{:S(2)}, u32[]{:S(2)}) collective-permute-start(f32[424,128]{1,0:T(8,128)S(1)} %get-tuple-element.35.rest_0_), channel_id=1, source_target_pairs={{0,16},{16,0},{1,17},{17,1},{2,18},{18,2},{3,19},{19,3},{4,20},{20... | collective-permute-start | bytes 651272 | tf_op jit(solution)/shard_map/ppermute | solution.py:688
  3.6 0.1 collective-permute-done.refs_1_.other_ref
  3.7 0.0 copy-done
  3.7 0.0 copy-done.3
  3.7 0.0 copy-done.4
  3.7 0.3 %copy-done.2 = s32[8,128]{1,0:T(8,128)S(1)} copy-done((s32[8,128]{1,0:T(8,128)S(1)}, s32[8,128]{1,0:T(8,128)}, u32[]{:S(2)}) %copy-start.2) | copy-done | bytes 4120
  4.0 0.2 shard_map.84
  4.2 1.6 %collective-permute-start.1 = (f32[416,128]{1,0:T(8,128)S(1)}, f32[416,128]{1,0:T(8,128)S(1)}, u32[]{:S(2)}, u32[]{:S(2)}) collective-permute-start(f32[416,128]{1,0:T(8,128)S(1)} %get-tuple-element.31), channel_id=1, source_target_pairs={{0,4},{4,0},{8,12},{12,8},{1,5},{5,1},{9,13},{13,9},{2,6},{6,2},{1... | collective-permute-start | bytes 638984 | tf_op jit(solution)/shard_map/ppermute | solution.py:684
  5.8 3.0 %collective-permute-start.2 = (f32[416,128]{1,0:T(8,128)S(1)}, f32[416,128]{1,0:T(8,128)S(1)}, u32[]{:S(2)}, u32[]{:S(2)}) collective-permute-start(f32[416,128]{1,0:T(8,128)S(1)} %get-tuple-element.32), channel_id=1, source_target_pairs={{4,8},{8,4},{5,9},{9,5},{6,10},{10,6},{7,11},{11,7},{20,24},{24,20... | collective-permute-start | bytes 638984 | tf_op jit(solution)/shard_map/ppermute | solution.py:684
  8.8 0.0 copy-start.1
  8.8 3.3 %collective-permute-start.4 = (f32[64,128]{1,0:T(8,128)S(1)}, f32[64,128]{1,0:T(8,128)S(1)}, u32[]{:S(2)}, u32[]{:S(2)}) collective-permute-start(f32[64,128]{1,0:T(8,128)S(1)} %get-tuple-element.40), channel_id=1, source_target_pairs={{1,2},{2,1},{5,6},{6,5},{9,10},{10,9},{13,14},{14,13},{17,18},{18,... | collective-permute-start | bytes 98312 | tf_op jit(solution)/shard_map/ppermute | solution.py:684
  12.2 0.1 collective-permute-start.5
  12.3 1.7 %shard_map.83 = (f32[1536,128]{1,0:T(8,128)S(1)}, f32[1336,128]{1,0:T(8,128)S(1)}) custom-call(f32[1536,128]{1,0:T(8,128)S(1)} %get-tuple-element.28.field_ref, f32[192,128]{1,0:T(8,128)S(1)} %bitcast.6, f32[192,128]{1,0:T(8,128)S(1)} %collective-permute-done.refs_1_.other_ref, s32[8,128]{1,0:T(8,128)S(1)} %copy-done.2, f32[8,128]{1,0:T(8,128)S(1)} %copy-done.3, ...), custom_call_target="tpu_custom_call" | custom-call | tf_op jit(solution)/shard_map/pallas_call | solution.py:664
  13.9 0.0 collective-permute-done.3.rest_1_
  13.9 0.0 collective-permute-done.1.xev_ref
  13.9 0.0 collective-permute-done.2.xod_ref
  14.0 0.0 copy-done.1
  14.0 1.0 %shard_map.85 = (f32[1536,128]{1,0:T(8,128)S(1)}, f32[192,128]{1,0:T(8,128)S(1)}, f32[128,128]{1,0:T(8,128)S(1)}, f32[136,128]{1,0:T(8,128)S(1)}) custom-call(f32[1536,128]{1,0:T(8,128)S(1)} %get-tuple-element.28.field_ref, f32[1536,128]{1,0:T(8,128)S(1)} %get-tuple-element.29.part_ref, f32[416,128]{1,0:T(8,128)S(1)} %collective-permute-done.1.xev_ref, ...), custom_call_target="tpu_custom_call" | custom-call | tf_op jit(solution)/shard_map/pallas_call | solution.py:664
  15.0 0.0 collective-permute-done.4.yod_ref
  15.0 0.0 collective-permute-done.5.yev_ref
  15.0 0.8 %shard_map.86 = (f32[384,128]{1,0:T(8,128)S(1)}, f32[384,128]{1,0:T(8,128)S(1)}, f32[48,128]{1,0:T(8,128)S(1)}, f32[192,128]{1,0:T(8,128)S(1)}, f32[128,128]{1,0...) custom-call(f32[1536,128]{1,0:T(8,128)S(1)} %get-tuple-element.36.field_ref, ...), custom_call_target="tpu_custom_call" | custom-call | tf_op jit(solution)/shard_map/pallas_call | solution.py:664
  15.8 0.1 collective-permute-start.6
  15.9 4.0 %collective-permute-start.7 = (f32[384,128]{1,0:T(8,128)S(1)}, f32[384,128]{1,0:T(8,128)S(1)}, u32[]{:S(2)}, u32[]{:S(2)}) collective-permute-start(f32[384,128]{1,0:T(8,128)S(1)} %get-tuple-element.45), channel_id=1, source_target_pairs={{4,8},{8,4},{5,9},{9,5},{6,10},{10,6},{7,11},{11,7},{20,24},{24,20... | collective-permute-start | bytes 589832 | tf_op jit(solution)/shard_map/ppermute | solution.py:684
  19.8 0.6 %collective-permute-start.8 = (f32[48,128]{1,0:T(8,128)S(1)}, f32[48,128]{1,0:T(8,128)S(1)}, u32[]{:S(2)}, u32[]{:S(2)}) collective-permute-start(f32[48,128]{1,0:T(8,128)S(1)} %get-tuple-element.48), channel_id=1, source_target_pairs={{0,1},{1,0},{2,3},{3,2},{4,5},{5,4},{6,7},{7,6},{8,9},{9,8},{10,11... | collective-permute-start | bytes 73736 | tf_op jit(solution)/shard_map/ppermute | solution.py:684
  20.5 2.1 %collective-permute-start.9 = (f32[48,128]{1,0:T(8,128)S(1)}, f32[48,128]{1,0:T(8,128)S(1)}, u32[]{:S(2)}, u32[]{:S(2)}) collective-permute-start(f32[48,128]{1,0:T(8,128)S(1)} %get-tuple-element.48), channel_id=1, source_target_pairs={{1,2},{2,1},{5,6},{6,5},{9,10},{10,9},{13,14},{14,13},{17,18},{18,... | collective-permute-start | bytes 73736 | tf_op jit(solution)/shard_map/ppermute | solution.py:684
  22.5 1.3 %collective-permute-start.10 = (f32[128,128]{1,0:T(8,128)S(1)}, f32[128,128]{1,0:T(8,128)S(1)}, u32[]{:S(2)}, u32[]{:S(2)}) collective-permute-start(f32[128,128]{1,0:T(8,128)S(1)} %get-tuple-element.50.rest_0_), channel_id=1, source_target_pairs={{0,16},{16,0},{1,17},{17,1},{2,18},{18,2},{3,19},{19,3},{4,20},{20... | collective-permute-start | bytes 196616 | tf_op jit(solution)/shard_map/ppermute | solution.py:688
  23.9 1.9 %shard_map.87 = (f32[1536,128]{1,0:T(8,128)S(1)}, f32[1536,128]{1,0:T(8,128)S(1)}) custom-call(f32[1536,128]{1,0:T(8,128)S(1)} %get-tuple-element.36.field_ref, f32[192,128]{1,0:T(8,128)S(1)} %get-tuple-element.41.refs_0_, f32[1336,128]{1,0:T(8,128)S(1)} %get-tuple-element.33.inner.refs_1_), custom_call_target="tpu_custom_call" | custom-call | flops 2000000000 | bytes 400000000 | tf_op jit(solution)/shard_map/pallas_call | solution.py:664
  25.8 0.0 collective-permute-done.6.xev_ref
  25.8 0.0 collective-permute-done.7.xod_ref
  25.8 0.6 %shard_map.88.part_ref = f32[1536,128]{1,0:T(8,128)S(1)} custom-call(f32[1536,128]{1,0:T(8,128)S(1)} %get-tuple-element.42.field_ref, f32[1536,128]{1,0:T(8,128)S(1)} %get-tuple-element.43.part_ref, f32[384,128]{1,0:T(8,128)S(1)} %collective-permute-done.6.xev_ref, f32[384,128]{1,0:T(8,128)S(1)} %collective-permute-done.7.xod_ref, ...), custom_call_target="tpu_custom_call" | custom-call | flops 2000000000 | bytes 400000000 | tf_op jit(solution)/shard_map/pallas_call | solution.py:664
  26.3 0.0 collective-permute-done.8.yev_ref
  26.4 0.0 collective-permute-done.9.yod_ref
  26.4 0.0 collective-permute-done.10.rest_1_
  26.4 1.7 %shard_map.89 = f32[1536,128]{1,0:T(8,128)} custom-call(f32[1536,128]{1,0:T(8,128)S(1)} %get-tuple-element.42.field_ref, f32[1536,128]{1,0:T(8,128)S(1)} %shard_map.88.part_ref, f32[192,128]{1,0:T(8,128)S(1)} %get-tuple-element.47.strips_ref, f32[48,128]{1,0:T(8,128)S(1)} %collective-permute-done.8.yev_ref, f32[48,128]{1,0:T(8,128)S(1)} %collective-permute-done.9.yod_ref, ...), custom_call_target="tpu_custom_call" | custom-call | tf_op jit(solution)/shard_map/pallas_call | solution.py:664
Async XLA Ops:
  0.0 3.7 %collective-permute-start = (f32[192,128]{1,0:T(8,128)}, f32[192,128]{1,0:T(8,128)S(1)}, u32[]{:S(2)}, u32[]{:S(2)}) collective-permute-start(f32[192,128]{1,0:T(8,128)} %bitcast.4), channel_id=1, source_target_pairs={{0,16},{16,0},{1,17},{17,1},{2,18},{18,2},{3,19},{19,3},{4,20},{20... | collective-permute-start | bytes 294920 | tf_op jit(solution)/shard_map/ppermute | solution.py:688
  1.2 2.4 %copy-start = (f32[3,8,8,128]{3,2,1,0:T(8,128)S(1)}, f32[3,8,8,128]{3,2,1,0:T(8,128)}, u32[]{:S(2)}) copy-start(f32[3,8,8,128]{3,2,1,0:T(8,128)} %param.9) | copy-start | bytes 294916
  1.2 2.4 %copy-start.3 = (f32[8,128]{1,0:T(8,128)S(1)}, f32[8,128]{1,0:T(8,128)}, u32[]{:S(2)}) copy-start(f32[8,128]{1,0:T(8,128)} %east_ref.3) | copy-start | bytes 12292
  1.2 2.4 %copy-start.4 = (f32[8,128]{1,0:T(8,128)S(1)}, f32[8,128]{1,0:T(8,128)}, u32[]{:S(2)}) copy-start(f32[8,128]{1,0:T(8,128)} %north_ref.1) | copy-start | bytes 12292
  3.3 0.7 %copy-start.2 = (s32[8,128]{1,0:T(8,128)S(1)}, s32[8,128]{1,0:T(8,128)}, u32[]{:S(2)}) copy-start(s32[8,128]{1,0:T(8,128)} %depth_ref.3) | copy-start | bytes 12292
  3.3 10.6 %collective-permute-start.3 = (f32[424,128]{1,0:T(8,128)S(1)}, f32[424,128]{1,0:T(8,128)S(1)}, u32[]{:S(2)}, u32[]{:S(2)}) collective-permute-start(f32[424,128]{1,0:T(8,128)S(1)} %get-tuple-element.35.rest_0_), channel_id=1, source_target_pairs={{0,16},{16,0},{1,17},{17,1},{2,18},{18,2},{3,19},{19,3},{4,20},{20... | collective-permute-start | bytes 651272 | tf_op jit(solution)/shard_map/ppermute | solution.py:688
  4.2 9.7 %collective-permute-start.1 = (f32[416,128]{1,0:T(8,128)S(1)}, f32[416,128]{1,0:T(8,128)S(1)}, u32[]{:S(2)}, u32[]{:S(2)}) collective-permute-start(f32[416,128]{1,0:T(8,128)S(1)} %get-tuple-element.31), channel_id=1, source_target_pairs={{0,4},{4,0},{8,12},{12,8},{1,5},{5,1},{9,13},{13,9},{2,6},{6,2},{1... | collective-permute-start | bytes 638984 | tf_op jit(solution)/shard_map/ppermute | solution.py:684
  5.8 8.1 %collective-permute-start.2 = (f32[416,128]{1,0:T(8,128)S(1)}, f32[416,128]{1,0:T(8,128)S(1)}, u32[]{:S(2)}, u32[]{:S(2)}) collective-permute-start(f32[416,128]{1,0:T(8,128)S(1)} %get-tuple-element.32), channel_id=1, source_target_pairs={{4,8},{8,4},{5,9},{9,5},{6,10},{10,6},{7,11},{11,7},{20,24},{24,20... | collective-permute-start | bytes 638984 | tf_op jit(solution)/shard_map/ppermute | solution.py:684
  8.8 5.1 %copy-start.1 = (f32[16,8,128]{2,1,0:T(8,128)S(1)}, f32[16,8,128]{2,1,0:T(8,128)}, u32[]{:S(2)}) copy-start(f32[16,8,128]{2,1,0:T(8,128)} %param.13) | copy-start | bytes 196612
  8.8 6.1 %collective-permute-start.4 = (f32[64,128]{1,0:T(8,128)S(1)}, f32[64,128]{1,0:T(8,128)S(1)}, u32[]{:S(2)}, u32[]{:S(2)}) collective-permute-start(f32[64,128]{1,0:T(8,128)S(1)} %get-tuple-element.40), channel_id=1, source_target_pairs={{1,2},{2,1},{5,6},{6,5},{9,10},{10,9},{13,14},{14,13},{17,18},{18,... | collective-permute-start | bytes 98312 | tf_op jit(solution)/shard_map/ppermute | solution.py:684
  12.2 2.8 %collective-permute-start.5 = (f32[64,128]{1,0:T(8,128)S(1)}, f32[64,128]{1,0:T(8,128)S(1)}, u32[]{:S(2)}, u32[]{:S(2)}) collective-permute-start(f32[64,128]{1,0:T(8,128)S(1)} %get-tuple-element.40), channel_id=1, source_target_pairs={{0,1},{1,0},{2,3},{3,2},{4,5},{5,4},{6,7},{7,6},{8,9},{9,8},{10,11... | collective-permute-start | bytes 98312 | tf_op jit(solution)/shard_map/ppermute | solution.py:684
  15.8 10.0 %collective-permute-start.6 = (f32[384,128]{1,0:T(8,128)S(1)}, f32[384,128]{1,0:T(8,128)S(1)}, u32[]{:S(2)}, u32[]{:S(2)}) collective-permute-start(f32[384,128]{1,0:T(8,128)S(1)} %get-tuple-element.44), channel_id=1, source_target_pairs={{0,4},{4,0},{8,12},{12,8},{1,5},{5,1},{9,13},{13,9},{2,6},{6,2},{1... | collective-permute-start | bytes 589832 | tf_op jit(solution)/shard_map/ppermute | solution.py:684
  15.9 9.9 %collective-permute-start.7 = (f32[384,128]{1,0:T(8,128)S(1)}, f32[384,128]{1,0:T(8,128)S(1)}, u32[]{:S(2)}, u32[]{:S(2)}) collective-permute-start(f32[384,128]{1,0:T(8,128)S(1)} %get-tuple-element.45), channel_id=1, source_target_pairs={{4,8},{8,4},{5,9},{9,5},{6,10},{10,6},{7,11},{11,7},{20,24},{24,20... | collective-permute-start | bytes 589832 | tf_op jit(solution)/shard_map/ppermute | solution.py:684
  19.8 6.5 %collective-permute-start.8 = (f32[48,128]{1,0:T(8,128)S(1)}, f32[48,128]{1,0:T(8,128)S(1)}, u32[]{:S(2)}, u32[]{:S(2)}) collective-permute-start(f32[48,128]{1,0:T(8,128)S(1)} %get-tuple-element.48), channel_id=1, source_target_pairs={{0,1},{1,0},{2,3},{3,2},{4,5},{5,4},{6,7},{7,6},{8,9},{9,8},{10,11... | collective-permute-start | bytes 73736 | tf_op jit(solution)/shard_map/ppermute | solution.py:684
  20.5 5.9 %collective-permute-start.9 = (f32[48,128]{1,0:T(8,128)S(1)}, f32[48,128]{1,0:T(8,128)S(1)}, u32[]{:S(2)}, u32[]{:S(2)}) collective-permute-start(f32[48,128]{1,0:T(8,128)S(1)} %get-tuple-element.48), channel_id=1, source_target_pairs={{1,2},{2,1},{5,6},{6,5},{9,10},{10,9},{13,14},{14,13},{17,18},{18,... | collective-permute-start | bytes 73736 | tf_op jit(solution)/shard_map/ppermute | solution.py:684
  22.5 3.8 %collective-permute-start.10 = (f32[128,128]{1,0:T(8,128)S(1)}, f32[128,128]{1,0:T(8,128)S(1)}, u32[]{:S(2)}, u32[]{:S(2)}) collective-permute-start(f32[128,128]{1,0:T(8,128)S(1)} %get-tuple-element.50.rest_0_), channel_id=1, source_target_pairs={{0,16},{16,0},{1,17},{17,1},{2,18},{18,2},{3,19},{19,3},{4,20},{20... | collective-permute-start | bytes 196616 | tf_op jit(solution)/shard_map/ppermute | solution.py:688

commit v7 on v6

--- a/solution.py
+++ b/solution.py
@@ -8,10 +8,9 @@
 from jax.sharding import PartitionSpec as P
 
 STEPS = 2
-LONG = pl.CostEstimate(flops=2_000_000_000, bytes_accessed=400_000_000, transcendentals=0)
 SUB = 8
 LIM = 48 * 1024 * 1024
-INSIDE, FINISH, LAST = 3, 3, 3
+INSIDE, FINISH, BOTH, LAST = 3, 3, 3, 3
 
 
 def with_halo(cells, sides, width):
@@ -402,15 +401,7 @@
     return (lane < 2) | (lane >= 126)
 
 
-def inside_kernel(g, ahead, first, field_ref, *refs):
-    if first:
-        mine_ref, other_ref, depth_ref, east_ref, north_ref, part_ref, cf = refs
-        inner_coefficients(
-            g, cf, flux_reader(g, mine_ref, other_ref), depth_ref[...].astype(jnp.float32),
-            east_ref[...], north_ref[...],
-        )
-    else:
-        tend_ref, cf, whole_ref, part_ref = refs
+def inside(g, cf, field_ref, part_ref, tend_ref=None, whole_ref=None):
     sub = sublanes()
     ends, top, bottom = end_lanes(), sub == 0, sub == SUB - 1
 
@@ -433,7 +424,7 @@
             index = [r * g.LH + lh for lh in range(g.LH)]
             at = [pl.ds(base + k * SUB, SUB) for k in index]
             cells = [field_ref[a, :] for a in at]
-            if not first:
+            if whole_ref is not None:
                 cells = [c + end_columns(g, tend_ref, t, k) for k, c in zip(index, cells)]
                 for a, c in zip(at, cells):
                     whole_ref[a, :] = c
@@ -454,7 +445,17 @@
             for a, new, high, low in zip(at, news, flow, shift_up(flow)):
                 part_ref[a, :] = new + (high - low)
 
-    each_tracer(g, ahead, one)
+    return one
+
+
+def inside_kernel(
+    g, ahead, field_ref, mine_ref, other_ref, depth_ref, east_ref, north_ref, part_ref, cf
+):
+    inner_coefficients(
+        g, cf, flux_reader(g, mine_ref, other_ref), depth_ref[...].astype(jnp.float32),
+        east_ref[...], north_ref[...],
+    )
+    each_tracer(g, ahead, inside(g, cf, field_ref, part_ref))
 
 
 def strip_tendency(g, cf, full, i):
@@ -580,7 +581,7 @@
 
 
 def second_messages_kernel(
-    g, field_ref, strips_ref, next_ref, prey_ref, extra_ref, yod_ref, yev_ref, taste_ref,
+    g, field_ref, strips_ref, next_ref, prey_ref, extra_ref, yev_ref, yod_ref, taste_ref,
     xev2_ref, xod2_ref, y2_ref, strips2_ref, prey2_ref, tend_ref, ends, grazed,
 ):
     x_even = is_even("gx")
@@ -611,28 +612,46 @@
     each_tracer(g, 6, one)
 
 
-def border_two_kernel(g, ahead, field_ref, part_ref, xev_ref, xod_ref, inner, outer, out_ref):
+def transport_two_kernel(
+    g, total, ahead, field_ref, tend_ref, xev_ref, xod_ref, inner, outer, grazers_ref, taste_ref, *rest
+):
+    prey_refs, (out_ref, whole_ref, part_ref, factor) = rest[:-4], rest[-4:]
+    set_factor(g, total, factor, grazers_ref, prey_refs)
     x_sides = reader(is_even("gx"), xev_ref, xod_ref)
-
-    def one(t):
-        base = pl.multiple_of(t * g.tile, g.tile)
+    early = inside(g, inner, field_ref, part_ref, tend_ref, whole_ref)
+
+    def late(t):
+        taste = taste_of(taste_ref, t)
 
         def emit(r, lh, old, new):
-            out_ref[pl.ds(base + (r * g.LH + lh) * SUB, SUB), :] = new
-
-        finish(g, inner, outer, t, field_ref, part_ref, x_sides, emit)
-
-    each_tracer(g, ahead, one)
+            k = r * g.LH + lh
+            out_ref[rows8(t * g.K + k), :] = new - (taste * factor[rows8(k), :]) * old
+
+        finish(g, inner, outer, t, whole_ref, part_ref, x_sides, emit)
+
+    def group(body, i):
+        for more in range(ahead):
+            body(i * ahead + more)
+
+    def both(i, carry):
+        group(late, i - 1)
+        group(early, i)
+        return carry
+
+    groups = g.T // ahead
+    group(early, 0)
+    lax.fori_loop(1, groups, both, 0)
+    group(late, groups - 1)
+    for t in range(groups * ahead, g.T):
+        early(t)
+        late(t)
 
 
 def result_kernel(
-    g, total, ahead, field_ref, part_ref, strips_ref, yev_ref, yod_ref, ends, grazers_ref, taste_ref,
-    *rest,
+    g, ahead, field_ref, strips_ref, yod_ref, yev_ref, ends, out_ref, tend_ref, leaving, sems
 ):
-    prey_refs, (out_ref, factor, tend_ref, leaving, sems) = rest[:-5], rest[-5:]
     y_sides = reader(is_even("gy"), yev_ref, yod_ref)
     all_strip_tendencies(g, ends, strips_ref, y_sides, tend_ref)
-    set_factor(g, total, factor, grazers_ref, prey_refs)
 
     def departure(t):
         at = pl.ds(pl.multiple_of(t * g.tile, g.tile), g.tile)
@@ -640,13 +659,10 @@
 
     def one(t):
         base = pl.multiple_of(t * g.tile, g.tile)
-        taste = taste_of(taste_ref, t)
         for r in range(g.R):
             for lh in range(g.LH):
                 k = r * g.LH + lh
-                at = rows8(t * g.K + k)
-                new = part_ref[at, :] + end_columns(g, tend_ref, t, k)
-                new = new - (taste * factor[rows8(k), :]) * field_ref[at, :]
+                new = field_ref[rows8(t * g.K + k), :] + end_columns(g, tend_ref, t, k)
                 leaving[pl.ds(base + lh * SUB * g.R + r, SUB, stride=g.R), :] = new
         departure(t).start()
 
@@ -655,7 +671,7 @@
         departure(t).wait()
 
 
-def call(body, outs, operands, far=0, far_out=False, scratch=(), cost=None):
+def call(body, outs, operands, far=0, far_out=False, scratch=()):
     spaces = [pltpu.HBM if i < far else pltpu.VMEM for i in range(len(operands))]
     operands = [
         pltpu.with_memory_space_constraint(a, space) if space == pltpu.HBM else a
@@ -671,7 +687,6 @@
             for rows in scratch
         ],
         compiler_params=pltpu.CompilerParams(vmem_limit_bytes=LIM),
-        cost_estimate=cost,
     )(*operands)
 
 
@@ -702,7 +717,7 @@
 def on_device(tracers, fluxes, diff_east, diff_north, column_depth, grazers, groups, preference):
     tr_dev, levels, rows, cols = tracers.shape
     parts = lax.axis_size("tracer")
-    if not (cols == 128 and rows * levels == cols and levels == 2 * SUB and rows % SUB == 0):
+    if not (cols == 128 and rows == SUB and levels == 2 * SUB and tr_dev % 2 == 0):
         return plain(
             tracers, fluxes, diff_east, diff_north, column_depth, grazers, groups, preference
         )
@@ -736,9 +751,8 @@
         [field, strips, mine, other, column_depth, diff_east, diff_north],
     )
     messages = neighbours(*messages)
-    messages = messages[0], messages[1], messages[3], messages[2]
     part, inner = call(
-        functools.partial(inside_kernel, g, INSIDE, True),
+        functools.partial(inside_kernel, g, INSIDE),
         [cells, g.inner.rows],
         [field, mine, other, column_depth, diff_east, diff_north],
     )
@@ -757,22 +771,19 @@
     )
     prey = all_prey(prey)
     messages = neighbours(*messages)
-    field, part = call(
-        functools.partial(inside_kernel, g, INSIDE, False), [cells, cells], [field, tend, inner],
-        cost=LONG,
-    )
-    (part,) = call(
-        functools.partial(border_two_kernel, g, FINISH),
+    messages = messages[0], messages[1], messages[3], messages[2]
+    (field,) = call(
+        functools.partial(transport_two_kernel, g, total, BOTH),
         [cells],
-        [field, part, *messages[:2], inner, outer],
-        cost=LONG,
+        [field, tend, *messages[:2], inner, outer, grazers, taste, *prey],
+        scratch=[cells, cells, g.tile],
     )
     (out,) = call(
-        functools.partial(result_kernel, g, total, LAST),
+        functools.partial(result_kernel, g, LAST),
         [cells],
-        [field, part, strips, *messages[2:], ends, grazers, taste, *prey],
+        [field, strips, *messages[2:], ends],
         far_out=True,
-        scratch=[g.tile, g.T * g.SR, cells, copies],
+        scratch=[g.T * g.SR, cells, copies],
     )
     return out.reshape(tracers.shape)
 

time: 28.4 us -> 28.4 us (level)
  starting transfers between devices: 17.6 us -> 17.9 us
    ppermute x8, starting transfers between devices: 14.7 us -> 15.1 us  [pair_swap(): return lax.ppermute(values, axis, pairs)]
    pallas_call x8 -> x7, Pallas kernels: 9.82 us -> 9.55 us  [call(): pl.pallas_call(body, out_shape=[jax.ShapeDtypeStruct((rows, 128), jnp.flo...]
  transfers between devices with their start and end apart: 11 -> 11, of which waited for: 1 -> 1; matrix products, arithmetic and copies ran while one was open for 0% -> 0% of each run, Pallas kernels for 26% -> 25%
where the time goes in v7:
time: 28.4 us; the launch traced here: 28.1 us
  starting transfers between devices  17.9 us (63%)
  Pallas kernels  9.55 us (34%)
  local copies, waits for them, and re-layouts  0.34 us (1%)
    ppermute x8, starting transfers between devices, pair_swap(): return lax.ppermute(values, axis, pairs)  15.1 us
    pallas_call x7, Pallas kernels, call(): pl.pallas_call(body, out_shape=[jax.ShapeDtypeStruct((rows, 128), jnp.flo...  9.55 us
    ppermute x3, starting transfers between devices, tracer_swap(): return lax.ppermute(values, 'tracer', [(0, 1), (1, 0)])  2.85 us
  transfers between devices with their start and end apart: 11, of which 1 were waited for; matrix products, arithmetic and copies ran while one was open for 0% of the time, Pallas kernels for 25%

profile of v7, /device:TPU:9, one launch (start us, length us, event | category | flops | bytes accessed | tf_op | source)
XLA Modules:
  0.0 28.1 jit_solution(3090210268939930245)
XLA Ops:
  0.0 1.2 %collective-permute-start = (f32[192,128]{1,0:T(8,128)}, f32[192,128]{1,0:T(8,128)S(1)}, u32[]{:S(2)}, u32[]{:S(2)}) collective-permute-start(f32[192,128]{1,0:T(8,128)} %bitcast.4), channel_id=1, source_target_pairs={{0,16},{16,0},{1,17},{17,1},{2,18},{18,2},{3,19},{19,3},{4,20},{20... | collective-permute-start | bytes 294920 | tf_op jit(solution)/shard_map/ppermute | solution.py:703
  1.2 0.0 copy-start
  1.2 0.0 copy-start.3
  1.2 0.0 copy-start.4
  1.2 2.1 %shard_map.82 = (f32[1536,128]{1,0:T(8,128)S(1)}, f32[192,128]{1,0:T(8,128)S(1)}, f32[424,128]{1,0:T(8,128)S(1)}, f32[96,128]{1,0:T(8,128)S(1)}) custom-call(f32[1536,128]{1,0:T(8,128)} %bitcast.10, s32[12]{0:T(128)} %groups_far.1, f32[16]{0:T(128)} %pref_far.1), custom_call_target="tpu_custom_call" | custom-call | tf_op jit(solution)/shard_map/pallas_call | solution.py:680
  3.3 0.0 copy-start.2
  3.3 0.3 %collective-permute-start.3 = (f32[424,128]{1,0:T(8,128)S(1)}, f32[424,128]{1,0:T(8,128)S(1)}, u32[]{:S(2)}, u32[]{:S(2)}) collective-permute-start(f32[424,128]{1,0:T(8,128)S(1)} %get-tuple-element.33.rest_0_), channel_id=1, source_target_pairs={{0,16},{16,0},{1,17},{17,1},{2,18},{18,2},{3,19},{19,3},{4,20},{20... | collective-permute-start | bytes 651272 | tf_op jit(solution)/shard_map/ppermute | solution.py:703
  3.6 0.1 collective-permute-done.other_ref
  3.7 0.0 copy-done
  3.7 0.0 copy-done.3
  3.7 0.0 copy-done.4
  3.7 0.3 %copy-done.2 = s32[8,128]{1,0:T(8,128)S(1)} copy-done((s32[8,128]{1,0:T(8,128)S(1)}, s32[8,128]{1,0:T(8,128)}, u32[]{:S(2)}) %copy-start.2) | copy-done | bytes 4120
  4.0 0.2 shard_map.84
  4.2 1.6 %collective-permute-start.1 = (f32[416,128]{1,0:T(8,128)S(1)}, f32[416,128]{1,0:T(8,128)S(1)}, u32[]{:S(2)}, u32[]{:S(2)}) collective-permute-start(f32[416,128]{1,0:T(8,128)S(1)} %get-tuple-element.29), channel_id=1, source_target_pairs={{0,4},{4,0},{8,12},{12,8},{1,5},{5,1},{9,13},{13,9},{2,6},{6,2},{1... | collective-permute-start | bytes 638984 | tf_op jit(solution)/shard_map/ppermute | solution.py:699
  5.8 3.0 %collective-permute-start.2 = (f32[416,128]{1,0:T(8,128)S(1)}, f32[416,128]{1,0:T(8,128)S(1)}, u32[]{:S(2)}, u32[]{:S(2)}) collective-permute-start(f32[416,128]{1,0:T(8,128)S(1)} %get-tuple-element.30), channel_id=1, source_target_pairs={{4,8},{8,4},{5,9},{9,5},{6,10},{10,6},{7,11},{11,7},{20,24},{24,20... | collective-permute-start | bytes 638984 | tf_op jit(solution)/shard_map/ppermute | solution.py:699
  8.8 0.0 copy-start.1
  8.8 0.2 collective-permute-start.4
  9.1 4.3 %collective-permute-start.5 = (f32[64,128]{1,0:T(8,128)S(1)}, f32[64,128]{1,0:T(8,128)S(1)}, u32[]{:S(2)}, u32[]{:S(2)}) collective-permute-start(f32[64,128]{1,0:T(8,128)S(1)} %get-tuple-element.38), channel_id=1, source_target_pairs={{1,2},{2,1},{5,6},{6,5},{9,10},{10,9},{13,14},{14,13},{17,18},{18,... | collective-permute-start | bytes 98312 | tf_op jit(solution)/shard_map/ppermute | solution.py:699
  13.4 1.7 %shard_map.83 = (f32[1536,128]{1,0:T(8,128)S(1)}, f32[1336,128]{1,0:T(8,128)S(1)}) custom-call(f32[1536,128]{1,0:T(8,128)S(1)} %get-tuple-element.26.field_ref, f32[192,128]{1,0:T(8,128)S(1)} %bitcast.6, f32[192,128]{1,0:T(8,128)S(1)} %collective-permute-done.other_ref, s32[8,128]{1,0:T(8,128)S(1)} %copy-done.2, f32[8,128]{1,0:T(8,128)S(1)} %copy-done.3, ...), custom_call_target="tpu_custom_call" | custom-call | tf_op jit(solution)/shard_map/pallas_call | solution.py:680
  15.1 0.0 collective-permute-done.3.rest_1_
  15.1 0.0 collective-permute-done.1.xev_ref
  15.1 0.0 collective-permute-done.2.xod_ref
  15.1 0.0 copy-done.1
  15.1 1.0 %shard_map.85 = (f32[1536,128]{1,0:T(8,128)S(1)}, f32[192,128]{1,0:T(8,128)S(1)}, f32[128,128]{1,0:T(8,128)S(1)}, f32[136,128]{1,0:T(8,128)S(1)}) custom-call(f32[1536,128]{1,0:T(8,128)S(1)} %get-tuple-element.26.field_ref, f32[1536,128]{1,0:T(8,128)S(1)} %get-tuple-element.27.part_ref, f32[416,128]{1,0:T(8,128)S(1)} %collective-permute-done.1.xev_ref, ...), custom_call_target="tpu_custom_call" | custom-call | tf_op jit(solution)/shard_map/pallas_call | solution.py:680
  16.1 0.0 collective-permute-done.4.yev_ref
  16.1 0.0 collective-permute-done.5.yod_ref
  16.1 0.8 %shard_map.86 = (f32[384,128]{1,0:T(8,128)S(1)}, f32[384,128]{1,0:T(8,128)S(1)}, f32[48,128]{1,0:T(8,128)S(1)}, f32[192,128]{1,0:T(8,128)S(1)}, f32[128,128]{1,0...) custom-call(f32[1536,128]{1,0:T(8,128)S(1)} %get-tuple-element.34.field_ref, ...), custom_call_target="tpu_custom_call" | custom-call | tf_op jit(solution)/shard_map/pallas_call | solution.py:680
  16.9 0.1 collective-permute-start.6
  17.0 3.1 %collective-permute-start.7 = (f32[384,128]{1,0:T(8,128)S(1)}, f32[384,128]{1,0:T(8,128)S(1)}, u32[]{:S(2)}, u32[]{:S(2)}) collective-permute-start(f32[384,128]{1,0:T(8,128)S(1)} %get-tuple-element.41), channel_id=1, source_target_pairs={{4,8},{8,4},{5,9},{9,5},{6,10},{10,6},{7,11},{11,7},{20,24},{24,20... | collective-permute-start | bytes 589832 | tf_op jit(solution)/shard_map/ppermute | solution.py:699
  20.1 1.3 %collective-permute-start.8 = (f32[128,128]{1,0:T(8,128)S(1)}, f32[128,128]{1,0:T(8,128)S(1)}, u32[]{:S(2)}, u32[]{:S(2)}) collective-permute-start(f32[128,128]{1,0:T(8,128)S(1)} %get-tuple-element.43.rest_0_), channel_id=1, source_target_pairs={{0,16},{16,0},{1,17},{17,1},{2,18},{18,2},{3,19},{19,3},{4,20},{20... | collective-permute-start | bytes 196616 | tf_op jit(solution)/shard_map/ppermute | solution.py:703
  21.4 0.0 collective-permute-start.10
  21.4 2.8 %collective-permute-start.9 = (f32[48,128]{1,0:T(8,128)S(1)}, f32[48,128]{1,0:T(8,128)S(1)}, u32[]{:S(2)}, u32[]{:S(2)}) collective-permute-start(f32[48,128]{1,0:T(8,128)S(1)} %get-tuple-element.45), channel_id=1, source_target_pairs={{1,2},{2,1},{5,6},{6,5},{9,10},{10,9},{13,14},{14,13},{17,18},{18,... | collective-permute-start | bytes 73736 | tf_op jit(solution)/shard_map/ppermute | solution.py:699
  24.2 0.0 collective-permute-done.8.rest_1_
  24.2 0.0 collective-permute-done.6.xev_ref
  24.2 0.0 collective-permute-done.7.xod_ref
  24.2 2.2 %shard_map.87.field_ref = f32[1536,128]{1,0:T(8,128)S(1)} custom-call(f32[1536,128]{1,0:T(8,128)S(1)} %get-tuple-element.34.field_ref, f32[192,128]{1,0:T(8,128)S(1)} %get-tuple-element.39.tend_ref, f32[384,128]{1,0:T(8,128)S(1)} %collective-permute-done.6.xev_ref, f32[384,128]{1,0:T(8,128)S(1)} %collective-permute-done.7.xod_ref, ...), custom_call_target="tpu_custom_call" | custom-call | tf_op jit(solution)/shard_map/pallas_call | solution.py:680
  26.4 0.0 collective-permute-done.10.yev_ref
  26.4 0.0 collective-permute-done.9.yod_ref
  26.4 1.6 %shard_map.88 = f32[1536,128]{1,0:T(8,128)} custom-call(f32[1536,128]{1,0:T(8,128)S(1)} %shard_map.87.field_ref, f32[192,128]{1,0:T(8,128)S(1)} %get-tuple-element.44.strips_ref, f32[48,128]{1,0:T(8,128)S(1)} %collective-permute-done.9.yod_ref, f32[48,128]{1,0:T(8,128)S(1)} %collective-permute-done.10.yev_ref, f32[160,128]{1,0:T(8,128)S(1)} %get-tuple-element.46.ends), custom_call_target="tpu_custom_call" | custom-call | tf_op jit(solution)/shard_map/pallas_call | solution.py:680
Async XLA Ops:
  0.0 3.7 %collective-permute-start = (f32[192,128]{1,0:T(8,128)}, f32[192,128]{1,0:T(8,128)S(1)}, u32[]{:S(2)}, u32[]{:S(2)}) collective-permute-start(f32[192,128]{1,0:T(8,128)} %bitcast.4), channel_id=1, source_target_pairs={{0,16},{16,0},{1,17},{17,1},{2,18},{18,2},{3,19},{19,3},{4,20},{20... | collective-permute-start | bytes 294920 | tf_op jit(solution)/shard_map/ppermute | solution.py:703
  1.2 2.4 %copy-start = (f32[3,8,8,128]{3,2,1,0:T(8,128)S(1)}, f32[3,8,8,128]{3,2,1,0:T(8,128)}, u32[]{:S(2)}) copy-start(f32[3,8,8,128]{3,2,1,0:T(8,128)} %param.9) | copy-start | bytes 294916
  1.2 2.4 %copy-start.3 = (f32[8,128]{1,0:T(8,128)S(1)}, f32[8,128]{1,0:T(8,128)}, u32[]{:S(2)}) copy-start(f32[8,128]{1,0:T(8,128)} %east_ref.5) | copy-start | bytes 12292
  1.2 2.4 %copy-start.4 = (f32[8,128]{1,0:T(8,128)S(1)}, f32[8,128]{1,0:T(8,128)}, u32[]{:S(2)}) copy-start(f32[8,128]{1,0:T(8,128)} %north_ref.3) | copy-start | bytes 12292
  3.3 0.7 %copy-start.2 = (s32[8,128]{1,0:T(8,128)S(1)}, s32[8,128]{1,0:T(8,128)}, u32[]{:S(2)}) copy-start(s32[8,128]{1,0:T(8,128)} %depth_ref.5) | copy-start | bytes 12292
  3.3 11.7 %collective-permute-start.3 = (f32[424,128]{1,0:T(8,128)S(1)}, f32[424,128]{1,0:T(8,128)S(1)}, u32[]{:S(2)}, u32[]{:S(2)}) collective-permute-start(f32[424,128]{1,0:T(8,128)S(1)} %get-tuple-element.33.rest_0_), channel_id=1, source_target_pairs={{0,16},{16,0},{1,17},{17,1},{2,18},{18,2},{3,19},{19,3},{4,20},{20... | collective-permute-start | bytes 651272 | tf_op jit(solution)/shard_map/ppermute | solution.py:703
  4.2 10.9 %collective-permute-start.1 = (f32[416,128]{1,0:T(8,128)S(1)}, f32[416,128]{1,0:T(8,128)S(1)}, u32[]{:S(2)}, u32[]{:S(2)}) collective-permute-start(f32[416,128]{1,0:T(8,128)S(1)} %get-tuple-element.29), channel_id=1, source_target_pairs={{0,4},{4,0},{8,12},{12,8},{1,5},{5,1},{9,13},{13,9},{2,6},{6,2},{1... | collective-permute-start | bytes 638984 | tf_op jit(solution)/shard_map/ppermute | solution.py:699
  5.8 9.3 %collective-permute-start.2 = (f32[416,128]{1,0:T(8,128)S(1)}, f32[416,128]{1,0:T(8,128)S(1)}, u32[]{:S(2)}, u32[]{:S(2)}) collective-permute-start(f32[416,128]{1,0:T(8,128)S(1)} %get-tuple-element.30), channel_id=1, source_target_pairs={{4,8},{8,4},{5,9},{9,5},{6,10},{10,6},{7,11},{11,7},{20,24},{24,20... | collective-permute-start | bytes 638984 | tf_op jit(solution)/shard_map/ppermute | solution.py:699
  8.8 6.3 %copy-start.1 = (f32[16,8,128]{2,1,0:T(8,128)S(1)}, f32[16,8,128]{2,1,0:T(8,128)}, u32[]{:S(2)}) copy-start(f32[16,8,128]{2,1,0:T(8,128)} %param.13) | copy-start | bytes 196612
  8.8 7.3 %collective-permute-start.4 = (f32[64,128]{1,0:T(8,128)S(1)}, f32[64,128]{1,0:T(8,128)S(1)}, u32[]{:S(2)}, u32[]{:S(2)}) collective-permute-start(f32[64,128]{1,0:T(8,128)S(1)} %get-tuple-element.38), channel_id=1, source_target_pairs={{0,1},{1,0},{2,3},{3,2},{4,5},{5,4},{6,7},{7,6},{8,9},{9,8},{10,11... | collective-permute-start | bytes 98312 | tf_op jit(solution)/shard_map/ppermute | solution.py:699
  9.1 7.1 %collective-permute-start.5 = (f32[64,128]{1,0:T(8,128)S(1)}, f32[64,128]{1,0:T(8,128)S(1)}, u32[]{:S(2)}, u32[]{:S(2)}) collective-permute-start(f32[64,128]{1,0:T(8,128)S(1)} %get-tuple-element.38), channel_id=1, source_target_pairs={{1,2},{2,1},{5,6},{6,5},{9,10},{10,9},{13,14},{14,13},{17,18},{18,... | collective-permute-start | bytes 98312 | tf_op jit(solution)/shard_map/ppermute | solution.py:699
  16.9 7.3 %collective-permute-start.6 = (f32[384,128]{1,0:T(8,128)S(1)}, f32[384,128]{1,0:T(8,128)S(1)}, u32[]{:S(2)}, u32[]{:S(2)}) collective-permute-start(f32[384,128]{1,0:T(8,128)S(1)} %get-tuple-element.40), channel_id=1, source_target_pairs={{0,4},{4,0},{8,12},{12,8},{1,5},{5,1},{9,13},{13,9},{2,6},{6,2},{1... | collective-permute-start | bytes 589832 | tf_op jit(solution)/shard_map/ppermute | solution.py:699
  17.0 7.2 %collective-permute-start.7 = (f32[384,128]{1,0:T(8,128)S(1)}, f32[384,128]{1,0:T(8,128)S(1)}, u32[]{:S(2)}, u32[]{:S(2)}) collective-permute-start(f32[384,128]{1,0:T(8,128)S(1)} %get-tuple-element.41), channel_id=1, source_target_pairs={{4,8},{8,4},{5,9},{9,5},{6,10},{10,6},{7,11},{11,7},{20,24},{24,20... | collective-permute-start | bytes 589832 | tf_op jit(solution)/shard_map/ppermute | solution.py:699
  20.1 4.1 %collective-permute-start.8 = (f32[128,128]{1,0:T(8,128)S(1)}, f32[128,128]{1,0:T(8,128)S(1)}, u32[]{:S(2)}, u32[]{:S(2)}) collective-permute-start(f32[128,128]{1,0:T(8,128)S(1)} %get-tuple-element.43.rest_0_), channel_id=1, source_target_pairs={{0,16},{16,0},{1,17},{17,1},{2,18},{18,2},{3,19},{19,3},{4,20},{20... | collective-permute-start | bytes 196616 | tf_op jit(solution)/shard_map/ppermute | solution.py:703
  21.4 5.0 %collective-permute-start.10 = (f32[48,128]{1,0:T(8,128)S(1)}, f32[48,128]{1,0:T(8,128)S(1)}, u32[]{:S(2)}, u32[]{:S(2)}) collective-permute-start(f32[48,128]{1,0:T(8,128)S(1)} %get-tuple-element.45), channel_id=1, source_target_pairs={{0,1},{1,0},{2,3},{3,2},{4,5},{5,4},{6,7},{7,6},{8,9},{9,8},{10,11... | collective-permute-start | bytes 73736 | tf_op jit(solution)/shard_map/ppermute | solution.py:699
  21.4 5.0 %collective-permute-start.9 = (f32[48,128]{1,0:T(8,128)S(1)}, f32[48,128]{1,0:T(8,128)S(1)}, u32[]{:S(2)}, u32[]{:S(2)}) collective-permute-start(f32[48,128]{1,0:T(8,128)S(1)} %get-tuple-element.45), channel_id=1, source_target_pairs={{1,2},{2,1},{5,6},{6,5},{9,10},{10,9},{13,14},{14,13},{17,18},{18,... | collective-permute-start | bytes 73736 | tf_op jit(solution)/shard_map/ppermute | solution.py:699

commit v8 on v7

--- a/solution.py
+++ b/solution.py
@@ -10,7 +10,7 @@
 STEPS = 2
 SUB = 8
 LIM = 48 * 1024 * 1024
-INSIDE, FINISH, BOTH, LAST = 3, 3, 3, 3
+INSIDE, FINISH, BOTH, LAST = 3, 3, 3, 6
 
 
 def with_halo(cells, sides, width):
@@ -244,18 +244,26 @@
         body(t)
 
 
-def flux_reader(g, mine_ref, other_ref):
+def level_rows(g, r, lh, base=0):
+    return pl.ds(base + lh * g.R + r, SUB, stride=g.LH * g.R)
+
+
+def flux_reader(g, fluxes_ref):
+    def flux(dim, r, lh):
+        return fluxes_ref[level_rows(g, r, lh, dim * g.tile), :]
+
+    return flux
+
+
+def join_fluxes(g, mine_ref, other_ref, out_ref):
     first = lax.axis_index("tracer") == 0
     single = lax.axis_size("tracer") != 2
-
-    def flux(dim, r, lh):
-        at = pl.ds(dim * g.R * SUB + r, SUB, stride=g.R)
-        a, b = mine_ref[at, :], other_ref[at, :]
-        if single:
-            return (a, b)[lh]
-        return jnp.where(first, (a, b)[lh], (b, a)[lh])
-
-    return flux
+    some = g.R * SUB
+    for dim in range(3):
+        a, b = (ref[dim * some : (dim + 1) * some, :] for ref in (mine_ref, other_ref))
+        at = dim * g.tile
+        out_ref[at : at + some, :] = a if single else jnp.where(first, a, b)
+        out_ref[at + some : at + 2 * some, :] = b if single else jnp.where(first, b, a)
 
 
 def load_kernel(
@@ -289,7 +297,7 @@
         for r in range(g.R):
             for lh in range(g.LH):
                 at = (r * g.LH + lh) * SUB
-                v = landed[pl.ds(base + lh * SUB * g.R + r, SUB, stride=g.R), :]
+                v = landed[level_rows(g, r, lh, base), :]
                 field_ref[pl.ds(base + at, SUB), :] = v
                 parts.append(v)
                 prey_ref[at : at + SUB, :] += taste * v
@@ -301,10 +309,11 @@
 
 def first_messages_kernel(
     g, field_ref, strips_ref, mine_ref, other_ref, depth_ref, east_ref, north_ref,
-    xev_ref, xod_ref, y_ref, extra_ref,
+    xev_ref, xod_ref, y_ref, extra_ref, fluxes_ref,
 ):
     x_even = is_even("gx")
-    flux = flux_reader(g, mine_ref, other_ref)
+    join_fluxes(g, mine_ref, other_ref, fluxes_ref)
+    flux = flux_reader(g, fluxes_ref)
     zero = jnp.zeros((SUB, 128), jnp.float32)
 
     def put(at, low, high):
@@ -334,7 +343,7 @@
 
 
 def wet_levels(g, depths):
-    level = [(sublanes() + SUB * lh).astype(jnp.float32) for lh in range(g.LH)]
+    level = [(g.LH * sublanes() + lh).astype(jnp.float32) for lh in range(g.LH)]
     return [[level[lh] < d for lh in range(g.LH)] for d in depths]
 
 
@@ -346,7 +355,7 @@
     for r in range(g.R):
         tab.set(cf, "kx", r + 1, 2.0 * spread(east, r))
         tab.set(cf, "ky", r, 2.0 * roll(spread(north, r), 1, 1))
-        flux_z = [roll(flux(2, r, lh), 1, 0) for lh in range(g.LH)]
+        flux_z = [flux(2, r, lh) for lh in range(g.LH)]
         for lh in range(g.LH):
             k, here = r * g.LH + lh, wet[r][lh]
             if r:
@@ -357,7 +366,7 @@
             tab.set_open(cf, "y", k, opened)
             tab.set_flux(cf, "y", k, opened, roll(flux(1, r, lh), 1, 1))
             opened = here if lh else here & (sub > 0)
-            above = jnp.where(sub == 0, flux_z[lh - 1], flux_z[lh]) if lh else flux_z[lh]
+            above = flux_z[lh - 1] if lh else roll(flux_z[-1], 1, 0)
             tab.set_open(cf, "z", k, opened)
             tab.set_flux(cf, "z", k, opened, above)
 
@@ -379,7 +388,7 @@
 def strip_coefficients(g, cf, extra_y, extra_ref):
     tab, lane = g.ends, lanes()
     half = (lane // WIDE) % g.LH
-    level = (sublanes() + SUB * half).astype(jnp.float32)
+    level = (g.LH * sublanes() + half).astype(jnp.float32)
     for i in range(g.NV):
         full = []
         for which in range(3):
@@ -402,21 +411,16 @@
 
 
 def inside(g, cf, field_ref, part_ref, tend_ref=None, whole_ref=None):
-    sub = sublanes()
-    ends, top, bottom = end_lanes(), sub == 0, sub == SUB - 1
+    ends = end_lanes()
 
     def coef(name, index):
         return g.inner.get(cf, name, index)
 
     def shift_down(v):
-        rolled = [roll(x, 1, 0) for x in v]
-        return rolled[:1] + [
-            jnp.where(top, rolled[i - 1], rolled[i]) for i in range(1, g.LH)
-        ]
+        return [roll(v[-1], 1, 0), *v[:-1]]
 
     def shift_up(v):
-        rolled = [roll(x, -1, 0) for x in v]
-        return [jnp.where(bottom, rolled[(i + 1) % g.LH], rolled[i]) for i in range(g.LH)]
+        return [*v[1:], roll(v[0], -1, 0)]
 
     def one(t):
         base = pl.multiple_of(t * g.tile, g.tile)
@@ -449,10 +453,10 @@
 
 
 def inside_kernel(
-    g, ahead, field_ref, mine_ref, other_ref, depth_ref, east_ref, north_ref, part_ref, cf
+    g, ahead, field_ref, fluxes_ref, depth_ref, east_ref, north_ref, part_ref, cf
 ):
     inner_coefficients(
-        g, cf, flux_reader(g, mine_ref, other_ref), depth_ref[...].astype(jnp.float32),
+        g, cf, flux_reader(g, fluxes_ref), depth_ref[...].astype(jnp.float32),
         east_ref[...], north_ref[...],
     )
     each_tracer(g, ahead, inside(g, cf, field_ref, part_ref))
@@ -493,7 +497,7 @@
         for lh in range(g.LH):
             at = rows8(r * g.LH + lh)
             prey = sum(ref[at, :] for ref in prey_refs)
-            grazers = grazers_ref[pl.ds(lh * SUB * g.R + r, SUB, stride=g.R), :]
+            grazers = grazers_ref[level_rows(g, r, lh), :]
             factor[at, :] = grazers / (1.0 + 4.0 * prey / total)
 
 
@@ -548,13 +552,13 @@
 
 def border_kernel(
     g, total, ahead,
-    field_ref, part_ref, xev_ref, xod_ref, inner, mine_ref, other_ref, depth_ref, east_ref,
+    field_ref, part_ref, xev_ref, xod_ref, inner, fluxes_ref, depth_ref, east_ref,
     grazers_ref, taste_ref, *rest,
 ):
     prey_refs, (out_ref, strips_ref, prey_ref, outer, factor) = rest[:-5], rest[-5:]
     x_sides = reader(is_even("gx"), xev_ref, xod_ref)
     outer_coefficients(
-        g, outer, lambda i: x_sides(g.T * 2 * g.LH + i), flux_reader(g, mine_ref, other_ref),
+        g, outer, lambda i: x_sides(g.T * 2 * g.LH + i), flux_reader(g, fluxes_ref),
         depth_ref[...].astype(jnp.float32), east_ref[...],
     )
     set_factor(g, total, factor, grazers_ref, prey_refs)
@@ -663,7 +667,7 @@
             for lh in range(g.LH):
                 k = r * g.LH + lh
                 new = field_ref[rows8(t * g.K + k), :] + end_columns(g, tend_ref, t, k)
-                leaving[pl.ds(base + lh * SUB * g.R + r, SUB, stride=g.R), :] = new
+                leaving[level_rows(g, r, lh, base), :] = new
         departure(t).start()
 
     each_tracer(g, ahead, one)
@@ -745,21 +749,21 @@
     prey = all_prey(prey)
     x_rows = g.T * 2 * g.L
     x_more = x_rows + g.L + 2 * SUB
-    *messages, extra = call(
+    *messages, extra, fluxes = call(
         functools.partial(first_messages_kernel, g),
-        [x_more, x_more, g.my1 * SUB, 3 * g.SR],
+        [x_more, x_more, g.my1 * SUB, 3 * g.SR, 3 * g.tile],
         [field, strips, mine, other, column_depth, diff_east, diff_north],
     )
     messages = neighbours(*messages)
     part, inner = call(
         functools.partial(inside_kernel, g, INSIDE),
         [cells, g.inner.rows],
-        [field, mine, other, column_depth, diff_east, diff_north],
+        [field, fluxes, column_depth, diff_east, diff_north],
     )
     field, next_strips, next_prey, outer = call(
         functools.partial(border_kernel, g, total, FINISH),
         [cells, g.T * g.SR, g.tile, g.outer.rows],
-        [field, part, *messages[:2], inner, mine, other, column_depth, diff_east, grazers, taste,
+        [field, part, *messages[:2], inner, fluxes, column_depth, diff_east, grazers, taste,
          *prey],
         scratch=[g.tile],
     )

time: 28.4 us -> 28.2 us (level)
  transfers between devices with their start and end apart: 11 -> 11, of which waited for: 1 -> 0; matrix products, arithmetic and copies ran while one was open for 0% -> 0% of each run, Pallas kernels for 25% -> 26%
where the time goes in v8:
time: 28.2 us; the launch traced here: 28 us
  starting transfers between devices  17.9 us (63%)
  Pallas kernels  9.45 us (34%)
  local copies, waits for them, and re-layouts  0.39 us (1%)
    ppermute x8, starting transfers between devices, pair_swap(): return lax.ppermute(values, axis, pairs)  15.1 us
    pallas_call x7, Pallas kernels, call(): pl.pallas_call(body, out_shape=[jax.ShapeDtypeStruct((rows, 128), jnp.flo...  9.45 us
    ppermute x3, starting transfers between devices, tracer_swap(): return lax.ppermute(values, 'tracer', [(0, 1), (1, 0)])  2.84 us
  transfers between devices with their start and end apart: 11, of which 0 were waited for; matrix products, arithmetic and copies ran while one was open for 0% of the time, Pallas kernels for 26%

profile of v8, /device:TPU:9, one launch (start us, length us, event | category | flops | bytes accessed | tf_op | source)
XLA Modules:
  0.0 28.0 jit_solution(7845958303535256993)
XLA Ops:
  0.0 1.2 %collective-permute-start = (f32[192,128]{1,0:T(8,128)}, f32[192,128]{1,0:T(8,128)S(1)}, u32[]{:S(2)}, u32[]{:S(2)}) collective-permute-start(f32[192,128]{1,0:T(8,128)} %bitcast.6), channel_id=1, source_target_pairs={{0,16},{16,0},{1,17},{17,1},{2,18},{18,2},{3,19},{19,3},{4,20},{20... | collective-permute-start | bytes 294920 | tf_op jit(solution)/shard_map/ppermute | solution.py:707
  1.2 0.0 copy-start.1
  1.2 0.0 copy-start.3
  1.2 0.0 copy-start.4
  1.2 2.1 %shard_map.82 = (f32[1536,128]{1,0:T(8,128)S(1)}, f32[192,128]{1,0:T(8,128)S(1)}, f32[424,128]{1,0:T(8,128)S(1)}, f32[96,128]{1,0:T(8,128)S(1)}) custom-call(f32[1536,128]{1,0:T(8,128)} %bitcast.8, s32[12]{0:T(128)} %groups_far.1, f32[16]{0:T(128)} %pref_far.1), custom_call_target="tpu_custom_call" | custom-call | tf_op jit(solution)/shard_map/pallas_call | solution.py:684
  3.4 0.0 copy-start.2
  3.4 0.3 %collective-permute-start.3 = (f32[424,128]{1,0:T(8,128)S(1)}, f32[424,128]{1,0:T(8,128)S(1)}, u32[]{:S(2)}, u32[]{:S(2)}) collective-permute-start(f32[424,128]{1,0:T(8,128)S(1)} %get-tuple-element.35.rest_0_), channel_id=1, source_target_pairs={{0,16},{16,0},{1,17},{17,1},{2,18},{18,2},{3,19},{19,3},{4,20},{20... | collective-permute-start | bytes 651272 | tf_op jit(solution)/shard_map/ppermute | solution.py:707
  3.7 0.0 collective-permute-done.other_ref
  3.7 0.0 copy-done.1
  3.7 0.0 copy-done.3
  3.7 0.0 copy-done.4
  3.7 0.4 %copy-done.2 = s32[8,128]{1,0:T(8,128)S(1)} copy-done((s32[8,128]{1,0:T(8,128)S(1)}, s32[8,128]{1,0:T(8,128)}, u32[]{:S(2)}) %copy-start.2) | copy-done | bytes 4120
  4.1 0.2 shard_map.83
  4.3 1.5 %collective-permute-start.1 = (f32[416,128]{1,0:T(8,128)S(1)}, f32[416,128]{1,0:T(8,128)S(1)}, u32[]{:S(2)}, u32[]{:S(2)}) collective-permute-start(f32[416,128]{1,0:T(8,128)S(1)} %get-tuple-element.31), channel_id=1, source_target_pairs={{0,4},{4,0},{8,12},{12,8},{1,5},{5,1},{9,13},{13,9},{2,6},{6,2},{1... | collective-permute-start | bytes 638984 | tf_op jit(solution)/shard_map/ppermute | solution.py:703
  5.8 3.0 %collective-permute-start.2 = (f32[416,128]{1,0:T(8,128)S(1)}, f32[416,128]{1,0:T(8,128)S(1)}, u32[]{:S(2)}, u32[]{:S(2)}) collective-permute-start(f32[416,128]{1,0:T(8,128)S(1)} %get-tuple-element.32), channel_id=1, source_target_pairs={{4,8},{8,4},{5,9},{9,5},{6,10},{10,6},{7,11},{11,7},{20,24},{24,20... | collective-permute-start | bytes 638984 | tf_op jit(solution)/shard_map/ppermute | solution.py:703
  8.8 0.2 collective-permute-start.4
  9.1 4.3 %collective-permute-start.5 = (f32[64,128]{1,0:T(8,128)S(1)}, f32[64,128]{1,0:T(8,128)S(1)}, u32[]{:S(2)}, u32[]{:S(2)}) collective-permute-start(f32[64,128]{1,0:T(8,128)S(1)} %get-tuple-element.40), channel_id=1, source_target_pairs={{1,2},{2,1},{5,6},{6,5},{9,10},{10,9},{13,14},{14,13},{17,18},{18,... | collective-permute-start | bytes 98312 | tf_op jit(solution)/shard_map/ppermute | solution.py:703
  13.4 0.0 copy-start
  13.4 1.5 %shard_map.84 = (f32[1536,128]{1,0:T(8,128)S(1)}, f32[1336,128]{1,0:T(8,128)S(1)}) custom-call(f32[1536,128]{1,0:T(8,128)S(1)} %get-tuple-element.27.field_ref, f32[384,128]{1,0:T(8,128)S(1)} %get-tuple-element.29.fluxes_ref, s32[8,128]{1,0:T(8,128)S(1)} %copy-done.2, f32[8,128]{1,0:T(8,128)S(1)} %copy-done.3, f32[8,128]{1,0:T(8,128)S(1)} %copy-done.4), custom_call_target="tpu_custom_call" | custom-call | tf_op jit(solution)/shard_map/pallas_call | solution.py:684
  15.0 0.0 collective-permute-done.3.rest_1_
  15.0 0.0 collective-permute-done.1.xev_ref
  15.0 0.0 collective-permute-done.2.xod_ref
  15.0 0.0 copy-done
  15.0 1.0 %shard_map.85 = (f32[1536,128]{1,0:T(8,128)S(1)}, f32[192,128]{1,0:T(8,128)S(1)}, f32[128,128]{1,0:T(8,128)S(1)}, f32[136,128]{1,0:T(8,128)S(1)}) custom-call(f32[1536,128]{1,0:T(8,128)S(1)} %get-tuple-element.27.field_ref, f32[1536,128]{1,0:T(8,128)S(1)} %get-tuple-element.30.part_ref, f32[416,128]{1,0:T(8,128)S(1)} %collective-permute-done.1.xev_ref, ...), custom_call_target="tpu_custom_call" | custom-call | tf_op jit(solution)/shard_map/pallas_call | solution.py:684
  16.0 0.0 collective-permute-done.4.yev_ref
  16.0 0.0 collective-permute-done.5.yod_ref
  16.0 0.8 %shard_map.86 = (f32[384,128]{1,0:T(8,128)S(1)}, f32[384,128]{1,0:T(8,128)S(1)}, f32[48,128]{1,0:T(8,128)S(1)}, f32[192,128]{1,0:T(8,128)S(1)}, f32[128,128]{1,0...) custom-call(f32[1536,128]{1,0:T(8,128)S(1)} %get-tuple-element.36.field_ref, ...), custom_call_target="tpu_custom_call" | custom-call | tf_op jit(solution)/shard_map/pallas_call | solution.py:684
  16.8 0.1 collective-permute-start.6
  16.9 3.1 %collective-permute-start.7 = (f32[384,128]{1,0:T(8,128)S(1)}, f32[384,128]{1,0:T(8,128)S(1)}, u32[]{:S(2)}, u32[]{:S(2)}) collective-permute-start(f32[384,128]{1,0:T(8,128)S(1)} %get-tuple-element.43), channel_id=1, source_target_pairs={{4,8},{8,4},{5,9},{9,5},{6,10},{10,6},{7,11},{11,7},{20,24},{24,20... | collective-permute-start | bytes 589832 | tf_op jit(solution)/shard_map/ppermute | solution.py:703
  20.0 1.3 %collective-permute-start.8 = (f32[128,128]{1,0:T(8,128)S(1)}, f32[128,128]{1,0:T(8,128)S(1)}, u32[]{:S(2)}, u32[]{:S(2)}) collective-permute-start(f32[128,128]{1,0:T(8,128)S(1)} %get-tuple-element.45.rest_0_), channel_id=1, source_target_pairs={{0,16},{16,0},{1,17},{17,1},{2,18},{18,2},{3,19},{19,3},{4,20},{20... | collective-permute-start | bytes 196616 | tf_op jit(solution)/shard_map/ppermute | solution.py:707
  21.3 0.0 collective-permute-start.10
  21.3 2.9 %collective-permute-start.9 = (f32[48,128]{1,0:T(8,128)S(1)}, f32[48,128]{1,0:T(8,128)S(1)}, u32[]{:S(2)}, u32[]{:S(2)}) collective-permute-start(f32[48,128]{1,0:T(8,128)S(1)} %get-tuple-element.47), channel_id=1, source_target_pairs={{1,2},{2,1},{5,6},{6,5},{9,10},{10,9},{13,14},{14,13},{17,18},{18,... | collective-permute-start | bytes 73736 | tf_op jit(solution)/shard_map/ppermute | solution.py:703
  24.2 0.0 collective-permute-done.8.rest_1_
  24.2 0.0 collective-permute-done.6.xev_ref
  24.2 0.0 collective-permute-done.7.xod_ref
  24.2 2.2 %shard_map.87.field_ref = f32[1536,128]{1,0:T(8,128)S(1)} custom-call(f32[1536,128]{1,0:T(8,128)S(1)} %get-tuple-element.36.field_ref, f32[192,128]{1,0:T(8,128)S(1)} %get-tuple-element.41.tend_ref, f32[384,128]{1,0:T(8,128)S(1)} %collective-permute-done.6.xev_ref, f32[384,128]{1,0:T(8,128)S(1)} %collective-permute-done.7.xod_ref, ...), custom_call_target="tpu_custom_call" | custom-call | tf_op jit(solution)/shard_map/pallas_call | solution.py:684
  26.4 0.0 collective-permute-done.10.yev_ref
  26.4 0.0 collective-permute-done.9.yod_ref
  26.4 1.5 %shard_map.88 = f32[1536,128]{1,0:T(8,128)} custom-call(f32[1536,128]{1,0:T(8,128)S(1)} %shard_map.87.field_ref, f32[192,128]{1,0:T(8,128)S(1)} %get-tuple-element.46.strips_ref, f32[48,128]{1,0:T(8,128)S(1)} %collective-permute-done.9.yod_ref, f32[48,128]{1,0:T(8,128)S(1)} %collective-permute-done.10.yev_ref, f32[160,128]{1,0:T(8,128)S(1)} %get-tuple-element.48.ends), custom_call_target="tpu_custom_call" | custom-call | tf_op jit(solution)/shard_map/pallas_call | solution.py:684
Async XLA Ops:
  0.0 3.7 %collective-permute-start = (f32[192,128]{1,0:T(8,128)}, f32[192,128]{1,0:T(8,128)S(1)}, u32[]{:S(2)}, u32[]{:S(2)}) collective-permute-start(f32[192,128]{1,0:T(8,128)} %bitcast.6), channel_id=1, source_target_pairs={{0,16},{16,0},{1,17},{17,1},{2,18},{18,2},{3,19},{19,3},{4,20},{20... | collective-permute-start | bytes 294920 | tf_op jit(solution)/shard_map/ppermute | solution.py:707
  1.2 2.5 %copy-start.1 = (f32[3,8,8,128]{3,2,1,0:T(8,128)S(1)}, f32[3,8,8,128]{3,2,1,0:T(8,128)}, u32[]{:S(2)}) copy-start(f32[3,8,8,128]{3,2,1,0:T(8,128)} %param.9) | copy-start | bytes 294916
  1.2 2.5 %copy-start.3 = (f32[8,128]{1,0:T(8,128)S(1)}, f32[8,128]{1,0:T(8,128)}, u32[]{:S(2)}) copy-start(f32[8,128]{1,0:T(8,128)} %east_ref.5) | copy-start | bytes 12292
  1.2 2.5 %copy-start.4 = (f32[8,128]{1,0:T(8,128)S(1)}, f32[8,128]{1,0:T(8,128)}, u32[]{:S(2)}) copy-start(f32[8,128]{1,0:T(8,128)} %north_ref.3) | copy-start | bytes 12292
  3.4 0.7 %copy-start.2 = (s32[8,128]{1,0:T(8,128)S(1)}, s32[8,128]{1,0:T(8,128)}, u32[]{:S(2)}) copy-start(s32[8,128]{1,0:T(8,128)} %depth_ref.5) | copy-start | bytes 12292
  3.4 11.6 %collective-permute-start.3 = (f32[424,128]{1,0:T(8,128)S(1)}, f32[424,128]{1,0:T(8,128)S(1)}, u32[]{:S(2)}, u32[]{:S(2)}) collective-permute-start(f32[424,128]{1,0:T(8,128)S(1)} %get-tuple-element.35.rest_0_), channel_id=1, source_target_pairs={{0,16},{16,0},{1,17},{17,1},{2,18},{18,2},{3,19},{19,3},{4,20},{20... | collective-permute-start | bytes 651272 | tf_op jit(solution)/shard_map/ppermute | solution.py:707
  4.3 10.6 %collective-permute-start.1 = (f32[416,128]{1,0:T(8,128)S(1)}, f32[416,128]{1,0:T(8,128)S(1)}, u32[]{:S(2)}, u32[]{:S(2)}) collective-permute-start(f32[416,128]{1,0:T(8,128)S(1)} %get-tuple-element.31), channel_id=1, source_target_pairs={{0,4},{4,0},{8,12},{12,8},{1,5},{5,1},{9,13},{13,9},{2,6},{6,2},{1... | collective-permute-start | bytes 638984 | tf_op jit(solution)/shard_map/ppermute | solution.py:703
  5.8 9.2 %collective-permute-start.2 = (f32[416,128]{1,0:T(8,128)S(1)}, f32[416,128]{1,0:T(8,128)S(1)}, u32[]{:S(2)}, u32[]{:S(2)}) collective-permute-start(f32[416,128]{1,0:T(8,128)S(1)} %get-tuple-element.32), channel_id=1, source_target_pairs={{4,8},{8,4},{5,9},{9,5},{6,10},{10,6},{7,11},{11,7},{20,24},{24,20... | collective-permute-start | bytes 638984 | tf_op jit(solution)/shard_map/ppermute | solution.py:703
  8.8 7.2 %collective-permute-start.4 = (f32[64,128]{1,0:T(8,128)S(1)}, f32[64,128]{1,0:T(8,128)S(1)}, u32[]{:S(2)}, u32[]{:S(2)}) collective-permute-start(f32[64,128]{1,0:T(8,128)S(1)} %get-tuple-element.40), channel_id=1, source_target_pairs={{0,1},{1,0},{2,3},{3,2},{4,5},{5,4},{6,7},{7,6},{8,9},{9,8},{10,11... | collective-permute-start | bytes 98312 | tf_op jit(solution)/shard_map/ppermute | solution.py:703
  9.1 7.0 %collective-permute-start.5 = (f32[64,128]{1,0:T(8,128)S(1)}, f32[64,128]{1,0:T(8,128)S(1)}, u32[]{:S(2)}, u32[]{:S(2)}) collective-permute-start(f32[64,128]{1,0:T(8,128)S(1)} %get-tuple-element.40), channel_id=1, source_target_pairs={{1,2},{2,1},{5,6},{6,5},{9,10},{10,9},{13,14},{14,13},{17,18},{18,... | collective-permute-start | bytes 98312 | tf_op jit(solution)/shard_map/ppermute | solution.py:703
  13.4 1.6 %copy-start = (f32[16,8,128]{2,1,0:T(8,128)S(1)}, f32[16,8,128]{2,1,0:T(8,128)}, u32[]{:S(2)}) copy-start(f32[16,8,128]{2,1,0:T(8,128)} %param.13) | copy-start | bytes 196612
  16.8 7.4 %collective-permute-start.6 = (f32[384,128]{1,0:T(8,128)S(1)}, f32[384,128]{1,0:T(8,128)S(1)}, u32[]{:S(2)}, u32[]{:S(2)}) collective-permute-start(f32[384,128]{1,0:T(8,128)S(1)} %get-tuple-element.42), channel_id=1, source_target_pairs={{0,4},{4,0},{8,12},{12,8},{1,5},{5,1},{9,13},{13,9},{2,6},{6,2},{1... | collective-permute-start | bytes 589832 | tf_op jit(solution)/shard_map/ppermute | solution.py:703
  16.9 7.3 %collective-permute-start.7 = (f32[384,128]{1,0:T(8,128)S(1)}, f32[384,128]{1,0:T(8,128)S(1)}, u32[]{:S(2)}, u32[]{:S(2)}) collective-permute-start(f32[384,128]{1,0:T(8,128)S(1)} %get-tuple-element.43), channel_id=1, source_target_pairs={{4,8},{8,4},{5,9},{9,5},{6,10},{10,6},{7,11},{11,7},{20,24},{24,20... | collective-permute-start | bytes 589832 | tf_op jit(solution)/shard_map/ppermute | solution.py:703
  20.0 4.2 %collective-permute-start.8 = (f32[128,128]{1,0:T(8,128)S(1)}, f32[128,128]{1,0:T(8,128)S(1)}, u32[]{:S(2)}, u32[]{:S(2)}) collective-permute-start(f32[128,128]{1,0:T(8,128)S(1)} %get-tuple-element.45.rest_0_), channel_id=1, source_target_pairs={{0,16},{16,0},{1,17},{17,1},{2,18},{18,2},{3,19},{19,3},{4,20},{20... | collective-permute-start | bytes 196616 | tf_op jit(solution)/shard_map/ppermute | solution.py:707
  21.3 5.1 %collective-permute-start.10 = (f32[48,128]{1,0:T(8,128)S(1)}, f32[48,128]{1,0:T(8,128)S(1)}, u32[]{:S(2)}, u32[]{:S(2)}) collective-permute-start(f32[48,128]{1,0:T(8,128)S(1)} %get-tuple-element.47), channel_id=1, source_target_pairs={{0,1},{1,0},{2,3},{3,2},{4,5},{5,4},{6,7},{7,6},{8,9},{9,8},{10,11... | collective-permute-start | bytes 73736 | tf_op jit(solution)/shard_map/ppermute | solution.py:703
  21.3 5.1 %collective-permute-start.9 = (f32[48,128]{1,0:T(8,128)S(1)}, f32[48,128]{1,0:T(8,128)S(1)}, u32[]{:S(2)}, u32[]{:S(2)}) collective-permute-start(f32[48,128]{1,0:T(8,128)S(1)} %get-tuple-element.47), channel_id=1, source_target_pairs={{1,2},{2,1},{5,6},{6,5},{9,10},{10,9},{13,14},{14,13},{17,18},{18,... | collective-permute-start | bytes 73736 | tf_op jit(solution)/shard_map/ppermute | solution.py:703

commit v9 on v8

--- a/solution.py
+++ b/solution.py
@@ -10,7 +10,7 @@
 STEPS = 2
 SUB = 8
 LIM = 48 * 1024 * 1024
-INSIDE, FINISH, BOTH, LAST = 3, 3, 3, 6
+INSIDE, FINISH, BOTH, LAST = 3, 3, 2, 6
 
 
 def with_halo(cells, sides, width):
@@ -125,6 +125,7 @@
             hx=(rows + 1) * self.LH, px=(rows + 1) * self.LH, mx=(rows + 1) * self.LH,
             kx=rows + 1, hy=self.K, py=self.K, my=self.K, ky=rows,
             hz=self.K, pz=self.K, mz=self.K,
+            hyu=self.K, pyu=self.K, myu=self.K, kyu=rows,
         )
         self.outer = Table(
             hx=4 * self.LH, px=2 * self.LH, mx=2 * self.LH, kx=1
@@ -351,10 +352,11 @@
     tab, sub = g.inner, sublanes()
     depths = [spread(depth, r) for r in range(g.R)]
     wet = wet_levels(g, depths)
-    wet_before = wet_levels(g, [roll(d, 1, 1) for d in depths])
+    wet_before, wet_after = (wet_levels(g, [roll(d, by, 1) for d in depths]) for by in (1, -1))
     for r in range(g.R):
         tab.set(cf, "kx", r + 1, 2.0 * spread(east, r))
         tab.set(cf, "ky", r, 2.0 * roll(spread(north, r), 1, 1))
+        tab.set(cf, "kyu", r, 2.0 * spread(north, r))
         flux_z = [flux(2, r, lh) for lh in range(g.LH)]
         for lh in range(g.LH):
             k, here = r * g.LH + lh, wet[r][lh]
@@ -365,6 +367,9 @@
             opened = here & wet_before[r][lh]
             tab.set_open(cf, "y", k, opened)
             tab.set_flux(cf, "y", k, opened, roll(flux(1, r, lh), 1, 1))
+            opened = here & wet_after[r][lh]
+            tab.set_open(cf, "yu", k, opened)
+            tab.set_flux(cf, "yu", k, opened, flux(1, r, lh))
             opened = here if lh else here & (sub > 0)
             above = flux_z[lh - 1] if lh else roll(flux_z[-1], 1, 0)
             tab.set_open(cf, "z", k, opened)
@@ -435,10 +440,20 @@
             news = []
             for k, c in zip(index, cells):
                 j = coef("hy", k) * (c - roll(c, 1, 1))
-                s = limited(j, roll(j, -1, 1))
-                flow = coef("py", k) * roll(c + s, 1, 1) + coef("my", k) * (c - s)
+                if whole_ref is None:
+                    j_up = roll(j, -1, 1)
+                else:
+                    j_up = coef("hyu", k) * (roll(c, -1, 1) - c)
+                s = limited(j, j_up)
+                left, right = c + s, c - s
+                flow = coef("py", k) * roll(left, 1, 1) + coef("my", k) * right
                 flow = flow - coef("ky", r) * j
-                news.append(c + jnp.where(ends, 0.0, flow - roll(flow, -1, 1)))
+                if whole_ref is None:
+                    flow_up = roll(flow, -1, 1)
+                else:
+                    flow_up = coef("pyu", k) * left + coef("myu", k) * roll(right, -1, 1)
+                    flow_up = flow_up - coef("kyu", r) * j_up
+                news.append(c + jnp.where(ends, 0.0, flow - flow_up))
             j = [coef("hz", k) * (c - a) for k, c, a in zip(index, cells, shift_down(cells))]
             s = [limited(a, b) for a, b in zip(j, shift_up(j))]
             above = shift_down([c + v for c, v in zip(cells, s)])

time: 28.2 us -> 28 us (level)
  transfers between devices with their start and end apart: 11 -> 11, of which waited for: 0 -> 0; matrix products, arithmetic and copies ran while one was open for 0% -> 0% of each run, Pallas kernels for 26% -> 25%
where the time goes in v9:
time: 28 us; the launch traced here: 27.8 us
  starting transfers between devices  17.9 us (64%)
  Pallas kernels  9.25 us (33%)
  local copies, waits for them, and re-layouts  0.39 us (1%)
    ppermute x8, starting transfers between devices, pair_swap(): return lax.ppermute(values, axis, pairs)  15.1 us
    pallas_call x7, Pallas kernels, call(): pl.pallas_call(body, out_shape=[jax.ShapeDtypeStruct((rows, 128), jnp.flo...  9.25 us
    ppermute x3, starting transfers between devices, tracer_swap(): return lax.ppermute(values, 'tracer', [(0, 1), (1, 0)])  2.84 us
  transfers between devices with their start and end apart: 11, of which 0 were waited for; matrix products, arithmetic and copies ran while one was open for 0% of the time, Pallas kernels for 25%

profile of v9, /device:TPU:9, one launch (start us, length us, event | category | flops | bytes accessed | tf_op | source)
XLA Modules:
  0.0 27.8 jit_solution(11024997338270367425)
XLA Ops:
  0.0 1.2 %collective-permute-start = (f32[192,128]{1,0:T(8,128)}, f32[192,128]{1,0:T(8,128)S(1)}, u32[]{:S(2)}, u32[]{:S(2)}) collective-permute-start(f32[192,128]{1,0:T(8,128)} %bitcast.6), channel_id=1, source_target_pairs={{0,16},{16,0},{1,17},{17,1},{2,18},{18,2},{3,19},{19,3},{4,20},{20... | collective-permute-start | bytes 294920 | tf_op jit(solution)/shard_map/ppermute | solution.py:722
  1.2 0.0 copy-start.1
  1.2 0.0 copy-start.3
  1.2 0.0 copy-start.4
  1.2 2.1 %shard_map.82 = (f32[1536,128]{1,0:T(8,128)S(1)}, f32[192,128]{1,0:T(8,128)S(1)}, f32[424,128]{1,0:T(8,128)S(1)}, f32[96,128]{1,0:T(8,128)S(1)}) custom-call(f32[1536,128]{1,0:T(8,128)} %bitcast.8, s32[12]{0:T(128)} %groups_far.1, f32[16]{0:T(128)} %pref_far.1), custom_call_target="tpu_custom_call" | custom-call | tf_op jit(solution)/shard_map/pallas_call | solution.py:699
  3.4 0.0 copy-start.2
  3.4 0.3 %collective-permute-start.3 = (f32[424,128]{1,0:T(8,128)S(1)}, f32[424,128]{1,0:T(8,128)S(1)}, u32[]{:S(2)}, u32[]{:S(2)}) collective-permute-start(f32[424,128]{1,0:T(8,128)S(1)} %get-tuple-element.35.rest_0_), channel_id=1, source_target_pairs={{0,16},{16,0},{1,17},{17,1},{2,18},{18,2},{3,19},{19,3},{4,20},{20... | collective-permute-start | bytes 651272 | tf_op jit(solution)/shard_map/ppermute | solution.py:722
  3.7 0.0 collective-permute-done.other_ref
  3.7 0.0 copy-done.1
  3.7 0.0 copy-done.3
  3.7 0.0 copy-done.4
  3.7 0.4 %copy-done.2 = s32[8,128]{1,0:T(8,128)S(1)} copy-done((s32[8,128]{1,0:T(8,128)S(1)}, s32[8,128]{1,0:T(8,128)}, u32[]{:S(2)}) %copy-start.2) | copy-done | bytes 4120
  4.1 0.2 shard_map.83
  4.3 1.5 %collective-permute-start.1 = (f32[416,128]{1,0:T(8,128)S(1)}, f32[416,128]{1,0:T(8,128)S(1)}, u32[]{:S(2)}, u32[]{:S(2)}) collective-permute-start(f32[416,128]{1,0:T(8,128)S(1)} %get-tuple-element.31), channel_id=1, source_target_pairs={{0,4},{4,0},{8,12},{12,8},{1,5},{5,1},{9,13},{13,9},{2,6},{6,2},{1... | collective-permute-start | bytes 638984 | tf_op jit(solution)/shard_map/ppermute | solution.py:718
  5.8 3.0 %collective-permute-start.2 = (f32[416,128]{1,0:T(8,128)S(1)}, f32[416,128]{1,0:T(8,128)S(1)}, u32[]{:S(2)}, u32[]{:S(2)}) collective-permute-start(f32[416,128]{1,0:T(8,128)S(1)} %get-tuple-element.32), channel_id=1, source_target_pairs={{4,8},{8,4},{5,9},{9,5},{6,10},{10,6},{7,11},{11,7},{20,24},{24,20... | collective-permute-start | bytes 638984 | tf_op jit(solution)/shard_map/ppermute | solution.py:718
  8.8 0.2 collective-permute-start.4
  9.1 4.3 %collective-permute-start.5 = (f32[64,128]{1,0:T(8,128)S(1)}, f32[64,128]{1,0:T(8,128)S(1)}, u32[]{:S(2)}, u32[]{:S(2)}) collective-permute-start(f32[64,128]{1,0:T(8,128)S(1)} %get-tuple-element.40), channel_id=1, source_target_pairs={{1,2},{2,1},{5,6},{6,5},{9,10},{10,9},{13,14},{14,13},{17,18},{18,... | collective-permute-start | bytes 98312 | tf_op jit(solution)/shard_map/ppermute | solution.py:718
  13.4 0.0 copy-start
  13.4 1.5 %shard_map.84 = (f32[1536,128]{1,0:T(8,128)S(1)}, f32[1784,128]{1,0:T(8,128)S(1)}) custom-call(f32[1536,128]{1,0:T(8,128)S(1)} %get-tuple-element.27.field_ref, f32[384,128]{1,0:T(8,128)S(1)} %get-tuple-element.29.fluxes_ref, s32[8,128]{1,0:T(8,128)S(1)} %copy-done.2, f32[8,128]{1,0:T(8,128)S(1)} %copy-done.3, f32[8,128]{1,0:T(8,128)S(1)} %copy-done.4), custom_call_target="tpu_custom_call" | custom-call | tf_op jit(solution)/shard_map/pallas_call | solution.py:699
  15.0 0.0 collective-permute-done.3.rest_1_
  15.0 0.0 collective-permute-done.1.xev_ref
  15.0 0.0 collective-permute-done.2.xod_ref
  15.0 0.0 copy-done
  15.0 1.0 %shard_map.85 = (f32[1536,128]{1,0:T(8,128)S(1)}, f32[192,128]{1,0:T(8,128)S(1)}, f32[128,128]{1,0:T(8,128)S(1)}, f32[136,128]{1,0:T(8,128)S(1)}) custom-call(f32[1536,128]{1,0:T(8,128)S(1)} %get-tuple-element.27.field_ref, f32[1536,128]{1,0:T(8,128)S(1)} %get-tuple-element.30.part_ref, f32[416,128]{1,0:T(8,128)S(1)} %collective-permute-done.1.xev_ref, ...), custom_call_target="tpu_custom_call" | custom-call | tf_op jit(solution)/shard_map/pallas_call | solution.py:699
  16.0 0.0 collective-permute-done.4.yev_ref
  16.1 0.0 collective-permute-done.5.yod_ref
  16.1 0.8 %shard_map.86 = (f32[384,128]{1,0:T(8,128)S(1)}, f32[384,128]{1,0:T(8,128)S(1)}, f32[48,128]{1,0:T(8,128)S(1)}, f32[192,128]{1,0:T(8,128)S(1)}, f32[128,128]{1,0...) custom-call(f32[1536,128]{1,0:T(8,128)S(1)} %get-tuple-element.36.field_ref, ...), custom_call_target="tpu_custom_call" | custom-call | tf_op jit(solution)/shard_map/pallas_call | solution.py:699
  16.8 0.1 collective-permute-start.6
  16.9 3.1 %collective-permute-start.7 = (f32[384,128]{1,0:T(8,128)S(1)}, f32[384,128]{1,0:T(8,128)S(1)}, u32[]{:S(2)}, u32[]{:S(2)}) collective-permute-start(f32[384,128]{1,0:T(8,128)S(1)} %get-tuple-element.43), channel_id=1, source_target_pairs={{4,8},{8,4},{5,9},{9,5},{6,10},{10,6},{7,11},{11,7},{20,24},{24,20... | collective-permute-start | bytes 589832 | tf_op jit(solution)/shard_map/ppermute | solution.py:718
  20.0 1.3 %collective-permute-start.8 = (f32[128,128]{1,0:T(8,128)S(1)}, f32[128,128]{1,0:T(8,128)S(1)}, u32[]{:S(2)}, u32[]{:S(2)}) collective-permute-start(f32[128,128]{1,0:T(8,128)S(1)} %get-tuple-element.45.rest_0_), channel_id=1, source_target_pairs={{0,16},{16,0},{1,17},{17,1},{2,18},{18,2},{3,19},{19,3},{4,20},{20... | collective-permute-start | bytes 196616 | tf_op jit(solution)/shard_map/ppermute | solution.py:722
  21.3 0.0 collective-permute-start.10
  21.3 2.8 %collective-permute-start.9 = (f32[48,128]{1,0:T(8,128)S(1)}, f32[48,128]{1,0:T(8,128)S(1)}, u32[]{:S(2)}, u32[]{:S(2)}) collective-permute-start(f32[48,128]{1,0:T(8,128)S(1)} %get-tuple-element.47), channel_id=1, source_target_pairs={{1,2},{2,1},{5,6},{6,5},{9,10},{10,9},{13,14},{14,13},{17,18},{18,... | collective-permute-start | bytes 73736 | tf_op jit(solution)/shard_map/ppermute | solution.py:718
  24.2 0.0 collective-permute-done.8.rest_1_
  24.2 0.0 collective-permute-done.6.xev_ref
  24.2 0.0 collective-permute-done.7.xod_ref
  24.2 2.0 %shard_map.87.field_ref = f32[1536,128]{1,0:T(8,128)S(1)} custom-call(f32[1536,128]{1,0:T(8,128)S(1)} %get-tuple-element.36.field_ref, f32[192,128]{1,0:T(8,128)S(1)} %get-tuple-element.41.tend_ref, f32[384,128]{1,0:T(8,128)S(1)} %collective-permute-done.6.xev_ref, f32[384,128]{1,0:T(8,128)S(1)} %collective-permute-done.7.xod_ref, ...), custom_call_target="tpu_custom_call" | custom-call | tf_op jit(solution)/shard_map/pallas_call | solution.py:699
  26.2 0.0 collective-permute-done.10.yev_ref
  26.2 0.0 collective-permute-done.9.yod_ref
  26.2 1.5 %shard_map.88 = f32[1536,128]{1,0:T(8,128)} custom-call(f32[1536,128]{1,0:T(8,128)S(1)} %shard_map.87.field_ref, f32[192,128]{1,0:T(8,128)S(1)} %get-tuple-element.46.strips_ref, f32[48,128]{1,0:T(8,128)S(1)} %collective-permute-done.9.yod_ref, f32[48,128]{1,0:T(8,128)S(1)} %collective-permute-done.10.yev_ref, f32[160,128]{1,0:T(8,128)S(1)} %get-tuple-element.48.ends), custom_call_target="tpu_custom_call" | custom-call | tf_op jit(solution)/shard_map/pallas_call | solution.py:699
Async XLA Ops:
  0.0 3.7 %collective-permute-start = (f32[192,128]{1,0:T(8,128)}, f32[192,128]{1,0:T(8,128)S(1)}, u32[]{:S(2)}, u32[]{:S(2)}) collective-permute-start(f32[192,128]{1,0:T(8,128)} %bitcast.6), channel_id=1, source_target_pairs={{0,16},{16,0},{1,17},{17,1},{2,18},{18,2},{3,19},{19,3},{4,20},{20... | collective-permute-start | bytes 294920 | tf_op jit(solution)/shard_map/ppermute | solution.py:722
  1.2 2.5 %copy-start.1 = (f32[3,8,8,128]{3,2,1,0:T(8,128)S(1)}, f32[3,8,8,128]{3,2,1,0:T(8,128)}, u32[]{:S(2)}) copy-start(f32[3,8,8,128]{3,2,1,0:T(8,128)} %param.9) | copy-start | bytes 294916
  1.2 2.5 %copy-start.3 = (f32[8,128]{1,0:T(8,128)S(1)}, f32[8,128]{1,0:T(8,128)}, u32[]{:S(2)}) copy-start(f32[8,128]{1,0:T(8,128)} %east_ref.5) | copy-start | bytes 12292
  1.2 2.5 %copy-start.4 = (f32[8,128]{1,0:T(8,128)S(1)}, f32[8,128]{1,0:T(8,128)}, u32[]{:S(2)}) copy-start(f32[8,128]{1,0:T(8,128)} %north_ref.3) | copy-start | bytes 12292
  3.4 0.7 %copy-start.2 = (s32[8,128]{1,0:T(8,128)S(1)}, s32[8,128]{1,0:T(8,128)}, u32[]{:S(2)}) copy-start(s32[8,128]{1,0:T(8,128)} %depth_ref.5) | copy-start | bytes 12292
  3.4 11.6 %collective-permute-start.3 = (f32[424,128]{1,0:T(8,128)S(1)}, f32[424,128]{1,0:T(8,128)S(1)}, u32[]{:S(2)}, u32[]{:S(2)}) collective-permute-start(f32[424,128]{1,0:T(8,128)S(1)} %get-tuple-element.35.rest_0_), channel_id=1, source_target_pairs={{0,16},{16,0},{1,17},{17,1},{2,18},{18,2},{3,19},{19,3},{4,20},{20... | collective-permute-start | bytes 651272 | tf_op jit(solution)/shard_map/ppermute | solution.py:722
  4.3 10.7 %collective-permute-start.1 = (f32[416,128]{1,0:T(8,128)S(1)}, f32[416,128]{1,0:T(8,128)S(1)}, u32[]{:S(2)}, u32[]{:S(2)}) collective-permute-start(f32[416,128]{1,0:T(8,128)S(1)} %get-tuple-element.31), channel_id=1, source_target_pairs={{0,4},{4,0},{8,12},{12,8},{1,5},{5,1},{9,13},{13,9},{2,6},{6,2},{1... | collective-permute-start | bytes 638984 | tf_op jit(solution)/shard_map/ppermute | solution.py:718
  5.8 9.2 %collective-permute-start.2 = (f32[416,128]{1,0:T(8,128)S(1)}, f32[416,128]{1,0:T(8,128)S(1)}, u32[]{:S(2)}, u32[]{:S(2)}) collective-permute-start(f32[416,128]{1,0:T(8,128)S(1)} %get-tuple-element.32), channel_id=1, source_target_pairs={{4,8},{8,4},{5,9},{9,5},{6,10},{10,6},{7,11},{11,7},{20,24},{24,20... | collective-permute-start | bytes 638984 | tf_op jit(solution)/shard_map/ppermute | solution.py:718
  8.8 7.2 %collective-permute-start.4 = (f32[64,128]{1,0:T(8,128)S(1)}, f32[64,128]{1,0:T(8,128)S(1)}, u32[]{:S(2)}, u32[]{:S(2)}) collective-permute-start(f32[64,128]{1,0:T(8,128)S(1)} %get-tuple-element.40), channel_id=1, source_target_pairs={{0,1},{1,0},{2,3},{3,2},{4,5},{5,4},{6,7},{7,6},{8,9},{9,8},{10,11... | collective-permute-start | bytes 98312 | tf_op jit(solution)/shard_map/ppermute | solution.py:718
  9.1 7.0 %collective-permute-start.5 = (f32[64,128]{1,0:T(8,128)S(1)}, f32[64,128]{1,0:T(8,128)S(1)}, u32[]{:S(2)}, u32[]{:S(2)}) collective-permute-start(f32[64,128]{1,0:T(8,128)S(1)} %get-tuple-element.40), channel_id=1, source_target_pairs={{1,2},{2,1},{5,6},{6,5},{9,10},{10,9},{13,14},{14,13},{17,18},{18,... | collective-permute-start | bytes 98312 | tf_op jit(solution)/shard_map/ppermute | solution.py:718
  13.4 1.6 %copy-start = (f32[16,8,128]{2,1,0:T(8,128)S(1)}, f32[16,8,128]{2,1,0:T(8,128)}, u32[]{:S(2)}) copy-start(f32[16,8,128]{2,1,0:T(8,128)} %param.13) | copy-start | bytes 196612
  16.8 7.4 %collective-permute-start.6 = (f32[384,128]{1,0:T(8,128)S(1)}, f32[384,128]{1,0:T(8,128)S(1)}, u32[]{:S(2)}, u32[]{:S(2)}) collective-permute-start(f32[384,128]{1,0:T(8,128)S(1)} %get-tuple-element.42), channel_id=1, source_target_pairs={{0,4},{4,0},{8,12},{12,8},{1,5},{5,1},{9,13},{13,9},{2,6},{6,2},{1... | collective-permute-start | bytes 589832 | tf_op jit(solution)/shard_map/ppermute | solution.py:718
  16.9 7.3 %collective-permute-start.7 = (f32[384,128]{1,0:T(8,128)S(1)}, f32[384,128]{1,0:T(8,128)S(1)}, u32[]{:S(2)}, u32[]{:S(2)}) collective-permute-start(f32[384,128]{1,0:T(8,128)S(1)} %get-tuple-element.43), channel_id=1, source_target_pairs={{4,8},{8,4},{5,9},{9,5},{6,10},{10,6},{7,11},{11,7},{20,24},{24,20... | collective-permute-start | bytes 589832 | tf_op jit(solution)/shard_map/ppermute | solution.py:718
  20.0 4.2 %collective-permute-start.8 = (f32[128,128]{1,0:T(8,128)S(1)}, f32[128,128]{1,0:T(8,128)S(1)}, u32[]{:S(2)}, u32[]{:S(2)}) collective-permute-start(f32[128,128]{1,0:T(8,128)S(1)} %get-tuple-element.45.rest_0_), channel_id=1, source_target_pairs={{0,16},{16,0},{1,17},{17,1},{2,18},{18,2},{3,19},{19,3},{4,20},{20... | collective-permute-start | bytes 196616 | tf_op jit(solution)/shard_map/ppermute | solution.py:722
  21.3 4.9 %collective-permute-start.10 = (f32[48,128]{1,0:T(8,128)S(1)}, f32[48,128]{1,0:T(8,128)S(1)}, u32[]{:S(2)}, u32[]{:S(2)}) collective-permute-start(f32[48,128]{1,0:T(8,128)S(1)} %get-tuple-element.47), channel_id=1, source_target_pairs={{0,1},{1,0},{2,3},{3,2},{4,5},{5,4},{6,7},{7,6},{8,9},{9,8},{10,11... | collective-permute-start | bytes 73736 | tf_op jit(solution)/shard_map/ppermute | solution.py:718
  21.3 4.9 %collective-permute-start.9 = (f32[48,128]{1,0:T(8,128)S(1)}, f32[48,128]{1,0:T(8,128)S(1)}, u32[]{:S(2)}, u32[]{:S(2)}) collective-permute-start(f32[48,128]{1,0:T(8,128)S(1)} %get-tuple-element.47), channel_id=1, source_target_pairs={{1,2},{2,1},{5,6},{6,5},{9,10},{10,9},{13,14},{14,13},{17,18},{18,... | collective-permute-start | bytes 73736 | tf_op jit(solution)/shard_map/ppermute | solution.py:718
